TPU v7x, 32 devices: a whole 2x2x4 slice. The times are simulated.
32 devices in a mesh: section: 2 (over core), dp: 16 (over z, y, x).
Axes of the slice: x: 2, y: 2, z: 4, core: 2. Of those that a mesh axis runs over, the one named last changes fastest.
Arguments:
- tokens_in: bfloat16 [8192, 1152], P('dp'), may hold values from -6 to 6
- cotangent: bfloat16 [8192, 1152], P('dp'), may hold values from -6 to 6
- targets: bfloat16 [8192, 768], P('dp'), may hold values from -6 to 6
- buckets: int32 [32], P('dp'), may hold values from 0 to 999
- counts: int32 [16], replicated, may hold values from 1 to 2, as said below
- time_table: float32 [1000, 1152], replicated, may hold values from -6 to 6
- modulate_weight: bfloat16 [2, 1152, 6912], P('section', 'dp'), may hold values from -0.1875 to 0.1875
- modulate_bias: bfloat16 [2, 6912], P('section', 'dp'), may hold values from -3 to 3
- qkv_weight: bfloat16 [2, 1152, 3456], P('section', 'dp'), may hold values from -0.1875 to 0.1875
- qv_bias: bfloat16 [2, 2304], P('section', 'dp'), may hold values from -3 to 3
- attn_weight: bfloat16 [2, 1152, 1152], P('section', 'dp'), may hold values from -0.75 to 0.75
- attn_bias: bfloat16 [2, 1152], P('section', 'dp'), may hold values from -3 to 3
- up_weight: bfloat16 [2, 1152, 4608], P('section', 'dp'), may hold values from -0.1875 to 0.1875
- up_bias: bfloat16 [2, 4608], P('section', 'dp'), may hold values from -3 to 3
- down_weight: bfloat16 [2, 4608, 1152], P('section', 'dp'), may hold values from -0.09375 to 0.09375
- down_bias: bfloat16 [2, 1152], P('section', 'dp'), may hold values from -3 to 3
- project_in_weight: bfloat16 [1152, 2048], P('dp'), may hold values from -0.1875 to 0.1875
- project_in_bias: bfloat16 [2048], P('dp'), may hold values from -3 to 3
- project_mid_weight: bfloat16 [2048, 2048], P('dp'), may hold values from -0.125 to 0.125
- project_mid_bias: bfloat16 [2048], P('dp'), may hold values from -3 to 3
- project_out_weight: bfloat16 [2048, 768], P('dp'), may hold values from -0.125 to 0.125
- project_out_bias: bfloat16 [768], P('dp'), may hold values from -3 to 3
Outputs:
- streams: bfloat16 [2, 8192, 1152], P('section', 'dp')
- loss: float32 [], replicated
- grad_time_table: float32 [1000, 1152], replicated
- grad_modulate_weight: float32 [2, 1152, 6912], P('section', 'dp')
- grad_modulate_bias: float32 [2, 6912], P('section', 'dp')
- grad_qkv_weight: float32 [2, 1152, 3456], P('section', 'dp')
- grad_qv_bias: float32 [2, 2304], P('section', 'dp')
- grad_attn_weight: float32 [2, 1152, 1152], P('section', 'dp')
- grad_attn_bias: float32 [2, 1152], P('section', 'dp')
- grad_up_weight: float32 [2, 1152, 4608], P('section', 'dp')
- grad_up_bias: float32 [2, 4608], P('section', 'dp')
- grad_down_weight: float32 [2, 4608, 1152], P('section', 'dp')
- grad_down_bias: float32 [2, 1152], P('section', 'dp')
- grad_project_in_weight: float32 [1152, 2048], P(None, ('section', 'dp'))
- grad_project_in_bias: float32 [2048], P(('section', 'dp'))
- grad_project_mid_weight: float32 [2048, 2048], P(('section', 'dp'))
- grad_project_mid_bias: float32 [2048], P(('section', 'dp'))
- grad_project_out_weight: float32 [2048, 768], P(('section', 'dp'))
- grad_project_out_bias: float32 [768], replicated
Inputs may be any that keep to these rules, and one draw needn't show every extreme that they name: The first counts[d] image slots of index d of dp are live, the others are not; some index has all 2 live.
All inputs are finite; a program needn't handle non-finite values.
Results may differ from a plain program's by a relative error of at most 0.019.
Values may be sent and summed in bfloat16 or wider, within the bound.
A program may use at most 1 GiB of HBM per device.

v0:
```python
import jax
import jax.numpy as jnp
from jax import lax
from jax.sharding import PartitionSpec as P

HEADS = 16
SEQ = 256
MICRO = 2


EPSILON = 1e-06
HIGHEST = lax.Precision.HIGHEST


def from_behind(array, axis, by):
    peers = lax.axis_size(axis)
    pairs = [(i, i + by) for i in range(peers) if 0 <= i + by < peers]
    return lax.ppermute(array, axis, pairs)


def narrow(values):
    return values.astype(jnp.bfloat16)


def product(left_side, right_side):
    return jnp.dot(left_side, right_side, preferred_element_type=jnp.float32)


def product_left_t(left_side, right_side):
    return lax.dot_general(
        left_side, right_side, (((0,), (0,)), ((), ())), preferred_element_type=jnp.float32
    )


def product_right_t(left_side, right_side):
    return lax.dot_general(
        left_side, right_side, (((1,), (1,)), ((), ())), preferred_element_type=jnp.float32
    )


def layer_norm(values):
    center = values - jnp.mean(values, -1, keepdims=True)
    inverse = lax.rsqrt(jnp.mean(center * center, -1, keepdims=True) + EPSILON)
    return (center * inverse, inverse)


def norm_back(grad_in, normed, inverse):
    return inverse * (
        grad_in
        - jnp.mean(grad_in, -1, keepdims=True)
        - normed * jnp.mean(grad_in * normed, -1, keepdims=True)
    )


def local_grad(function, primal, cotangent_in):
    return jax.vjp(function, primal)[1](cotangent_in)[0]


def gelu_tanh(values):
    return jax.nn.gelu(values, approximate=True)


def column_sums(values):
    return jnp.sum(values.astype(jnp.float32), 0)


def guarded(predicate, work_fn, operands):

    def skipped(operands_in):
        return jax.tree.map(jnp.zeros_like, work_fn(operands_in))

    return lax.cond(predicate, work_fn, skipped, operands)


def block_forward(hidden, silu_rows, weights):
    (
        mod_weight,
        mod_bias,
        pack_weight,
        pack_bias,
        out_weight,
        out_bias,
        first_weight,
        first_bias,
        second_weight,
        second_bias,
    ) = weights
    images = silu_rows.shape[0]
    channels = hidden.shape[1]
    seq_len = hidden.shape[0] // images
    head_size = channels // HEADS
    scaling = head_size ** (-0.5)
    modulation = product(silu_rows, mod_weight) + mod_bias.astype(jnp.float32)
    pieces = modulation.reshape(images, 6, 1, channels)
    residual = hidden.astype(jnp.float32).reshape(images, seq_len, channels)
    normed_a, inverse_a = layer_norm(residual)
    attn_input = narrow(normed_a * (1.0 + pieces[:, 1]) + pieces[:, 0]).reshape(-1, channels)
    pack_full = jnp.concatenate(
        [pack_bias[:channels], jnp.zeros((channels,), pack_bias.dtype), pack_bias[channels:]]
    )
    packed = narrow(product(attn_input, pack_weight) + pack_full.astype(jnp.float32))
    split_heads = packed.reshape(images, seq_len, 3, HEADS, head_size)
    queries, key_rows, values = (split_heads[:, :, 0], split_heads[:, :, 1], split_heads[:, :, 2])
    scores = (
        jnp.einsum("nqhd,nkhd->nhqk", queries, key_rows, preferred_element_type=jnp.float32)
        * scaling
    )
    scores = scores - jnp.max(scores, -1, keepdims=True)
    exponent = jnp.exp(scores)
    probabilities = exponent / jnp.sum(exponent, -1, keepdims=True)
    mixed_rows = narrow(
        jnp.einsum(
            "nhqk,nkhd->nqhd", narrow(probabilities), values, preferred_element_type=jnp.float32
        )
    ).reshape(-1, channels)
    attn_out = product(mixed_rows, out_weight) + out_bias.astype(jnp.float32)
    after_attn = residual + pieces[:, 2] * attn_out.reshape(images, seq_len, channels)
    normed_m, inverse_m = layer_norm(after_attn)
    mlp_input = narrow(normed_m * (1.0 + pieces[:, 4]) + pieces[:, 3]).reshape(-1, channels)
    pre_act = product(mlp_input, first_weight) + first_bias.astype(jnp.float32)
    activation = narrow(gelu_tanh(pre_act))
    mlp_out = product(activation, second_weight) + second_bias.astype(jnp.float32)
    final_rows = after_attn + pieces[:, 5] * mlp_out.reshape(images, seq_len, channels)
    saved_state = (
        pieces,
        normed_a,
        inverse_a,
        attn_input,
        queries,
        key_rows,
        values,
        probabilities,
        mixed_rows,
        attn_out,
        normed_m,
        inverse_m,
        mlp_input,
        pre_act,
        activation,
        mlp_out,
    )
    return (final_rows.reshape(-1, channels), saved_state)


def block_backward(saved_state, silu_rows, weights, grad_out):
    (
        mod_weight,
        mod_bias,
        pack_weight,
        pack_bias,
        out_weight,
        out_bias,
        first_weight,
        first_bias,
        second_weight,
        second_bias,
    ) = weights
    (
        pieces,
        normed_a,
        inverse_a,
        attn_input,
        queries,
        key_rows,
        values,
        probabilities,
        mixed_rows,
        attn_out,
        normed_m,
        inverse_m,
        mlp_input,
        pre_act,
        activation,
        mlp_out,
    ) = saved_state
    images, seq_len, channels = normed_a.shape
    head_size = queries.shape[-1]
    scaling = head_size ** (-0.5)
    grad_final = grad_out.reshape(images, seq_len, channels)
    grad_mlp = narrow((pieces[:, 5] * grad_final).reshape(-1, channels))
    gate_m_grad = jnp.sum(grad_final * mlp_out.reshape(images, seq_len, channels), 1)
    second_w_grad = product_left_t(activation, grad_mlp)
    second_b_grad = column_sums(grad_mlp)
    grad_pre = narrow(local_grad(gelu_tanh, pre_act, product_right_t(grad_mlp, second_weight)))
    first_w_grad = product_left_t(mlp_input, grad_pre)
    first_b_grad = column_sums(grad_pre)
    grad_min = product_right_t(grad_pre, first_weight).reshape(images, seq_len, channels)
    shift_m_grad = jnp.sum(grad_min, 1)
    scale_m_grad = jnp.sum(grad_min * normed_m, 1)
    grad_after = grad_final + norm_back(grad_min * (1.0 + pieces[:, 4]), normed_m, inverse_m)
    grad_attn = narrow((pieces[:, 2] * grad_after).reshape(-1, channels))
    gate_a_grad = jnp.sum(grad_after * attn_out.reshape(images, seq_len, channels), 1)
    out_w_grad = product_left_t(mixed_rows, grad_attn)
    out_b_grad = column_sums(grad_attn)
    grad_mixed = narrow(product_right_t(grad_attn, out_weight)).reshape(
        images, seq_len, HEADS, head_size
    )
    grad_probs = jnp.einsum(
        "nqhd,nkhd->nhqk", grad_mixed, values, preferred_element_type=jnp.float32
    )
    grad_values = jnp.einsum(
        "nhqk,nqhd->nkhd", narrow(probabilities), grad_mixed, preferred_element_type=jnp.float32
    )
    grad_scores = narrow(
        probabilities * (grad_probs - jnp.sum(grad_probs * probabilities, -1, keepdims=True))
    )
    grad_queries = (
        jnp.einsum("nhqk,nkhd->nqhd", grad_scores, key_rows, preferred_element_type=jnp.float32)
        * scaling
    )
    grad_keys = (
        jnp.einsum("nhqk,nqhd->nkhd", grad_scores, queries, preferred_element_type=jnp.float32)
        * scaling
    )
    grad_packed = narrow(
        jnp.stack([grad_queries, grad_keys, grad_values], 2).reshape(-1, 3 * channels)
    )
    pack_w_grad = product_left_t(attn_input, grad_packed)
    pack_sums = column_sums(grad_packed)
    pack_b_grad = jnp.concatenate([pack_sums[:channels], pack_sums[2 * channels :]])
    grad_ain = product_right_t(grad_packed, pack_weight).reshape(images, seq_len, channels)
    shift_a_grad = jnp.sum(grad_ain, 1)
    scale_a_grad = jnp.sum(grad_ain * normed_a, 1)
    grad_input = grad_after + norm_back(grad_ain * (1.0 + pieces[:, 1]), normed_a, inverse_a)
    grad_mod = narrow(
        jnp.stack(
            [shift_a_grad, scale_a_grad, gate_a_grad, shift_m_grad, scale_m_grad, gate_m_grad], 1
        ).reshape(images, 6 * channels)
    )
    mod_w_grad = product_left_t(silu_rows, grad_mod)
    mod_b_grad = column_sums(grad_mod)
    grad_silu = product_right_t(grad_mod, mod_weight)
    weight_grads = (
        mod_w_grad,
        mod_b_grad,
        pack_w_grad,
        pack_b_grad,
        out_w_grad,
        out_b_grad,
        first_w_grad,
        first_b_grad,
        second_w_grad,
        second_b_grad,
    )
    return (grad_input.reshape(-1, channels), weight_grads, grad_silu)


def head_pass(hidden_rows, target_rows, live_rows, head_weights):
    in_weight, in_bias, mid_weight, mid_bias, out_weight, out_bias = head_weights
    pre_first = product(hidden_rows, in_weight) + in_bias.astype(jnp.float32)
    act_first = narrow(jax.nn.silu(pre_first))
    pre_second = product(act_first, mid_weight) + mid_bias.astype(jnp.float32)
    act_second = narrow(jax.nn.silu(pre_second))
    feature = product(act_second, out_weight) + out_bias.astype(jnp.float32)
    inverse_feature = lax.rsqrt(jnp.sum(feature * feature, -1, keepdims=True) + EPSILON)
    unit_feature = feature * inverse_feature
    target_float = target_rows.astype(jnp.float32)
    unit_target = target_float * lax.rsqrt(
        jnp.sum(target_float * target_float, -1, keepdims=True) + EPSILON
    )
    cosine = jnp.sum(unit_feature * unit_target, -1)
    loss_part = 0.5 * jnp.sum(live_rows * (1.0 - cosine))
    grad_unit = -0.5 * live_rows[:, None] * unit_target
    grad_feature = narrow(
        inverse_feature
        * (grad_unit - unit_feature * jnp.sum(grad_unit * unit_feature, -1, keepdims=True))
    )
    out_w_grad = product_left_t(act_second, grad_feature)
    out_b_grad = column_sums(grad_feature)
    grad_second = narrow(
        local_grad(jax.nn.silu, pre_second, product_right_t(grad_feature, out_weight))
    )
    mid_w_grad = product_left_t(act_first, grad_second)
    mid_b_grad = column_sums(grad_second)
    grad_first = narrow(
        local_grad(jax.nn.silu, pre_first, product_right_t(grad_second, mid_weight))
    )
    in_w_grad = product_left_t(hidden_rows, grad_first)
    in_b_grad = column_sums(grad_first)
    grad_hidden = product_right_t(grad_first, in_weight)
    return (
        loss_part,
        (in_w_grad, in_b_grad, mid_w_grad, mid_b_grad, out_w_grad, out_b_grad),
        grad_hidden,
    )


def on_device(
    tokens_in,
    cotangent,
    targets,
    buckets,
    counts,
    time_table,
    modulate_weight,
    modulate_bias,
    qkv_weight,
    qv_bias,
    attn_weight,
    attn_bias,
    up_weight,
    up_bias,
    down_weight,
    down_bias,
    project_in_weight,
    project_in_bias,
    project_mid_weight,
    project_mid_bias,
    project_out_weight,
    project_out_bias,
):
    section_index = lax.axis_index("section")
    is_first = section_index == 0
    data_index = lax.axis_index("dp")
    gathered = (
        lax.all_gather(modulate_weight[0], "dp", axis=0, tiled=True),
        lax.all_gather(modulate_bias[0], "dp", axis=0, tiled=True),
        lax.all_gather(qkv_weight[0], "dp", axis=0, tiled=True),
        lax.all_gather(qv_bias[0], "dp", axis=0, tiled=True),
        lax.all_gather(attn_weight[0], "dp", axis=0, tiled=True),
        lax.all_gather(attn_bias[0], "dp", axis=0, tiled=True),
        lax.all_gather(up_weight[0], "dp", axis=0, tiled=True),
        lax.all_gather(up_bias[0], "dp", axis=0, tiled=True),
        lax.all_gather(down_weight[0], "dp", axis=0, tiled=True),
        lax.all_gather(down_bias[0], "dp", axis=0, tiled=True),
        lax.all_gather(project_in_weight, "dp", axis=0, tiled=True),
        lax.all_gather(project_in_bias, "dp", axis=0, tiled=True),
        lax.all_gather(project_mid_weight, "dp", axis=0, tiled=True),
        lax.all_gather(project_mid_bias, "dp", axis=0, tiled=True),
        lax.all_gather(project_out_weight, "dp", axis=0, tiled=True),
        lax.all_gather(project_out_bias, "dp", axis=0, tiled=True),
    )
    block_weights = tuple(gathered[:10])
    head_weights = tuple(gathered[10:])
    channels = tokens_in.shape[1]
    image_count = tokens_in.shape[0] // SEQ
    micro_images = image_count // MICRO
    micro_rows = micro_images * SEQ
    image_live = (jnp.arange(image_count, dtype=jnp.int32) < counts[data_index]).astype(jnp.float32)
    token_live = jnp.repeat(image_live, SEQ)
    total_live = jnp.sum(counts).astype(jnp.float32) * SEQ
    one_hot = (
        buckets[:, None] == jnp.arange(time_table.shape[0], dtype=jnp.int32)[None, :]
    ).astype(jnp.float32)
    conditioning = jnp.dot(one_hot, time_table, precision=HIGHEST)
    silu_rows = narrow(jax.nn.silu(conditioning))
    arrived_fwd = jnp.zeros((micro_rows, channels), jnp.bfloat16)
    arrived_back = jnp.zeros((micro_rows, channels), jnp.bfloat16)
    streams = jnp.zeros((image_count * SEQ, channels), jnp.float32)
    silu_total = jnp.zeros((image_count, channels), jnp.float32)
    loss_total = jnp.zeros((), jnp.float32)
    head_total = tuple((jnp.zeros(weight.shape, jnp.float32) for weight in head_weights))
    block_total = tuple((jnp.zeros(weight.shape, jnp.float32) for weight in block_weights))
    head_list = []
    for tick_index in range(MICRO + 2):
        sent_rows = None
        if tick_index < MICRO:
            lower = tick_index * micro_rows
            front_operands = (
                tokens_in[lower : lower + micro_rows],
                silu_rows[tick_index * micro_images : (tick_index + 1) * micro_images],
                targets[lower : lower + micro_rows],
                token_live[lower : lower + micro_rows],
            )

            def front_work(operands_in):
                hidden_rows, silu_part, target_part, live_part = operands_in
                final_rows, saved_state = block_forward(hidden_rows, silu_part, block_weights)
                out_rows = narrow(final_rows)
                loss_part, head_part, grad_hidden = head_pass(
                    out_rows, target_part, live_part, head_weights
                )
                return (out_rows, loss_part, head_part, grad_hidden)

            front_result = guarded(is_first, front_work, front_operands)
            sent_rows = front_result[0]
            loss_total = loss_total + front_result[1]
            head_total = tuple((total + part for total, part in zip(head_total, front_result[2])))
            head_list.append(front_result[3])
        if tick_index >= 1:
            back_micro = tick_index - 2 + section_index
            back_valid = (back_micro >= 0) & (back_micro < MICRO)
            back_slot = jnp.clip(back_micro, 0, MICRO - 1)
            own_rows = lax.dynamic_slice_in_dim(tokens_in, back_slot * micro_rows, micro_rows, 0)
            hidden_rows = jnp.where(is_first, own_rows, arrived_fwd)
            silu_part = lax.dynamic_slice_in_dim(
                silu_rows, back_slot * micro_images, micro_images, 0
            )
            live_part = lax.dynamic_slice_in_dim(token_live, back_slot * micro_rows, micro_rows, 0)
            outer_grad = (
                lax.dynamic_slice_in_dim(cotangent, back_slot * micro_rows, micro_rows, 0).astype(
                    jnp.float32
                )
                * live_part[:, None]
            )
            first_slot = tick_index - 2
            if 0 <= first_slot < MICRO:
                head_extra = head_list[first_slot]
            else:
                head_extra = jnp.zeros((micro_rows, channels), jnp.float32)
            grad_rows = jnp.where(
                is_first, arrived_back.astype(jnp.float32) + head_extra, outer_grad
            )
            stored = None

            def back_work(operands_in):
                hidden_in, silu_in, grad_in = operands_in
                final_rows, saved_state = block_forward(hidden_in, silu_in, block_weights)
                grad_input, weight_grads, grad_silu = block_backward(
                    saved_state, silu_in, block_weights, grad_in
                )
                return (final_rows, grad_input, weight_grads, grad_silu)

            final_rows, grad_input, weight_grads, grad_silu = guarded(
                back_valid, back_work, (hidden_rows, silu_part, grad_rows)
            )
            block_total = tuple((total + part for total, part in zip(block_total, weight_grads)))
            previous_silu = lax.dynamic_slice_in_dim(
                silu_total, back_slot * micro_images, micro_images, 0
            )
            silu_total = lax.dynamic_update_slice_in_dim(
                silu_total, previous_silu + grad_silu, back_slot * micro_images, 0
            )
            stream_rows = jnp.where(is_first, grad_input, final_rows * live_part[:, None])
            previous_rows = lax.dynamic_slice_in_dim(streams, back_slot * micro_rows, micro_rows, 0)
            streams = lax.dynamic_update_slice_in_dim(
                streams,
                jnp.where(back_valid, stream_rows, previous_rows),
                back_slot * micro_rows,
                0,
            )
            if tick_index <= MICRO:
                arrived_back = from_behind(narrow(grad_input), "section", -1)
        if sent_rows is not None:
            arrived_fwd = from_behind(sent_rows, "section", 1)
    block_shards = (
        lax.psum_scatter(block_total[0], "dp", scatter_dimension=0, tiled=True),
        lax.psum_scatter(block_total[1], "dp", scatter_dimension=0, tiled=True),
        lax.psum_scatter(block_total[2], "dp", scatter_dimension=0, tiled=True),
        lax.psum_scatter(block_total[3], "dp", scatter_dimension=0, tiled=True),
        lax.psum_scatter(block_total[4], "dp", scatter_dimension=0, tiled=True),
        lax.psum_scatter(block_total[5], "dp", scatter_dimension=0, tiled=True),
        lax.psum_scatter(block_total[6], "dp", scatter_dimension=0, tiled=True),
        lax.psum_scatter(block_total[7], "dp", scatter_dimension=0, tiled=True),
        lax.psum_scatter(block_total[8], "dp", scatter_dimension=0, tiled=True),
        lax.psum_scatter(block_total[9], "dp", scatter_dimension=0, tiled=True),
    )
    cond_grad = local_grad(jax.nn.silu, conditioning, silu_total)
    table_part = jnp.dot(one_hot.T, cond_grad, precision=HIGHEST)
    head_shards = (
        lax.psum_scatter(head_total[0], ("section", "dp"), scatter_dimension=1, tiled=True),
        lax.psum_scatter(head_total[1], ("section", "dp"), scatter_dimension=0, tiled=True),
        lax.psum_scatter(head_total[2], ("section", "dp"), scatter_dimension=0, tiled=True),
        lax.psum_scatter(head_total[3], ("section", "dp"), scatter_dimension=0, tiled=True),
        lax.psum_scatter(head_total[4], ("section", "dp"), scatter_dimension=0, tiled=True),
    )
    loss_sum, table_grad, out_bias_grad = lax.psum(
        (loss_total, table_part, head_total[5]), ("section", "dp")
    )
    loss_value = loss_sum / total_live
    return (
        narrow(streams)[None],
        loss_value,
        table_grad,
        block_shards[0][None],
        block_shards[1][None],
        block_shards[2][None],
        block_shards[3][None],
        block_shards[4][None],
        block_shards[5][None],
        block_shards[6][None],
        block_shards[7][None],
        block_shards[8][None],
        block_shards[9][None],
        head_shards[0],
        head_shards[1],
        head_shards[2],
        head_shards[3],
        head_shards[4],
        out_bias_grad,
    )


def solution(mesh):
    in_specs = (
        P("dp", None),
        P("dp", None),
        P("dp", None),
        P("dp"),
        P(),
        P(),
        P("section", "dp", None),
        P("section", "dp"),
        P("section", "dp", None),
        P("section", "dp"),
        P("section", "dp", None),
        P("section", "dp"),
        P("section", "dp", None),
        P("section", "dp"),
        P("section", "dp", None),
        P("section", "dp"),
        P("dp", None),
        P("dp"),
        P("dp", None),
        P("dp"),
        P("dp", None),
        P("dp"),
    )
    out_specs = (
        P("section", "dp", None),
        P(),
        P(),
        P("section", "dp", None),
        P("section", "dp"),
        P("section", "dp", None),
        P("section", "dp"),
        P("section", "dp", None),
        P("section", "dp"),
        P("section", "dp", None),
        P("section", "dp"),
        P("section", "dp", None),
        P("section", "dp"),
        P(None, ("section", "dp")),
        P(("section", "dp")),
        P(("section", "dp"), None),
        P(("section", "dp")),
        P(("section", "dp"), None),
        P(),
    )
    return jax.shard_map(
        on_device, mesh=mesh, in_specs=in_specs, out_specs=out_specs, check_vma=False
    )
```

profile of v0, /device:TPU:10, one launch (start us, length us, event | category | flops | bytes accessed | tf_op | source)
XLA Modules:
  0.0 3772.2 jit_solution(1959801517794142220)
XLA Ops:
  16.8 29.8 all-gather.10
  46.6 40.4 %all-gather.11 = bf16[16,1,128]{2,1,0:T(2,128)(2,1)S(1)} all-gather(bf16[1,1,128]{2,1,0:T(2,128)(2,1)S(1)} %bitcast.398), channel_id=1, replica_groups=mesh['section'=2,'dp'=16] {'dp'}, dimensions={0}, use_global_device_ids=true | all-gather | bytes 4352 | tf_op jit(solution)/shard_map/all_gather | solution.py:329
  89.0 69.1 %all-reduce.17 = (bf16[6912]{0:T(1024)(128)(2,1)S(1)}, bf16[2304]{0:T(1024)(128)(2,1)S(1)}, bf16[1152]{0:T(1024)(128)(2,1)S(1)}, bf16[4608]{0:T(1024)(128)(2,1)S...) all-reduce(bf16[6912]{0:T(1024)(128)(2,1)S(1)} %dynamic-update-slic, ...), channel_id=3, replica_groups=mesh['section'=2,'dp'=16] {'dp'}, use_global_device_ids=true, to_apply=%add | all-reduce | flops 16896 | bytes 67584 | tf_op jit(solution)/shard_map/all_gather | solution.py:317
  163.4 65.1 %all-gather.21.cloned.1.call-done = bf16[1152,2048]{1,0:T(8,128)(2,1)} async-done(((bf16[72,2048]{1,0:T(8,128)(2,1)}), bf16[1152,2048]{1,0:T(8,128)(2,1)}) %all-gather.21.cloned.1.call-update) | async-done | bytes 4718608 | tf_op jit(solution)/shard_map/all_gather | solution.py:326
  228.5 109.2 %all-gather.29.cloned.1.call-done = bf16[1,1152,3456]{2,1,0:T(8,128)(2,1)} async-done(((bf16[1,72,3456]{2,1,0:T(8,128)(2,1)}), bf16[1,1152,3456]{2,1,0:T(8,128)(2,1)}) %all-gather.29.cloned.1.call-update) | async-done | bytes 7962640 | tf_op jit(solution)/shard_map/all_gather | solution.py:318
  337.6 113.4 %all-gather.23.cloned.1.call-done = bf16[2048,2048]{1,0:T(8,128)(2,1)} async-done(((bf16[128,2048]{1,0:T(8,128)(2,1)}), bf16[2048,2048]{1,0:T(8,128)(2,1)}) %all-gather.23.cloned.1.call-update) | async-done | bytes 8388624 | tf_op jit(solution)/shard_map/all_gather | solution.py:328
  451.0 134.0 %all-gather.33.cloned.1.call-done = bf16[1,1152,4608]{2,1,0:T(8,128)(2,1)} async-done(((bf16[1,72,4608]{2,1,0:T(8,128)(2,1)}), bf16[1,1152,4608]{2,1,0:T(8,128)(2,1)}) %all-gather.33.cloned.1.call-update) | async-done | bytes 10616848 | tf_op jit(solution)/shard_map/all_gather | solution.py:322
  585.0 134.5 %all-gather.35.cloned.1.call-done = bf16[1,4608,1152]{2,1,0:T(8,128)(2,1)} async-done(((bf16[1,288,1152]{2,1,0:T(8,128)(2,1)}), bf16[1,4608,1152]{2,1,0:T(8,128)(2,1)}) %all-gather.35.cloned.1.call-update) | async-done | bytes 10616848 | tf_op jit(solution)/shard_map/all_gather | solution.py:324
  719.5 184.5 %all-gather.27.cloned.1.call-done = bf16[1,1152,6912]{2,1,0:T(8,128)(2,1)} async-done(((bf16[1,72,6912]{2,1,0:T(8,128)(2,1)}), bf16[1,1152,6912]{2,1,0:T(8,128)(2,1)}) %all-gather.27.cloned.1.call-update) | async-done | bytes 15925264 | tf_op jit(solution)/shard_map/all_gather | solution.py:316
  904.1 93.8 %conditional.5 = (bf16[256,1152]{1,0:T(8,128)(2,1)}, f32[]{:T(128)}, f32[2048]{0:T(1024)S(1)}, f32[2048,2048]{1,0:T(8,128)}, f32[2048]{0:T(1024)S(1)}, /*index=5...) conditional(s32[]{:T(128)} %convert_element_type.781, () %tuple.71, ...), branch_computations={%region_0.0_spmd, %region_1.16_spmd} | conditional | flops 21011476480 | bytes 267199712 | solution.py:72
  936.1 15.3 fusion.17
  1004.7 91.8 %conditional.7 = (bf16[256,1152]{1,0:T(8,128)(2,1)}, f32[]{:T(128)}, f32[2048]{0:T(1024)S(1)}, f32[2048,2048]{1,0:T(8,128)}, f32[2048]{0:T(1024)S(1)}, /*index=5...) conditional(s32[]{:T(128)} %convert_element_type.781, () %tuple.75, ...), branch_computations={%region_39.40_spmd, %region_40.55_spmd} | conditional | flops 21011476480 | bytes 267205728 | solution.py:72
  1037.8 15.2 fusion.129
  1099.5 44.6 %conditional.6 = (f32[256,1152]{1,0:T(8,128)}, f32[256,1152]{1,0:T(8,128)S(1)}, f32[1152,6912]{1,0:T(8,128)}, f32[6912]{0:T(1024)}, f32[1152,3456]{1,0:T(8,128)}...) conditional(s32[]{:T(128)} %convert_element_type.780, () %tuple.70, ...), branch_computations={%region_16.17_spmd, %region_17.39_spmd} | conditional | flops 25504710656 | bytes 525275776 | solution.py:72
  1154.2 141.7 %conditional.8 = (f32[256,1152]{1,0:T(8,128)}, f32[256,1152]{1,0:T(8,128)S(1)}, f32[1152,6912]{1,0:T(8,128)}, f32[6912]{0:T(1024)}, f32[1152,3456]{1,0:T(8,128)}...) conditional(s32[]{:T(128)} %convert_element_type.785, () %tuple.74, ...), branch_computations={%region_55.56_spmd, %region_56.78_spmd} | conditional | flops 25505005568 | bytes 522916512 | solution.py:72
  1284.6 11.4 broadcast_multiply_fusion.11
  1300.0 12.1 collective-permute-done.3
  1313.3 140.1 %conditional.9 = (f32[256,1152]{1,0:T(8,128)}, f32[256,1152]{1,0:T(8,128)}, f32[1152,6912]{1,0:T(8,128)}, f32[6912]{0:T(1024)}, f32[1152,3456]{1,0:T(8,128)}, /*...) conditional(s32[]{:T(128)} %convert_element_type.789, () %tuple.77, ...), branch_computations={%region_78.79_spmd, %region_79.101_spmd} | conditional | flops 25505005568 | bytes 499323392 | solution.py:72
  1489.2 18.8 add.1022
  1508.1 21.8 add_add_fusion.3
  1530.0 28.6 add_add_fusion.2
  1558.7 28.9 add_add_fusion.1
  1587.7 42.1 %add_add_fusion = f32[1152,6912]{1,0:T(8,128)} fusion(f32[1152,6912]{1,0:T(8,128)} %get-tuple-element.679, f32[1152,6912]{1,0:T(8,128)} %get-tuple-element.677, f32[1152,6912]{1,0:T(8,128)} %get-tuple-element.678), kind=kLoop, calls=%fused_computation.523 | loop fusion | flops 15925248 | bytes 127401984 | tf_op jit(solution)/shard_map/add | solution.py:417
  1636.1 42.3 %all-reduce.15 = (f32[]{:T(128)}, f32[2048]{0:T(1024)}, f32[2048]{0:T(1024)S(1)}, f32[768]{0:T(1024)}) all-reduce(f32[]{:T(128)S(6)} %add.997, f32[2048]{0:T(1024)} %add.1021, f32[2048]{0:T(1024)} %add.1023, f32[768]{0:T(1024)} %add.1025), channel_id=1, replica_groups=mesh['section'=2,'dp'=16] {'section','dp'}, use_global_device_ids=true, to_apply=%region_101.102 | all-reduce | flops 4865 | bytes 38920 | tf_op jit(solution)/shard_map/psum | solution.py:457
  1685.0 65.4 %all-reduce.16 = (f32[6912]{0:T(1024)S(1)}, f32[2304]{0:T(1024)S(1)}, f32[1152]{0:T(1024)S(1)}, f32[4608]{0:T(1024)S(1)}, f32[1152]{0:T(1024)S(1)}) all-reduce(f32[6912]{0:T(1024)S(1)} %add_add_fusion.5, f32[2304]{0:T(1024)S(1)} %add_add_fusion.7, ...), channel_id=13, replica_groups=mesh['section'=2,'dp'=16] {'dp'}, use_global_device_ids=true, to_apply=%region_105.106.clone | all-reduce | flops 16128 | bytes 129024
  1756.5 115.2 %reduce-scatter.27.cloned.1.call-done = f32[72,1152]{1,0:T(8,128)} async-done(((f32[1152,1152]{1,0:T(8,128)}), f32[72,1152]{1,0:T(8,128)}) %reduce-scatter.27.cloned.1.call-update) | async-done | bytes 331792
  1871.7 140.9 %reduce-scatter.19.cloned.1.call-done = f32[1152,64]{0,1:T(8,128)} async-done(((f32[1152,2048]{0,1:T(8,128)}), f32[1152,64]{0,1:T(8,128)}) %reduce-scatter.19.cloned.1.call-update) | async-done | bytes 294928 | tf_op jit(solution)/shard_map/reduce_scatter | solution.py:451
  2012.5 363.0 %reduce-scatter.21.cloned.1.call-done = f32[64,2048]{1,0:T(8,128)} async-done(((f32[2048,2048]{1,0:T(8,128)}), f32[64,2048]{1,0:T(8,128)}) %reduce-scatter.21.cloned.1.call-update) | async-done | bytes 524304 | tf_op jit(solution)/shard_map/reduce_scatter | solution.py:453
  2375.5 258.6 %reduce-scatter.25.cloned.1.call-done = f32[72,3456]{1,0:T(8,128)} async-done(((f32[1152,3456]{1,0:T(8,128)}), f32[72,3456]{1,0:T(8,128)}) %reduce-scatter.25.cloned.1.call-update) | async-done | bytes 995344
  2634.1 319.7 %reduce-scatter.15.cloned.1.call-done = f32[72,4608]{1,0:T(8,128)} async-done(((f32[1152,4608]{1,0:T(8,128)}), f32[72,4608]{1,0:T(8,128)}) %reduce-scatter.15.cloned.1.call-update) | async-done | bytes 1327120 | tf_op jit(solution)/shard_map/reduce_scatter | solution.py:443
  2953.9 319.0 %reduce-scatter.17.cloned.1.call-done = f32[288,1152]{1,0:T(8,128)} async-done(((f32[4608,1152]{1,0:T(8,128)}), f32[288,1152]{1,0:T(8,128)}) %reduce-scatter.17.cloned.1.call-update) | async-done | bytes 1327120 | tf_op jit(solution)/shard_map/reduce_scatter | solution.py:445
  3272.8 486.7 %reduce-scatter.13.cloned.1.call-done = f32[72,6912]{1,0:T(8,128)} async-done(((f32[1152,6912]{1,0:T(8,128)}), f32[72,6912]{1,0:T(8,128)}) %reduce-scatter.13.cloned.1.call-update) | async-done | bytes 1990672 | tf_op jit(solution)/shard_map/reduce_scatter | solution.py:437
  (647 shorter events, 553.7 us)
Async XLA Ops:
  7.3 80.3 %copy-start.149 = (bf16[1,72]{1,0:T(2,128)(2,1)S(1)}, bf16[1,72]{1,0:T(2,128)(2,1)}, u32[]{:S(2)}) copy-start(bf16[1,72]{1,0:T(2,128)(2,1)} %param.43) | copy-start | bytes 436
  7.3 80.5 %copy-start.150 = (bf16[1,72]{1,0:T(2,128)(2,1)S(1)}, bf16[1,72]{1,0:T(2,128)(2,1)}, u32[]{:S(2)}) copy-start(bf16[1,72]{1,0:T(2,128)(2,1)} %param.47) | copy-start | bytes 436
  7.3 80.8 %copy-start.151 = (bf16[48]{0:T(256)(128)(2,1)S(1)}, bf16[48]{0:T(256)(128)(2,1)}, u32[]{:S(2)}) copy-start(bf16[48]{0:T(256)(128)(2,1)} %param.53) | copy-start | bytes 292
  7.3 151.4 %copy-start.136 = (s32[2]{0:T(128)S(1)}, s32[2]{0:T(128)}, u32[]{:S(2)}) copy-start(s32[2]{0:T(128)} %param.35) | copy-start | bytes 28
  7.3 156.1 %all-gather.31.cloned.1.call-start = ((), (), s32[]{:S(2)}) async-start(), calls=%async_computation.20 | async-start | bytes 2820096 | tf_op jit(solution)/shard_map/all_gather | solution.py:320
  8.0 155.4 %all-gather.25.cloned.1.call-start = ((), (), s32[]{:S(2)}) async-start(), calls=%async_computation.10 | async-start | bytes 3342336 | tf_op jit(solution)/shard_map/all_gather | solution.py:330
  8.8 219.7 %all-gather.21.cloned.1.call-start = ((), (), s32[]{:S(2)}) async-start(), calls=%async_computation.8 | async-start | bytes 5013504 | tf_op jit(solution)/shard_map/all_gather | solution.py:326
  9.5 328.1 %all-gather.29.cloned.1.call-start = ((), (), s32[]{:S(2)}) async-start(), calls=%async_computation.19 | async-start | bytes 8460288 | tf_op jit(solution)/shard_map/all_gather | solution.py:318
  10.1 440.9 %all-gather.23.cloned.1.call-start = ((), (), s32[]{:S(2)}) async-start(), calls=%async_computation.9 | async-start | bytes 8912896 | tf_op jit(solution)/shard_map/all_gather | solution.py:328
  10.7 574.4 %all-gather.33.cloned.1.call-start = ((), (), s32[]{:S(2)}) async-start(), calls=%async_computation.21 | async-start | bytes 11280384 | tf_op jit(solution)/shard_map/all_gather | solution.py:322
  11.3 708.3 %all-gather.35.cloned.1.call-start = ((), (), s32[]{:S(2)}) async-start(), calls=%async_computation.22 | async-start | bytes 11280384 | tf_op jit(solution)/shard_map/all_gather | solution.py:324
  12.0 892.0 %all-gather.27.cloned.1.call-start = ((), (), s32[]{:S(2)}) async-start(), calls=%async_computation.18 | async-start | bytes 16920576 | tf_op jit(solution)/shard_map/all_gather | solution.py:316
  12.8 1743.7 %all-reduce.20.cloned.1.call-start = ((), (), s32[]{:S(2)}) async-start(), calls=%async_computation.11 | async-start | bytes 9216000 | tf_op jit(solution)/shard_map/psum | solution.py:457
  158.1 746.0 %copy-start.124 = (bf16[768]{0:T(1024)(128)(2,1)}, bf16[768]{0:T(1024)(128)(2,1)S(1)}, u32[]{:S(2)}) copy-start(bf16[768]{0:T(1024)(128)(2,1)S(1)} %get-tuple-element.793) | copy-start | bytes 4612
  158.8 745.3 %copy-start.140 = (f32[2]{0:T(128)}, f32[2]{0:T(128)S(1)}, u32[]{:S(2)}) copy-start(f32[2]{0:T(128)S(1)} %compare_convert_fusion) | copy-start | bytes 28
  158.8 745.3 %copy-start.11 = (bf16[512,1152]{1,0:T(8,128)(2,1)S(1)}, bf16[512,1152]{1,0:T(8,128)(2,1)}, u32[]{:S(2)}) copy-start(bf16[512,1152]{1,0:T(8,128)(2,1)} %param.32) | copy-start | bytes 3538948
  158.8 745.3 %copy-start.35 = (bf16[512,768]{1,0:T(8,128)(2,1)S(1)}, bf16[512,768]{1,0:T(8,128)(2,1)}, u32[]{:S(2)}) copy-start(bf16[512,768]{1,0:T(8,128)(2,1)} %param.34) | copy-start | bytes 2359300
  997.9 98.7 %collective-permute-start = (bf16[256,1152]{1,0:T(8,128)(2,1)}, bf16[256,1152]{1,0:T(8,128)(2,1)}, u32[]{:S(2)}, u32[]{:S(2)}) collective-permute-start(bf16[256,1152]{1,0:T(8,128)(2,1)} %get-tuple-element.662), channel_id=1, source_target_pairs={{0,16},{1,17},{2,18},{3,19},{4,20},{5,21},{6,22},{7,23},{8,24},{9,... | collective-permute-start | bytes 1769480 | tf_op jit(solution)/shard_map/ppermute | solution.py:18
  1001.4 95.2 %copy-start.123 = (f32[256]{0:T(256)}, f32[256]{0:T(256)S(1)}, u32[]{:S(2)}) copy-start(f32[256]{0:T(256)S(1)} %get-tuple-element.939) | copy-start | bytes 3076
  1146.0 5.2 collective-permute-start.2
  1147.3 6.1 collective-permute-start.1
  1297.9 14.3 collective-permute-start.3
  1313.2 142.3 %copy-start.93 = (f32[2,1152]{1,0:T(2,128)S(1)}, f32[2,1152]{1,0:T(2,128)}, u32[]{:S(2)}) copy-start(f32[2,1152]{1,0:T(2,128)} %get-tuple-element.943) | copy-start | bytes 27652
  1313.2 142.3 %copy-start.137 = (s32[2]{0:T(128)S(1)}, s32[2]{0:T(128)}, u32[]{:S(2)}) copy-start(s32[2]{0:T(128)} %param.35) | copy-start | bytes 28
  1460.7 295.8 %reduce-scatter.23.cloned.1.call-start = ((), (), s32[]{:S(2)}) async-start(), calls=%async_computation.17 | async-start | bytes 6488064 | tf_op jit(solution)/shard_map/reduce_scatter | solution.py:455
  1468.8 402.8 %reduce-scatter.27.cloned.1.call-start = ((), (), s32[]{:S(2)}) async-start(), calls=%async_computation.24 | async-start | bytes 5640192
  1477.9 534.6 %reduce-scatter.19.cloned.1.call-start = ((), (), s32[]{:S(2)}) async-start(), calls=%async_computation.15 | async-start | bytes 9732096 | tf_op jit(solution)/shard_map/reduce_scatter | solution.py:451
  1489.2 886.3 %reduce-scatter.21.cloned.1.call-start = ((), (), s32[]{:S(2)}) async-start(), calls=%async_computation.16 | async-start | bytes 17301504 | tf_op jit(solution)/shard_map/reduce_scatter | solution.py:453
  1508.0 1126.1 %reduce-scatter.25.cloned.1.call-start = ((), (), s32[]{:S(2)}) async-start(), calls=%async_computation.23 | async-start | bytes 16920576
  1530.0 1423.9 %reduce-scatter.15.cloned.1.call-start = ((), (), s32[]{:S(2)}) async-start(), calls=%async_computation.13 | async-start | bytes 22560768 | tf_op jit(solution)/shard_map/reduce_scatter | solution.py:443
  1558.6 1714.2 %reduce-scatter.17.cloned.1.call-start = ((), (), s32[]{:S(2)}) async-start(), calls=%async_computation.14 | async-start | bytes 22560768 | tf_op jit(solution)/shard_map/reduce_scatter | solution.py:445
  1587.6 2171.9 %reduce-scatter.13.cloned.1.call-start = ((), (), s32[]{:S(2)}) async-start(), calls=%async_computation.12 | async-start | bytes 33841152 | tf_op jit(solution)/shard_map/reduce_scatter | solution.py:437
  (146 other events, 1244.7 us)
Sparse Core Ops, SparseCore 0:
  10.8 65.9 all-gather.30
  79.6 67.0 all-gather.24
  149.5 78.9 all-gather.20
  231.0 106.5 all-gather.28
  340.3 110.7 all-gather.22
  453.7 131.3 all-gather.32
  587.8 131.6 all-gather.34
  722.3 181.6 all-gather.26
  1460.8 143.7 all-reduce.19
  1611.7 114.6 reduce-scatter.22
  1732.2 139.4 reduce-scatter.26
  1878.0 134.5 reduce-scatter.18
  2015.5 359.9 reduce-scatter.20
  2382.8 251.3 reduce-scatter.24
  2641.6 312.2 reduce-scatter.14
  2960.3 312.4 reduce-scatter.16
  3280.3 479.1 reduce-scatter.12
where the time goes:
time: 3780 us; the launch traced here: 3770 us
  waiting for transfers between devices  2760 us (73%)
  matrix products  374 us (10%)
  other arithmetic  256 us (7%)
  blocking collectives  247 us (7%)
  local copies, waits for them, and re-layouts  91.9 us (2%)
    reduce_scatter x1, waiting for transfers between devices, on_device(): lax.psum_scatter(block_total[0], 'dp', scatter_dimension=0, tiled=True)  487 us
    unnamed x19, waiting for transfers between devices  379 us
    reduce_scatter x1, waiting for transfers between devices, on_device(): lax.psum_scatter(head_total[2], ('section', 'dp'), scatter_dimension=0, t...  363 us
    reduce_scatter x1, waiting for transfers between devices, on_device(): lax.psum_scatter(block_total[6], 'dp', scatter_dimension=0, tiled=True)  320 us
    reduce_scatter x1, waiting for transfers between devices, on_device(): lax.psum_scatter(block_total[8], 'dp', scatter_dimension=0, tiled=True)  319 us
    all_gather x1, waiting for transfers between devices, on_device(): lax.all_gather(modulate_weight[0], 'dp', axis=0, tiled=True)  185 us
    add x15, other arithmetic, on_device(): total + part  171 us
    dot_general x24, matrix products, product(): return jnp.dot(left_side, right_side, preferred_element_type=jnp.float32)  159 us
  transfers between devices with their start and end apart: 21, of which 14 were waited for; matrix products, arithmetic and copies ran while one was open for 8% of the time, Pallas kernels for 0%

commit v1 on v0

v1 whole, which is shorter than its diff:
```python
import functools
import jax
import jax.numpy as jnp
from jax import lax
from jax.experimental import pallas as pl
from jax.experimental.pallas import tpu as pltpu
from jax.sharding import PartitionSpec as P

HEADS = 16
SEQ = 256
EPSILON = 1e-06
HIGHEST = lax.Precision.HIGHEST
MESH = pl.DeviceIdType.MESH
ANY = pl.BlockSpec(memory_space=pl.ANY)
DMA = pltpu.SemaphoreType.DMA


def narrow(values):
    return values.astype(jnp.bfloat16)


def wide(values):
    return values.astype(jnp.float32)


def product(left_side, right_side):
    return jnp.dot(left_side, right_side, preferred_element_type=jnp.float32)


def product_left_t(left_side, right_side):
    return lax.dot_general(
        left_side, right_side, (((0,), (0,)), ((), ())), preferred_element_type=jnp.float32
    )


def product_right_t(left_side, right_side):
    return lax.dot_general(
        left_side, right_side, (((1,), (1,)), ((), ())), preferred_element_type=jnp.float32
    )


def ring_of(place, length):
    half, side = place // 2, place % 2
    return side * (length - 1 - half) + (1 - side) * half


def place_of(spot, length):
    side = spot // (length // 2)
    half = side * (length - 1 - spot) + (1 - side) * spot
    return 2 * half + side


def whereabouts(length):
    core = lax.axis_index("section")
    index = lax.axis_index("dp")
    place, role = index // 2, index % 2
    spot = ring_of(place, length)
    step = 1 - 2 * core

    def at(offset):
        return place_of(lax.rem(spot + step * offset + 4 * length, length), length)

    return dict(
        core=core,
        place=place,
        role=role,
        at=at,
        onward=(core, 2 * at(1) + role),
        before=(core, 2 * at(-1) + role),
        sibling=(1 - core, index),
        partner=(1 - core, 2 * place + 1 - role),
    )


def greet(devices):
    barrier = pltpu.get_barrier_semaphore()
    for device in devices:
        pl.semaphore_signal(barrier, inc=1, device_id=device, device_id_type=MESH)
    pl.semaphore_wait(barrier, len(devices))


def remote(source, target, send_sem, recv_sem, device):
    return pltpu.make_async_remote_copy(
        src_ref=source,
        dst_ref=target,
        send_sem=send_sem,
        recv_sem=recv_sem,
        device_id=device,
        device_id_type=MESH,
    )


def gather_kernel(length, count, front_only, *refs):
    shards, full = refs[:count], refs[count : 2 * count]
    own_sem, ring_send, ring_recv, side_send, side_recv = refs[2 * count :]
    me = whereabouts(length)
    core, role, place, at = me["core"], me["role"], me["place"], me["at"]
    layers = range(count)
    if front_only:
        greet([me["onward"], me["before"], me["sibling"], me["partner"]])
    else:
        greet([me["onward"], me["before"], me["sibling"], me["partner"]])

    def onward(layer, turn):
        block = full[layer].at[2 * at(-turn) + core]
        return remote(
            block, block, ring_send.at[layer, turn], ring_recv.at[layer, turn], me["onward"]
        )

    def across(layer, turn):
        block = full[layer].at[2 * at(-turn) + core]
        return remote(
            block, block, side_send.at[layer, turn], side_recv.at[layer, turn], me["sibling"]
        )

    def from_sibling(layer, turn):
        block = full[layer].at[2 * at(turn) + 1 - core]
        return remote(
            block, block, side_send.at[layer, turn], side_recv.at[layer, turn], me["sibling"]
        )

    def work():
        for layer in layers:
            onward(layer, 0).start()
            across(layer, 0).start()

        def turn_body(turn, carry):
            for layer in layers:
                block = full[layer].at[2 * at(-turn) + core]
                remote(
                    block,
                    block,
                    ring_send.at[layer, turn - 1],
                    ring_recv.at[layer, turn - 1],
                    me["onward"],
                ).wait_recv()

                @pl.when(turn < length - 1)
                def _():
                    onward(layer, turn).start()

                across(layer, turn).start()
            return carry

        lax.fori_loop(1, length, turn_body, 0)

        def end_body(turn, carry):
            for layer in layers:

                @pl.when(turn < length - 1)
                def _():
                    onward(layer, turn).wait_send()

                across(layer, turn).wait_send()
                from_sibling(layer, turn).wait_recv()
            return carry

        lax.fori_loop(0, length, end_body, 0)

    mine = 2 * place + core
    if front_only:
        @pl.when((role == 0) & (core == 0))
        def _():
            copies = [
                pltpu.make_async_copy(shards[i], full[i].at[mine], own_sem.at[i]) for i in layers
            ]
            for copy in copies:
                copy.start()
            for copy in copies:
                copy.wait()

        def crossing(layer):
            return remote(
                shards[layer],
                full[layer].at[2 * place + role],
                own_sem.at[layer],
                side_recv.at[layer, length],
                me["partner"],
            )

        @pl.when((role == 1) & (core == 0))
        def _():
            for layer in layers:
                crossing(layer).start()
            for layer in layers:
                crossing(layer).wait_send()

        @pl.when((role == 0) & (core == 1))
        def _():
            for layer in layers:
                remote(
                    shards[layer],
                    full[layer].at[mine],
                    own_sem.at[layer],
                    side_recv.at[layer, length],
                    me["partner"],
                ).wait_recv()

        @pl.when(role == 0)
        def _():
            work()

    else:

        @pl.when(core == role)
        def _():
            copies = [
                pltpu.make_async_copy(shards[i], full[i].at[mine], own_sem.at[i]) for i in layers
            ]
            for copy in copies:
                copy.start()
            for copy in copies:
                copy.wait()

        @pl.when(core != role)
        def _():
            crossings = [
                remote(
                    shards[i],
                    full[i].at[2 * place + role],
                    own_sem.at[i],
                    side_recv.at[i, length],
                    me["partner"],
                )
                for i in layers
            ]
            for copy in crossings:
                copy.start()
            for i in layers:
                remote(
                    shards[i],
                    full[i].at[mine],
                    own_sem.at[i],
                    side_recv.at[i, length],
                    me["partner"],
                ).wait()

        work()


def gather(shards, front_only, collective_id):
    members = lax.axis_size("dp")
    length, count = members // 2, len(shards)
    moved = sum(shard.size * 2 for shard in shards) * members
    return pl.pallas_call(
        functools.partial(gather_kernel, length, count, front_only),
        out_shape=[jax.ShapeDtypeStruct((members,) + s.shape, s.dtype) for s in shards],
        in_specs=[ANY] * count,
        out_specs=[ANY] * count,
        scratch_shapes=[
            DMA((count,)),
            DMA((count, length)),
            DMA((count, length)),
            DMA((count, length)),
            DMA((count, length + 1)),
        ],
        compiler_params=pltpu.CompilerParams(
            collective_id=collective_id, has_side_effects=True
        ),
        cost_estimate=pl.CostEstimate(flops=0, bytes_accessed=16 * moved, transcendentals=0),
    )(*shards)


def tile_of(columns):
    for tile in (512, 384, 256, 128):
        if columns % tile == 0:
            return tile
    return columns


def reduce_kernel(length, count, front_only, *refs):
    lefts, rights = refs[:count], refs[count : 2 * count]
    outs = refs[2 * count : 3 * count]
    scratch = refs[3 * count :]
    left_all, right_all = scratch[:count], scratch[count : 2 * count]
    arrived, leaving = scratch[2 * count : 3 * count], scratch[3 * count : 4 * count]
    own_sem, side_send, side_recv, ring_send, ring_recv, last_send, last_recv = scratch[4 * count :]
    me = whereabouts(length)
    core, role, place, at = me["core"], me["role"], me["place"], me["at"]
    layers = range(count)
    greet([me["onward"], me["before"], me["sibling"], me["partner"]] + ([(core, 2 * place + 1 - role)] if front_only else []))
    final = length % 2

    def chunk(layer, slot, turn, add):
        spot = at(-(turn + 1))
        columns = rights[layer].shape[1]
        tile = tile_of(columns)

        def body(index, carry):
            start = pl.multiple_of(index * tile, tile)
            total = product(
                left_all[layer][0, spot], right_all[layer][0, :, pl.ds(start, tile)]
            ) + product(left_all[layer][1, spot], right_all[layer][1, :, pl.ds(start, tile)])
            if add:
                total = total + wide(arrived[layer][turn - 1, :, pl.ds(start, tile)])
            leaving[layer][slot, :, pl.ds(start, tile)] = narrow(total)
            return carry

        lax.fori_loop(0, columns // tile, body, 0)

    def onward(layer, slot, turn):
        return remote(
            leaving[layer].at[slot],
            arrived[layer].at[turn],
            ring_send.at[layer, slot],
            ring_recv.at[layer, turn],
            me["onward"],
        )

    def inputs(layer):
        return [
            pltpu.make_async_copy(
                lefts[layer].at[:, core], left_all[layer].at[0], own_sem.at[layer, 0]
            ),
            pltpu.make_async_copy(rights[layer], right_all[layer].at[0], own_sem.at[layer, 1]),
            remote(
                lefts[layer].at[:, 1 - core],
                left_all[layer].at[1],
                side_send.at[layer, 0],
                side_recv.at[layer, 0],
                me["sibling"],
            ),
            remote(
                rights[layer],
                right_all[layer].at[1],
                side_send.at[layer, 1],
                side_recv.at[layer, 1],
                me["sibling"],
            ),
        ]

    def work():
        for layer in layers:
            for copy in inputs(layer):
                copy.start()
        for layer in layers:
            for copy in inputs(layer):
                copy.wait()
            chunk(layer, 0, 0, False)
            onward(layer, 0, 0).start()

        def turn_body(turn, carry):
            slot = turn % 2
            for layer in layers:
                onward(layer, slot, turn - 1).wait_recv()

                @pl.when(turn >= 2)
                def _():
                    onward(layer, slot, turn).wait_send()

                chunk(layer, slot, turn, True)
                onward(layer, slot, turn).start()
            return carry

        lax.fori_loop(1, length - 1, turn_body, 0)
        slot = (length - 1) % 2
        for layer in layers:
            onward(layer, slot, length - 2).wait_recv()
            if length >= 3:
                onward(layer, slot, length - 2).wait_send()
            chunk(layer, slot, length - 1, True)
            finish(layer, slot)
        for layer in layers:
            onward(layer, 1 - slot, length - 2).wait_send()
            finished(layer, slot)

    def local_last(layer, slot):
        return pltpu.make_async_copy(leaving[layer].at[slot], outs[layer], last_send.at[layer, 0])

    def remote_last(layer, slot):
        return remote(
            leaving[layer].at[slot],
            outs[layer],
            last_send.at[layer, 0],
            last_recv.at[layer, 0],
            me["partner"],
        )

    if not front_only:

        def finish(layer, slot):
            @pl.when(core == role)
            def _():
                local_last(layer, slot).start()

            @pl.when(core != role)
            def _():
                remote_last(layer, slot).start()

        def finished(layer, slot):
            @pl.when(core == role)
            def _():
                local_last(layer, slot).wait()

            @pl.when(core != role)
            def _():
                remote_last(layer, slot).wait()

        work()
    else:
        def part(layer, slot, half):
            rows = outs[layer].shape[0]
            return leaving[layer].at[slot, pl.ds(half * rows, rows)]

        def keep(layer, slot):
            return pltpu.make_async_copy(
                part(layer, slot, 0), outs[layer], last_send.at[layer, 0]
            )

        def hand(layer, slot, half, device):
            return remote(
                part(layer, slot, half),
                outs[layer],
                last_send.at[layer, half],
                last_recv.at[layer, 0],
                device,
            )

        def moves(layer, slot, act):
            @pl.when(core == 0)
            def _():
                act(keep(layer, slot))
                act(hand(layer, slot, 1, me["sibling"]))

            @pl.when(core == 1)
            def _():
                act(hand(layer, slot, 0, (0, 2 * place + 1)))
                act(hand(layer, slot, 1, (1, 2 * place + 1)))

        def finish(layer, slot):
            moves(layer, slot, lambda copy: copy.start())

        def finished(layer, slot):
            @pl.when(core == 0)
            def _():
                keep(layer, slot).wait()
                hand(layer, slot, 1, me["sibling"]).wait_send()

            @pl.when(core == 1)
            def _():
                hand(layer, slot, 0, (0, 2 * place + 1)).wait_send()
                hand(layer, slot, 1, (1, 2 * place + 1)).wait_send()

        @pl.when(role == 0)
        def _():
            work()

        @pl.when((role == 1) | (core == 1))
        def _():
            for layer in layers:
                hand(layer, 0, 0, me["sibling"]).wait_recv()


def reduce(lefts, rights, front_only, collective_id):
    members = lax.axis_size("dp")
    length, count = members // 2, len(lefts)
    rows = [left.shape[2] for left in lefts]
    columns = [right.shape[1] for right in rights]
    tokens = rights[0].shape[0]
    halves = 2 if front_only else 1
    bf16 = jnp.bfloat16
    work = sum(r * c for r, c in zip(rows, columns)) * length
    return pl.pallas_call(
        functools.partial(reduce_kernel, length, count, front_only),
        out_shape=[
            jax.ShapeDtypeStruct((r // halves, c), bf16) for r, c in zip(rows, columns)
        ],
        in_specs=[ANY] * (2 * count),
        out_specs=[ANY] * count,
        scratch_shapes=[pltpu.VMEM((2, length, r, tokens), bf16) for r in rows]
        + [pltpu.VMEM((2, tokens, c), bf16) for c in columns]
        + [pltpu.VMEM((length - 1, r, c), bf16) for r, c in zip(rows, columns)]
        + [pltpu.VMEM((2, r, c), bf16) for r, c in zip(rows, columns)]
        + [
            DMA((count, 2)),
            DMA((count, 2)),
            DMA((count, 2)),
            DMA((count, 2)),
            DMA((count, length)),
            DMA((count, 2)),
            DMA((count, 1)),
        ],
        compiler_params=pltpu.CompilerParams(
            collective_id=collective_id, has_side_effects=True, vmem_limit_bytes=60 * 2**20
        ),
        cost_estimate=pl.CostEstimate(
            flops=4 * work * tokens, bytes_accessed=64 * work, transcendentals=0
        ),
    )(*lefts, *rights)


def layer_norm(values):
    center = values - jnp.mean(values, -1, keepdims=True)
    inverse = lax.rsqrt(jnp.mean(center * center, -1, keepdims=True) + EPSILON)
    return (center * inverse, inverse)


def norm_back(grad_in, normed, inverse):
    return inverse * (
        grad_in
        - jnp.mean(grad_in, -1, keepdims=True)
        - normed * jnp.mean(grad_in * normed, -1, keepdims=True)
    )


def local_grad(function, primal, cotangent_in):
    return jax.vjp(function, primal)[1](cotangent_in)[0]


def gelu_tanh(values):
    return jax.nn.gelu(values, approximate=True)


def column_sums(values):
    return jnp.sum(wide(values), 0)


def blocked_t(values, members):
    tokens, features = values.shape
    return values.T.reshape(members // 2, 2, features // members, tokens)


def block_forward(hidden, pieces, weights):
    pack_weight, pack_full, out_weight, out_bias, first_weight, first_bias, second_weight, second_bias = weights
    images = pieces.shape[0]
    channels = hidden.shape[1]
    seq_len = hidden.shape[0] // images
    head_size = channels // HEADS
    scaling = head_size ** (-0.5)
    residual = wide(hidden).reshape(images, seq_len, channels)
    normed_a, _ = layer_norm(residual)
    attn_input = narrow(normed_a * (1.0 + pieces[:, 1]) + pieces[:, 0]).reshape(-1, channels)
    packed = narrow(product(attn_input, pack_weight) + pack_full)
    split_heads = packed.reshape(images, seq_len, 3, HEADS, head_size)
    queries, key_rows, values = (split_heads[:, :, 0], split_heads[:, :, 1], split_heads[:, :, 2])
    scores = (
        jnp.einsum("nqhd,nkhd->nhqk", queries, key_rows, preferred_element_type=jnp.float32)
        * scaling
    )
    scores = scores - jnp.max(scores, -1, keepdims=True)
    exponent = jnp.exp(scores)
    probabilities = narrow(exponent / jnp.sum(exponent, -1, keepdims=True))
    mixed_rows = narrow(
        jnp.einsum("nhqk,nkhd->nqhd", probabilities, values, preferred_element_type=jnp.float32)
    ).reshape(-1, channels)
    attn_out = product(mixed_rows, out_weight) + out_bias
    after_attn = residual + pieces[:, 2] * attn_out.reshape(images, seq_len, channels)
    normed_m, _ = layer_norm(after_attn)
    mlp_input = narrow(normed_m * (1.0 + pieces[:, 4]) + pieces[:, 3]).reshape(-1, channels)
    pre_act = product(mlp_input, first_weight) + first_bias
    activation = narrow(gelu_tanh(pre_act))
    mlp_out = product(activation, second_weight) + second_bias
    final_rows = after_attn + pieces[:, 5] * mlp_out.reshape(images, seq_len, channels)
    saved_state = (
        attn_input,
        packed,
        probabilities,
        mixed_rows,
        attn_out,
        after_attn,
        mlp_input,
        pre_act,
        activation,
        mlp_out,
    )
    return (final_rows.reshape(-1, channels), saved_state)


def block_backward(hidden, saved_state, pieces, weights, grad_out, members):
    pack_weight, pack_full, out_weight, out_bias, first_weight, first_bias, second_weight, second_bias = weights
    (
        attn_input,
        packed,
        probabilities,
        mixed_rows,
        attn_out,
        after_attn,
        mlp_input,
        pre_act,
        activation,
        mlp_out,
    ) = saved_state
    images = pieces.shape[0]
    channels = hidden.shape[1]
    seq_len = hidden.shape[0] // images
    head_size = channels // HEADS
    scaling = head_size ** (-0.5)
    normed_m, inverse_m = layer_norm(after_attn)
    grad_final = grad_out.reshape(images, seq_len, channels)
    grad_mlp = narrow((pieces[:, 5] * grad_final).reshape(-1, channels))
    gate_m_grad = jnp.sum(grad_final * mlp_out.reshape(images, seq_len, channels), 1)
    second_b_grad = column_sums(grad_mlp)
    grad_pre = narrow(local_grad(gelu_tanh, pre_act, product_right_t(grad_mlp, second_weight)))
    first_b_grad = column_sums(grad_pre)
    grad_min = product_right_t(grad_pre, first_weight).reshape(images, seq_len, channels)
    shift_m_grad = jnp.sum(grad_min, 1)
    scale_m_grad = jnp.sum(grad_min * normed_m, 1)
    grad_after = grad_final + norm_back(grad_min * (1.0 + pieces[:, 4]), normed_m, inverse_m)
    grad_attn = narrow((pieces[:, 2] * grad_after).reshape(-1, channels))
    gate_a_grad = jnp.sum(grad_after * attn_out.reshape(images, seq_len, channels), 1)
    out_b_grad = column_sums(grad_attn)
    grad_mixed = narrow(product_right_t(grad_attn, out_weight)).reshape(
        images, seq_len, HEADS, head_size
    )
    split_heads = packed.reshape(images, seq_len, 3, HEADS, head_size)
    queries, key_rows, values = (split_heads[:, :, 0], split_heads[:, :, 1], split_heads[:, :, 2])
    grad_probs = jnp.einsum(
        "nqhd,nkhd->nhqk", grad_mixed, values, preferred_element_type=jnp.float32
    )
    grad_values = jnp.einsum(
        "nhqk,nqhd->nkhd", probabilities, grad_mixed, preferred_element_type=jnp.float32
    )
    probs_wide = wide(probabilities)
    grad_scores = narrow(
        probs_wide * (grad_probs - jnp.sum(grad_probs * probs_wide, -1, keepdims=True))
    )
    grad_queries = (
        jnp.einsum("nhqk,nkhd->nqhd", grad_scores, key_rows, preferred_element_type=jnp.float32)
        * scaling
    )
    grad_keys = (
        jnp.einsum("nhqk,nqhd->nkhd", grad_scores, queries, preferred_element_type=jnp.float32)
        * scaling
    )
    grad_packed = narrow(
        jnp.stack([grad_queries, grad_keys, grad_values], 2).reshape(-1, 3 * channels)
    )
    pack_sums = column_sums(grad_packed)
    pack_b_grad = jnp.concatenate([pack_sums[:channels], pack_sums[2 * channels :]])
    grad_ain = product_right_t(grad_packed, pack_weight).reshape(images, seq_len, channels)
    normed_a, inverse_a = layer_norm(wide(hidden).reshape(images, seq_len, channels))
    shift_a_grad = jnp.sum(grad_ain, 1)
    scale_a_grad = jnp.sum(grad_ain * normed_a, 1)
    grad_input = grad_after + norm_back(grad_ain * (1.0 + pieces[:, 1]), normed_a, inverse_a)
    grad_mod = narrow(
        jnp.stack(
            [shift_a_grad, scale_a_grad, gate_a_grad, shift_m_grad, scale_m_grad, gate_m_grad], 1
        ).reshape(images, 6 * channels)
    )
    lefts = tuple(blocked_t(v, members) for v in (activation, mlp_input, mixed_rows, attn_input))
    rights = (grad_mlp, grad_pre, grad_attn, grad_packed)
    bias_grads = (pack_b_grad, out_b_grad, first_b_grad, second_b_grad)
    return (grad_input.reshape(-1, channels), lefts, rights, bias_grads, grad_mod)


def head_pass(hidden_rows, target_rows, live_rows, head_weights, members):
    in_weight, in_bias, mid_weight, mid_bias, out_weight, out_bias = head_weights
    pre_first = product(hidden_rows, in_weight) + in_bias
    act_first = narrow(jax.nn.silu(pre_first))
    pre_second = product(act_first, mid_weight) + mid_bias
    act_second = narrow(jax.nn.silu(pre_second))
    feature = product(act_second, out_weight) + out_bias
    inverse_feature = lax.rsqrt(jnp.sum(feature * feature, -1, keepdims=True) + EPSILON)
    unit_feature = feature * inverse_feature
    target_float = wide(target_rows)
    unit_target = target_float * lax.rsqrt(
        jnp.sum(target_float * target_float, -1, keepdims=True) + EPSILON
    )
    cosine = jnp.sum(unit_feature * unit_target, -1)
    loss_part = 0.5 * jnp.sum(live_rows * (1.0 - cosine))
    grad_unit = -0.5 * live_rows[:, None] * unit_target
    grad_feature = narrow(
        inverse_feature
        * (grad_unit - unit_feature * jnp.sum(grad_unit * unit_feature, -1, keepdims=True))
    )
    grad_second = narrow(
        local_grad(jax.nn.silu, pre_second, product_right_t(grad_feature, out_weight))
    )
    grad_first = narrow(
        local_grad(jax.nn.silu, pre_first, product_right_t(grad_second, mid_weight))
    )
    grad_hidden = product_right_t(grad_first, in_weight)

    def in_halves(values):
        tokens, features = values.shape
        rows = features // (2 * members)
        cut = values.T.reshape(2, members, rows, tokens)
        return jnp.swapaxes(cut, 0, 1).reshape(members // 2, 2, 2 * rows, tokens)

    lefts = (in_halves(act_second), in_halves(act_first), in_halves(grad_first))
    rights = (grad_feature, grad_second, hidden_rows)
    sums = (column_sums(grad_first), column_sums(grad_second), column_sums(grad_feature))
    return (grad_hidden, loss_part, lefts, rights, sums)


def either(first_function, second_function, is_first, operands):
    shapes = jax.eval_shape(first_function or second_function, *operands)

    def zeros(*operands_in):
        return jax.tree.map(lambda leaf: jnp.zeros(leaf.shape, leaf.dtype), shapes)

    return lax.cond(is_first, first_function or zeros, second_function or zeros, *operands)


def on_device(
    tokens_in,
    cotangent,
    targets,
    buckets,
    counts,
    time_table,
    modulate_weight,
    modulate_bias,
    qkv_weight,
    qv_bias,
    attn_weight,
    attn_bias,
    up_weight,
    up_bias,
    down_weight,
    down_bias,
    project_in_weight,
    project_in_bias,
    project_mid_weight,
    project_mid_bias,
    project_out_weight,
    project_out_bias,
):
    members = lax.axis_size("dp")
    core = lax.axis_index("section")
    index = lax.axis_index("dp")
    place, role = index // 2, index % 2
    is_first = role == 0
    own = 2 * place + core
    channels = tokens_in.shape[1]
    images = tokens_in.shape[0] // SEQ
    pairs_swap, pairs_up, pairs_back = [], [], []
    for pair in range(members // 2):
        low, high = 2 * pair, 2 * pair + 1
        pairs_swap += [(low, low), (members + low, high), (high, members + low), (members + high, members + high)]
        pairs_up += [(low, high), (members + low, members + high)]
        pairs_back += [(high, low), (members + high, members + low)]
    axes = ("section", "dp")

    def swap(values):
        return lax.ppermute(values, axes, pairs_swap)

    section_biases = (qv_bias[0], attn_bias[0], up_bias[0], down_bias[0])
    head_biases = (project_in_bias, project_mid_bias, project_out_bias)
    parts = section_biases + head_biases
    widths = [part.shape[0] for part in parts]
    lanes = 16 * 128
    packed_bias = jnp.concatenate(
        list(parts) + [jnp.zeros((lanes - sum(widths),), jnp.bfloat16)]
    ).reshape(16, 128)
    all_bias, pack_weight, out_weight, first_weight, second_weight = gather(
        (packed_bias, qkv_weight[0], attn_weight[0], up_weight[0], down_weight[0]), False, 0
    )
    all_bias = all_bias.reshape(members, lanes)
    biases, offset = [], 0
    for width in widths:
        biases.append(wide(all_bias[:, offset : offset + width].reshape(-1)))
        offset += width
    pack_full = jnp.concatenate(
        [biases[0][:channels], jnp.zeros((channels,), jnp.float32), biases[0][channels:]]
    )

    def whole(values):
        return values.reshape(-1, values.shape[-1])

    block_weights = (
        whole(pack_weight),
        pack_full,
        whole(out_weight),
        biases[1],
        whole(first_weight),
        biases[2],
        whole(second_weight),
        biases[3],
    )

    all_buckets = lax.all_gather(buckets, "dp", axis=0, tiled=True)
    one_hot = (
        all_buckets[:, None] == jnp.arange(time_table.shape[0], dtype=jnp.int32)[None, :]
    ).astype(jnp.float32)
    conditioning = jnp.dot(one_hot, time_table, precision=HIGHEST)
    silu_all = narrow(jax.nn.silu(conditioning))
    depth = modulate_weight.shape[1]
    silu_depth = lax.dynamic_slice_in_dim(silu_all, index * depth, depth, 1)
    mod_part = product(silu_depth, modulate_weight[0])
    share = modulate_bias.shape[1]
    bias_row = lax.dynamic_update_slice_in_dim(
        jnp.zeros((mod_part.shape[1],), jnp.float32), wide(modulate_bias[0]), index * share, 0
    )
    mod_own = lax.psum_scatter(mod_part + bias_row[None], "dp", scatter_dimension=0, tiled=True)
    pieces = swap(mod_own).reshape(images, 6, 1, channels)

    own_counts = counts[own]
    image_live = (jnp.arange(images, dtype=jnp.int32) < own_counts).astype(jnp.float32)
    token_live = jnp.repeat(image_live, SEQ)
    total_live = wide(jnp.sum(counts)) * SEQ
    payload = swap(jnp.where(is_first, cotangent, tokens_in))
    crossed = core != role
    hidden_first = jnp.where(crossed, payload, tokens_in)
    outer = jnp.where(crossed, payload, cotangent)
    own_targets = swap(targets)

    final_rows, saved_state = either(
        lambda h, m, *w: block_forward(h, m, w),
        None,
        is_first,
        (hidden_first, pieces) + block_weights,
    )
    first_out = narrow(final_rows)
    hidden_second = lax.ppermute(first_out, axes, pairs_up)

    head_full = gather((project_in_weight, project_mid_weight, project_out_weight), True, 1)
    head_weights = (
        whole(head_full[0]),
        biases[4],
        whole(head_full[1]),
        biases[5],
        whole(head_full[2]),
        biases[6],
    )

    def back(first, second, mod, grad, target, live, block, head):
        final, state = block_forward(second, mod, block)
        outer_grad = wide(grad) * live[:, None]
        grad_input, lefts, rights, bias_grads, grad_mod = block_backward(
            second, state, mod, block, outer_grad, members
        )
        return (narrow(grad_input), narrow(final * live[:, None]), lefts, rights, bias_grads, grad_mod)

    def zeros_like_of(function, *operands):
        shapes = jax.eval_shape(function, *operands)
        return jax.tree.map(lambda leaf: jnp.zeros(leaf.shape, leaf.dtype), shapes)

    def do_head(first, target, live, head):
        return head_pass(first, target, live, head, members)

    def do_second(second, mod, grad, live, block):
        return back(None, second, mod, grad, None, live, block, None)

    operands = (first_out, hidden_second, pieces, outer, own_targets, token_live, block_weights, head_weights)

    def at_front(first, second, mod, grad, target, live, block, head):
        return (
            do_head(first, target, live, head),
            zeros_like_of(do_second, second, mod, grad, live, block),
        )

    def at_back(first, second, mod, grad, target, live, block, head):
        return (
            zeros_like_of(do_head, first, target, live, head),
            do_second(second, mod, grad, live, block),
        )

    head_result, second_result = lax.cond(is_first, at_front, at_back, *operands)
    grad_hidden, loss_part, head_lefts, head_rights, head_sums = head_result
    arrived_back = lax.ppermute(second_result[0], axes, pairs_back)
    head_grads = reduce(head_lefts, head_rights, True, 2)

    def do_first(hidden, state, mod, extra, back_grad, block, other):
        grad_input, lefts, rights, bias_grads, grad_mod = block_backward(
            hidden, state, mod, block, wide(back_grad) + extra, members
        )
        return (narrow(grad_input),) + (lefts, rights, bias_grads, grad_mod)

    def keep_second(hidden, state, mod, extra, back_grad, block, other):
        return other

    stream, lefts, rights, bias_grads, grad_mod = lax.cond(
        is_first,
        do_first,
        keep_second,
        hidden_first,
        saved_state,
        pieces,
        grad_hidden,
        arrived_back,
        block_weights,
        second_result[1:],
    )
    down_grad, up_grad, attn_grad, qkv_grad = reduce(lefts, rights, False, 3)
    stream_own = swap(stream)
    mod_grad_all = lax.all_gather(swap(grad_mod), "dp", axis=0, tiled=True)
    mod_w_grad = product_left_t(silu_depth, mod_grad_all)
    mod_b_grad = lax.dynamic_slice_in_dim(column_sums(mod_grad_all), index * share, share, 0)
    silu_part = product_right_t(mod_grad_all, modulate_weight[0])
    silu_parts = lax.all_gather(silu_part, axes, axis=0, tiled=False)
    silu_total = jnp.sum(silu_parts.reshape((2, members) + silu_part.shape), 0)
    silu_total = jnp.swapaxes(silu_total, 0, 1).reshape(silu_part.shape[0], channels)
    cond_grad = local_grad(jax.nn.silu, conditioning, silu_total)
    table_grad = jnp.dot(one_hot.T, cond_grad, precision=HIGHEST)

    block_sums = jnp.concatenate(bias_grads)
    mine = (jnp.arange(2) == role).astype(jnp.float32)[:, None] * block_sums[None]
    sums = lax.psum((mine, head_sums, loss_part), axes)
    section_sums = sums[0][core]
    in_sums, mid_sums, out_sums = sums[1]
    bias_outs, offset = [], 0
    for part, grads in zip(section_biases, bias_grads):
        width = part.shape[0]
        bias_outs.append(
            lax.dynamic_slice_in_dim(section_sums, offset + index * width, width, 0)[None]
        )
        offset += grads.shape[0]
    device = core * members + index
    head_share = in_sums.shape[0] // (2 * members)
    loss_value = sums[2] / total_live
    return (
        stream_own[None],
        loss_value,
        table_grad,
        mod_w_grad[None],
        mod_b_grad[None],
        wide(qkv_grad)[None],
        bias_outs[0],
        wide(attn_grad)[None],
        bias_outs[1],
        wide(up_grad)[None],
        bias_outs[2],
        wide(down_grad)[None],
        bias_outs[3],
        wide(head_grads[2]).T,
        lax.dynamic_slice_in_dim(in_sums, device * head_share, head_share, 0),
        wide(head_grads[1]),
        lax.dynamic_slice_in_dim(mid_sums, device * head_share, head_share, 0),
        wide(head_grads[0]),
        out_sums,
    )


def solution(mesh):
    in_specs = (
        P("dp", None),
        P("dp", None),
        P("dp", None),
        P("dp"),
        P(),
        P(),
        P("section", "dp", None),
        P("section", "dp"),
        P("section", "dp", None),
        P("section", "dp"),
        P("section", "dp", None),
        P("section", "dp"),
        P("section", "dp", None),
        P("section", "dp"),
        P("section", "dp", None),
        P("section", "dp"),
        P("dp", None),
        P("dp"),
        P("dp", None),
        P("dp"),
        P("dp", None),
        P("dp"),
    )
    out_specs = (
        P("section", "dp", None),
        P(),
        P(),
        P("section", "dp", None),
        P("section", "dp"),
        P("section", "dp", None),
        P("section", "dp"),
        P("section", "dp", None),
        P("section", "dp"),
        P("section", "dp", None),
        P("section", "dp"),
        P("section", "dp", None),
        P("section", "dp"),
        P(None, ("section", "dp")),
        P(("section", "dp")),
        P(("section", "dp"), None),
        P(("section", "dp")),
        P(("section", "dp"), None),
        P(),
    )
    return jax.shard_map(
        on_device, mesh=mesh, in_specs=in_specs, out_specs=out_specs, check_vma=False
    )
```

time: 3780 us -> 1280 us (0.34)
  waiting for transfers between devices: 2760 us -> 9.93 us
  Pallas kernels: 0 us -> 678 us
  matrix products: 374 us -> 110 us
  other arithmetic: 256 us -> 42.7 us
  starting transfers between devices: 9.34 us -> 86.9 us
  blocking collectives: 247 us -> 175 us
    reduce_scatter x6 -> x0, waiting for transfers between devices: 1630 us -> none  [the longest x1 487 us: on_device(): lax.psum_scatter(block_total[0], 'dp', scatter_dimension=0, tiled=True)]
    all_gather x8 -> x0, waiting for transfers between devices: 741 us -> none  [the longest x1 185 us: on_device(): lax.all_gather(modulate_weight[0], 'dp', axis=0, tiled=True)]
    pallas_call x0 -> x4, Pallas kernels: none -> 678 us  [the longest x2 422 us: reduce(): pl.pallas_call(functools.partial(reduce_kernel, length, count, front_only...]
    unnamed x19 -> x3, waiting for transfers between devices: 379 us -> 0.03 us
    add x21 -> x2, other arithmetic: 172 us -> 0.61 us  [the longest x1 0.61 us: block_forward(): 1.0 + pieces[:, 4]]
    dot_general x24 -> x5, matrix products: 159 us -> 39.7 us  [product(): return jnp.dot(left_side, right_side, preferred_element_type=jnp.float32)]
    dot_general x12 -> x1, matrix products: 81.5 us -> 2.41 us  [product_left_t(): lax.dot_general(left_side, right_side, (((0,), (0,)), ((), ())), preferre...]
    ppermute x4 -> x7, starting transfers between devices: 8.66 us -> 86.8 us  [the longest x5 83.2 us: swap(): return lax.ppermute(values, axes, pairs_swap)]
  transfers between devices with their start and end apart: 21 -> 9, of which waited for: 14 -> 2; matrix products, arithmetic and copies ran while one was open for 8% -> 3% of each run, Pallas kernels for 0% -> 28%
where the time goes in v1:
time: 1280 us; the launch traced here: 1260 us
  Pallas kernels  678 us (53%)
  blocking collectives  175 us (14%)
  local copies, waits for them, and re-layouts  114 us (9%)
  matrix products  110 us (9%)
  starting transfers between devices  86.9 us (7%)
  other arithmetic  42.7 us (3%)
  loops' own time  26 us (2%)
  between operations  18.9 us (1%)
    pallas_call x2, Pallas kernels, reduce(): pl.pallas_call(functools.partial(reduce_kernel, length, count, front_only...  422 us
    pallas_call x2, Pallas kernels, gather(): pl.pallas_call(functools.partial(gather_kernel, length, count, front_only...  255 us
    ppermute x5, starting transfers between devices, swap(): return lax.ppermute(values, axes, pairs_swap)  83.2 us
    all_gather x1, blocking collectives, on_device(): silu_parts = lax.all_gather(silu_part, axes, axis=0, tiled=False)  67.3 us
    psum x1, blocking collectives, on_device(): sums = lax.psum((mine, head_sums, loss_part), axes)  50.9 us
    dot_general x5, matrix products, product_right_t(): lax.dot_general(left_side, right_side, (((1,), (1,)), ((), ())), preferre...  46.5 us
    all_gather x1, blocking collectives, on_device(): mod_grad_all = lax.all_gather(swap(grad_mod), 'dp', axis=0, tiled=True)  43 us
    dot_general x5, matrix products, product(): return jnp.dot(left_side, right_side, preferred_element_type=jnp.float32)  39.7 us
  transfers between devices with their start and end apart: 9, of which 2 were waited for; matrix products, arithmetic and copies ran while one was open for 3% of the time, Pallas kernels for 28%

profile of v1, /device:TPU:10, one launch (start us, length us, event | category | flops | bytes accessed | tf_op | source)
XLA Modules:
  0.0 1260.4 jit_solution(11528500082339297469)
XLA Ops:
  12.2 13.7 %all-reduce = s32[32]{0:T(128)S(1)} all-reduce(s32[32]{0:T(128)S(1)} %dynamic-update-slice), channel_id=1, replica_groups=mesh['section'=2,'dp'=16] {'dp'}, use_global_device_ids=true, to_apply=%add | all-reduce | flops 32 | bytes 256
  26.0 4.7 add_divide_fusion.2
  36.6 235.7 %shard_map.357 = (bf16[16,16,128]{2,1,0:T(8,128)(2,1)}, bf16[16,72,3456]{2,1,0:T(8,128)(2,1)}, bf16[16,72,1152]{2,1,0:T(8,128)(2,1)}, bf16[16,72,4608]{2,1,0:T(8,128)(2,1)}, bf16[16,288,1152]{2,1,0:T(8,128)(2,1)}) custom-call(bf16[16,128]{1,0:T(8,128)(2,1)} %bitcast.518, bf16[72,3456]{1,0:T(8,128)(2,1)} %bitcast.506, bf16[72,1152]{1,0:T(8,128)(2,1)} %bitcast.511, ...), custom_call_target="tpu_custom_call" | custom-call | bytes 510656512 | tf_op jit(solution)/shard_map/pallas_call | solution.py:245
  275.2 4.4 collective-permute-start.1
  283.8 26.9 %conditional.3 = (bf16[512,1152]{1,0:T(8,128)(2,1)S(1)}, bf16[512,3456]{1,0:T(8,128)(2,1)}, bf16[2,16,256,256]{2,3,1,0:T(8,128)(2,1)}, bf16[512,1152]{0,1:T(8,12...) conditional(s32[]{:T(128)} %convert_element_type.315, () %tuple.41, ...), branch_computations={%region_1.2_spmd, %region_2.9_spmd} | conditional | flops 16975927296 | bytes 248839072 | solution.py:692
  283.8 4.7 broadcast.485
  313.1 71.3 %collective-permute-start.3 = (bf16[512,768]{1,0:T(8,128)(2,1)}, bf16[512,768]{1,0:T(8,128)(2,1)S(1)}, u32[]{:S(2)}, u32[]{:S(2)}) collective-permute-start(bf16[512,768]{1,0:T(8,128)(2,1)} %param.30), channel_id=1, source_target_pairs={{0,0},{16,1},{1,16},{17,17},{2,2},{18,3},{3,18},{19,19},{4,4},{20,... | collective-permute-start | bytes 2359304 | tf_op jit(solution)/shard_map/ppermute | solution.py:736
  386.3 19.7 %shard_map.358 = (bf16[16,72,2048]{2,1,0:T(8,128)(2,1)}, bf16[16,128,2048]{2,1,0:T(8,128)(2,1)}, bf16[16,128,768]{2,1,0:T(8,128)(2,1)}) custom-call(bf16[72,2048]{1,0:T(8,128)(2,1)} %refs_0_.1, bf16[128,2048]{1,0:T(8,128)(2,1)} %refs_1_.1, bf16[128,768]{1,0:T(8,128)(2,1)} %refs_2_.1), custom_call_target="tpu_custom_call" | custom-call | bytes 260046848 | tf_op jit(solution)/shard_map/pallas_call | solution.py:245
  407.2 8.8 collective-permute-done.3
  416.0 206.6 %conditional.4 = (f32[512,1152]{1,0:T(8,128)S(1)}, f32[]{:T(128)}, bf16[8,2,128,512]{3,2,1,0:T(8,128)(2,1)}, bf16[8,2,128,512]{3,2,1,0:T(8,128)(2,1)}, bf16[8,2,...) conditional(s32[]{:T(128)} %convert_element_type.315, ...), branch_computations={%region_9.31_spmd, %region_31.40_spmd} | conditional | flops 34635816960 | bytes 608866496 | solution.py:849
  419.1 9.6 add_convert_fusion.1
  428.7 13.6 %reshape.669 = bf16[2,256,3,16,72]{4,3,2,1,0:T(8,128)(2,1)} reshape(bf16[512,3456]{1,0:T(8,128)(2,1)} %add_convert_fusion.1) | data formatting | bytes 7077888 | tf_op jit(solution)/shard_map/cond/branch_0_fun/reshape | solution.py:534
  442.4 6.0 fusion.159
  456.1 6.3 fusion.161
  476.4 5.0 fusion.150
  484.8 10.5 fusion.42
  495.2 15.9 %convert_reduce_fusion.1 = (f32[4608]{0:T(1024)}, bf16[512,4608]{1,0:T(8,128)(2,1)}) fusion(f32[512,4608]{1,0:T(8,128)} %get-tuple-element.728, f32[4608]{0:T(1024)S(1)} %get-tuple-element.187, bf16[512,1152]{1,0:T(8,128)(2,1)} %get-tuple-element.805, bf16[4608,1152]{1,0:T(8,128)(2,1)S(1)} %bitcast.479), kind=kOutput, calls=%fused_computation.75 | convolution fusion | flops 5490077184 | bytes 25989120 | tf_op jit(solution)/shard_map/cond/branch_0_fun/dot_general | solution.py:37
  511.1 12.6 %fusion.63 = (f32[512]{0:T(512)S(1)}, f32[512]{0:T(512)S(1)}, f32[512,1152]{1,0:T(8,128)}) fusion(f32[2,1152]{1,0:T(2,128)S(1)} %get-tuple-element.711, f32[512]{0:T(512)S(1)} %add_rsqrt_fusion.2, f32[512,1152]{1,0:T(8,128)S(1)} %get-tuple-element.671, f32[512]{0:T(512)S(1)} %broadcast_multiply_fusion.6, bf16[512,4608]{1,0:T(8,128)(2,1)} %get-tuple-element.806, ...), kind=kOutput, calls=%fused_computation.131 | convolution fusion | flops 5439355904 | bytes 20071424 | tf_op jit(solution)/shard_map/cond/branch_0_fun/dot_general | solution.py:37
  523.8 13.5 %convert_reduce_fusion.4 = (f32[1152]{0:T(1024)}, bf16[512,1152]{1,0:T(8,128)(2,1)}, bf16[512,1152]{1,0:T(8,128)(2,1)}, f32[512,1152]{1,0:T(8,128)}) fusion(f32[512,1152]{1,0:T(8,128)} %get-tuple-element.663, f32[512]{0:T(512)S(1)} %broadcast_multiply_fusion.4, f32[512,1152]{1,0:T(8,128)S(1)} %get-tuple-element.671, f32[512]{0:T(512)S(1)} %broadcast_multiply_fusion.6, ...), kind=kOutput, calls=%fused_computation.117 | convolution fusion | flops 5469436928 | bytes 31916032 | tf_op jit(solution)/shard_map/cond/branch_0_fun/dot_general | solution.py:27
  540.4 4.7 reshape.670
  551.9 4.4 fusion.44
  565.2 14.5 %multiply_reduce_fusion.11 = (f32[2,256]{1,0:T(2,128)S(1)}, f32[2,256]{1,0:T(2,128)S(1)}, bf16[2,1152]{1,0:T(2,128)(2,1)S(1)}, bf16[2,1152]{1,0:T(2,128)(2,1)S(1...) fusion(f32[2,1152]{1,0:T(2,128)S(1)} %get-tuple-element.714, ...), kind=kOutput, calls=%fused_computation.132 | convolution fusion | flops 4094543360 | bytes 25729024 | tf_op jit(solution)/shard_map/cond/branch_0_fun/dot_general | solution.py:37
  580.0 5.9 add_convert_fusion.2
  592.0 6.7 copy.241
  624.9 50.9 %all-reduce.2 = (f32[]{:T(128)}, f32[2048]{0:T(1024)S(1)}, f32[2048]{0:T(1024)S(1)}, f32[768]{0:T(1024)}) all-reduce(f32[]{:T(128)} %get-tuple-element.335, f32[2048]{0:T(1024)S(1)} %get-tuple-element.360, f32[2048]{0:T(1024)S(1)} %get-tuple-element.362, ...), channel_id=1, replica_groups=mesh['section'=2,'dp'=16] {'section','dp'}, use_global_device_ids=true, to_apply=%region_61.62 | all-reduce | flops 4865 | bytes 38920 | tf_op jit(solution)/shard_map/psum | solution.py:889
  675.8 94.9 %shard_map.360 = (bf16[64,768]{1,0:T(8,128)(2,1)}, bf16[64,2048]{1,0:T(8,128)(2,1)}, bf16[64,1152]{1,0:T(8,128)(2,1)}) custom-call(bf16[8,2,128,512]{3,2,1,0:T(8,128)(2,1)} %get-tuple-element.353.refs_0_, bf16[8,2,128,512]{3,2,1,0:T(8,128)(2,1)} %get-tuple-element.354.refs_1_, bf16[8,2,128,512]{3,2,1,0:T(8,128)(2,1)} %get-tuple-element.355.refs_2_, ...), custom_call_target="tpu_custom_call" | custom-call | flops 8321499136 | bytes 260046848 | tf_op jit(solution)/shard_map/pallas_call | solution.py:463
  777.6 11.5 conditional.5
  777.6 5.8 copy.282
  789.1 327.4 %shard_map.359 = (bf16[288,1152]{1,0:T(8,128)(2,1)}, bf16[72,4608]{1,0:T(8,128)(2,1)}, bf16[72,1152]{1,0:T(8,128)(2,1)}, bf16[72,3456]{1,0:T(8,128)(2,1)}) custom-call(bf16[8,2,288,512]{3,2,1,0:T(8,128)(2,1)} %get-tuple-element.337.refs_0_, bf16[8,2,72,512]{3,2,1,0:T(8,128)(2,1)} %get-tuple-element.338.refs_1_, ...), custom_call_target="tpu_custom_call" | custom-call | flops 16307453952 | bytes 509607936 | tf_op jit(solution)/shard_map/pallas_call | solution.py:463
  1128.2 43.0 %all-gather.1 = bf16[16,2,6912]{2,1,0:T(2,128)(2,1)S(1)} all-gather(bf16[1,2,6912]{2,1,0:T(2,128)(2,1)S(1)} %bitcast.513), channel_id=1, replica_groups=mesh['section'=2,'dp'=16] {'dp'}, dimensions={0}, use_global_device_ids=true | all-gather | bytes 470016 | tf_op jit(solution)/shard_map/all_gather | solution.py:877
  1171.8 67.3 %all-gather = f32[1024,72]{1,0:T(8,128)S(1)} all-gather(f32[32,72]{1,0:T(8,128)S(1)} %fusion.132), channel_id=2, replica_groups=mesh['section'=2,'dp'=16] {'section','dp'}, dimensions={0}, use_global_device_ids=true | all-gather | bytes 304128 | tf_op jit(solution)/shard_map/all_gather | solution.py:881
  1241.8 4.4 fusion.137
  (277 shorter events, 129.7 us)
Async XLA Ops:
  7.2 24.7 %copy-start = (bf16[1,72,6912]{2,1,0:T(8,128)(2,1)S(1)}, bf16[1,72,6912]{2,1,0:T(8,128)(2,1)}, u32[]{:S(2)}) copy-start(bf16[1,72,6912]{2,1,0:T(8,128)(2,1)} %param.34) | copy-start | bytes 2985988
  7.2 18.7 %copy-start.65 = (bf16[1,432]{1,0:T(2,128)(2,1)S(1)}, bf16[1,432]{1,0:T(2,128)(2,1)}, u32[]{:S(2)}) copy-start(bf16[1,432]{1,0:T(2,128)(2,1)} %param.35) | copy-start | bytes 2596
  7.2 267.0 %all-reduce.8.cloned.1.call-start = ((), (), s32[]{:S(2)}) async-start(), calls=%async_computation.1 | async-start | bytes 1769472
  8.8 273.6 %collective-permute-start = (bf16[512,1152]{1,0:T(8,128)(2,1)S(1)}, bf16[512,1152]{1,0:T(8,128)(2,1)S(1)}, u32[]{:S(2)}, u32[]{:S(2)}) collective-permute-start(bf16[512,1152]{1,0:T(8,128)(2,1)S(1)} %broadcast_select_fusion.1), channel_id=1, source_target_pairs={{0,0},{16,1},{1,16},{17,17},{2,2},{18,3},{3,18},{19,19},{4,4},{20,... | collective-permute-start | bytes 3538952 | tf_op jit(solution)/shard_map/ppermute | solution.py:736
  30.7 241.7 %copy-start.43 = (f32[32,1152]{1,0:T(8,128)}, f32[32,1152]{1,0:T(8,128)S(1)}, u32[]{:S(2)}) copy-start(f32[32,1152]{1,0:T(8,128)S(1)} %get-tuple-element.765) | copy-start | bytes 442372
  31.6 240.8 %copy-start.48 = (bf16[32,72]{1,0:T(8,128)(2,1)}, bf16[32,72]{1,0:T(8,128)(2,1)S(1)}, u32[]{:S(2)}) copy-start(bf16[32,72]{1,0:T(8,128)(2,1)S(1)} %fusion.145) | copy-start | bytes 13828
  33.1 1213.9 %all-reduce.6.cloned.1.call-start = ((), (), s32[]{:S(2)}) async-start(), calls=%async_computation | async-start | bytes 147456 | tf_op jit(solution)/shard_map/psum | solution.py:889
  273.3 7.2 copy-start.46
  275.2 6.3 collective-permute-start.1
  283.1 101.3 %copy-start.76 = (s32[16]{0:T(128)S(1)}, s32[16]{0:T(128)}, u32[]{:S(2)}) copy-start(s32[16]{0:T(128)} %param.32) | copy-start | bytes 196
  311.8 104.2 %collective-permute-start.2 = (bf16[512,1152]{1,0:T(8,128)(2,1)}, bf16[512,1152]{1,0:T(8,128)(2,1)S(1)}, u32[]{:S(2)}, u32[]{:S(2)}) collective-permute-start(bf16[512,1152]{1,0:T(8,128)(2,1)} %get-tuple-element.304), channel_id=1, source_target_pairs={{0,1},{16,17},{2,3},{18,19},{4,5},{20,21},{6,7},{22,23},{8,9},{24,... | collective-permute-start | bytes 3538952 | tf_op jit(solution)/shard_map/ppermute | solution.py:805
  313.1 103.0 %collective-permute-start.3 = (bf16[512,768]{1,0:T(8,128)(2,1)}, bf16[512,768]{1,0:T(8,128)(2,1)S(1)}, u32[]{:S(2)}, u32[]{:S(2)}) collective-permute-start(bf16[512,768]{1,0:T(8,128)(2,1)} %param.30), channel_id=1, source_target_pairs={{0,0},{16,1},{1,16},{17,17},{2,2},{18,3},{3,18},{19,19},{4,4},{20,... | collective-permute-start | bytes 2359304 | tf_op jit(solution)/shard_map/ppermute | solution.py:736
  416.3 12.5 copy-start.50
  416.7 12.0 copy-start.54
  476.4 8.3 slice-start.9
  476.4 8.3 slice-start.10
  484.0 11.2 slice-start.3
  484.7 10.5 copy-start.38
  484.7 10.5 slice-start.4
  484.7 10.5 slice-start.5
  523.7 13.5 %copy-start.56 = (f32[512]{0:T(512)}, f32[512]{0:T(512)S(1)}, u32[]{:S(2)}) copy-start(f32[512]{0:T(512)S(1)} %broadcast_multiply_fusion.4) | copy-start | bytes 6148 | tf_op jit(solution)/shard_map/cond
  523.7 13.5 %copy-start.58 = (f32[512]{0:T(512)}, f32[512]{0:T(512)S(1)}, u32[]{:S(2)}) copy-start(f32[512]{0:T(512)S(1)} %broadcast_multiply_fusion.5) | copy-start | bytes 6148 | tf_op jit(solution)/shard_map/cond
  523.7 13.5 %copy-start.25 = (bf16[1152,1152]{1,0:T(8,128)(2,1)S(1)}, bf16[1152,1152]{1,0:T(8,128)(2,1)}, u32[]{:S(2)}) copy-start(bf16[1152,1152]{1,0:T(8,128)(2,1)} %get-tuple-element.183) | copy-start | bytes 7962628 | tf_op jit(solution)/shard_map/cond
  592.0 6.7 copy-start.39
  622.6 53.2 %copy-start.27 = (f32[512,1152]{1,0:T(8,128)}, f32[512,1152]{1,0:T(8,128)S(1)}, u32[]{:S(2)}) copy-start(f32[512,1152]{1,0:T(8,128)S(1)} %get-tuple-element.323) | copy-start | bytes 7077892
  622.6 155.0 %collective-permute-start.4 = (bf16[512,1152]{1,0:T(8,128)(2,1)}, bf16[512,1152]{1,0:T(8,128)(2,1)}, u32[]{:S(2)}, u32[]{:S(2)}) collective-permute-start(bf16[512,1152]{1,0:T(8,128)(2,1)} %get-tuple-element.322), channel_id=1, source_target_pairs={{1,0},{17,16},{3,2},{19,18},{5,4},{21,20},{7,6},{23,22},{9,8},{25,... | collective-permute-start | bytes 3538952 | tf_op jit(solution)/shard_map/ppermute | solution.py:851
  675.8 101.8 %copy-start.2 = (bf16[512,1152]{1,0:T(8,128)(2,1)S(1)}, bf16[512,1152]{1,0:T(8,128)(2,1)}, u32[]{:S(2)}) copy-start(bf16[512,1152]{1,0:T(8,128)(2,1)} %copy-done.1) | copy-start | bytes 3538948
  1118.9 6.2 copy-start.47
  1121.9 6.3 collective-permute-start.6
  1125.9 125.0 %collective-permute-start.5 = (bf16[512,1152]{1,0:T(8,128)(2,1)}, bf16[512,1152]{1,0:T(8,128)(2,1)S(1)}, u32[]{:S(2)}, u32[]{:S(2)}) collective-permute-start(bf16[512,1152]{1,0:T(8,128)(2,1)} %get-tuple-element.334), channel_id=1, source_target_pairs={{0,0},{16,1},{1,16},{17,17},{2,2},{18,3},{3,18},{19,19},{4,4},{20,... | collective-permute-start | bytes 3538952 | tf_op jit(solution)/shard_map/ppermute | solution.py:736
  1171.7 70.1 %copy-start.44 = (f32[32,1152]{1,0:T(8,128)S(1)}, f32[32,1152]{1,0:T(8,128)}, u32[]{:S(2)}) copy-start(f32[32,1152]{1,0:T(8,128)} %copy-done.43) | copy-start | bytes 442372
  1171.8 70.1 %copy-start.63 = (s32[32]{0:T(128)S(1)}, s32[32]{0:T(128)}, u32[]{:S(2)}) copy-start(s32[32]{0:T(128)} %copy-done.62) | copy-start | bytes 388
  (42 other events, 128.0 us)
Sparse Core Ops, SparseCore 0:
  33.3 120.2 all-reduce.7
  1121.0 121.3 all-reduce.5

commit v2 on v1

v2 whole, which is shorter than its diff:
```python
import functools
import jax
import jax.numpy as jnp
from jax import lax
from jax.experimental import pallas as pl
from jax.experimental.pallas import tpu as pltpu
from jax.sharding import PartitionSpec as P

HEADS = 16
SEQ = 256
EPSILON = 1e-06
HIGHEST = lax.Precision.HIGHEST
MESH = pl.DeviceIdType.MESH
ANY = pl.BlockSpec(memory_space=pl.ANY)
DMA = pltpu.SemaphoreType.DMA
VMEM_BYTES = 60 * 2**20


def narrow(values):
    return values.astype(jnp.bfloat16)


def wide(values):
    return values.astype(jnp.float32)


def product(left_side, right_side):
    return jnp.dot(left_side, right_side, preferred_element_type=jnp.float32)


def product_left_t(left_side, right_side):
    return lax.dot_general(
        left_side, right_side, (((0,), (0,)), ((), ())), preferred_element_type=jnp.float32
    )


def product_right_t(left_side, right_side):
    return lax.dot_general(
        left_side, right_side, (((1,), (1,)), ((), ())), preferred_element_type=jnp.float32
    )


def ring_of(place, length):
    half, side = place // 2, place % 2
    return side * (length - 1 - half) + (1 - side) * half


def place_of(spot, length):
    side = spot // (length // 2)
    half = side * (length - 1 - spot) + (1 - side) * spot
    return 2 * half + side


def whereabouts(length):
    core = lax.axis_index("section")
    index = lax.axis_index("dp")
    place, role = index // 2, index % 2
    spot = ring_of(place, length)
    step = 1 - 2 * core

    def at(offset):
        return place_of(lax.rem(spot + step * offset + 4 * length, length), length)

    return dict(
        core=core,
        place=place,
        role=role,
        at=at,
        onward=(core, 2 * at(1) + role),
        before=(core, 2 * at(-1) + role),
        sibling=(1 - core, index),
        partner=(1 - core, 2 * place + 1 - role),
    )


def greet(devices):
    barrier = pltpu.get_barrier_semaphore()
    for device in devices:
        pl.semaphore_signal(barrier, inc=1, device_id=device, device_id_type=MESH)
    pl.semaphore_wait(barrier, len(devices))


def remote(source, target, send_sem, recv_sem, device):
    return pltpu.make_async_remote_copy(
        src_ref=source,
        dst_ref=target,
        send_sem=send_sem,
        recv_sem=recv_sem,
        device_id=device,
        device_id_type=MESH,
    )


def each(first, last, body):
    def step(index, carry):
        body(index)
        return carry

    lax.fori_loop(first, last, step, 0)


def gather_kernel(length, count, heads, *refs):
    total = count + heads
    shards, mod_part = refs[:total], refs[total]
    full, mod_all = refs[total + 1 : 2 * total + 1], refs[2 * total + 1]
    (
        own_sem, swap_send, swap_recv, ring_send, ring_recv, side_send, side_recv,
        cross_send, cross_recv, mod_send, mod_recv, mod_sem,
    ) = refs[2 * total + 2 :]
    me = whereabouts(length)
    core, role, place, at = me["core"], me["role"], me["place"], me["at"]
    members = 2 * length
    index = 2 * place + role
    neighbour = (core, 2 * place + 1 - role)
    mine = 2 * place + core
    layers, head_layers = range(count), range(count, total)

    barrier = pltpu.get_barrier_semaphore()

    def signal(device):
        pl.semaphore_signal(barrier, inc=1, device_id=device, device_id_type=MESH)

    def greet_all(peer):
        other = (peer // members, lax.rem(peer, members))

        @pl.when((other[0] != core) | (other[1] != index))
        def _():
            signal(other)

    each(0, 2 * members, greet_all)
    pl.semaphore_wait(barrier, 2 * members - 1)

    def block(layer, turn):
        return full[layer].at[2 * at(-turn) + core]

    def onward(layer, turn):
        part = block(layer, turn)
        return remote(
            part, part, ring_send.at[layer, turn], ring_recv.at[layer, turn], me["onward"]
        )

    def across(layer, turn):
        part = block(layer, turn)
        return remote(
            part, part, side_send.at[layer, turn], side_recv.at[layer, turn], me["sibling"]
        )

    def from_sibling(layer, turn):
        part = full[layer].at[2 * at(turn) + 1 - core]
        return remote(
            part, part, side_send.at[layer, turn], side_recv.at[layer, turn], me["sibling"]
        )

    def own(layer):
        return pltpu.make_async_copy(shards[layer], full[layer].at[mine], own_sem.at[layer])

    def swap_out(layer):
        return remote(
            shards[layer], full[layer].at[index], swap_send.at[layer], swap_recv.at[layer],
            me["partner"],
        )

    def swap_in(layer):
        return remote(
            shards[layer], full[layer].at[mine], swap_send.at[layer], swap_recv.at[layer],
            me["partner"],
        )

    def lend(layer):
        return remote(
            shards[layer], full[layer].at[2 * place], swap_send.at[layer], swap_recv.at[layer],
            neighbour,
        )

    def cross(layer, turn):
        part = block(layer, turn)
        return remote(
            part, part, cross_send.at[layer - count, turn], cross_recv.at[layer - count, turn],
            neighbour,
        )

    @pl.when(core == role)
    def _():
        for layer in layers:
            own(layer).start()

    @pl.when(core != role)
    def _():
        for layer in layers:
            swap_out(layer).start()

    @pl.when(core == role)
    def _():
        for layer in head_layers:
            own(layer).start()

    @pl.when((core == 0) & (role == 0))
    def _():
        for layer in head_layers:
            lend(layer).start()

    def mod_target(peer):
        return (lax.rem(peer, 2), 2 * (peer // 2) + core)

    def mod_copy(peer):
        return remote(
            mod_part.at[peer], mod_all.at[index], mod_send.at[peer], mod_recv.at[index],
            mod_target(peer),
        )

    def mod_is_own(peer):
        return (core == role) & (peer == mine)

    mod_own = pltpu.make_async_copy(mod_part.at[mine], mod_all.at[index], mod_sem)

    def spread_mod():
        def start(peer):
            @pl.when(jnp.logical_not(mod_is_own(peer)))
            def _():
                mod_copy(peer).start()

        each(0, members, start)

        @pl.when(core == role)
        def _():
            mod_own.start()

    def gathered_mod():
        @pl.when(core == role)
        def _():
            mod_own.wait()

        def sent(peer):
            @pl.when(jnp.logical_not(mod_is_own(peer)))
            def _():
                mod_copy(peer).wait_send()

        each(0, members, sent)

        def came(source):
            @pl.when(jnp.logical_not((core == role) & (source == index)))
            def _():
                remote(
                    mod_part.at[0], mod_all.at[source], mod_send.at[0], mod_recv.at[source],
                    me["sibling"],
                ).wait_recv()

        each(0, members, came)

    def begin(layer):
        @pl.when(core == role)
        def _():
            own(layer).wait()

        @pl.when(core != role)
        def _():
            swap_in(layer).wait_recv()

        onward(layer, 0).start()
        across(layer, 0).start()

    def ring_turn(turn, more):
        for layer in layers:
            onward(layer, turn - 1).wait_recv()
            if more:
                onward(layer, turn).start()
            across(layer, turn).start()

    def ring_end():
        def end(turn):
            for layer in layers:
                onward(layer, turn).wait_send()
                across(layer, turn).wait_send()
                from_sibling(layer, turn).wait_recv()

        each(0, length - 1, end)
        for layer in layers:
            across(layer, length - 1).wait_send()
            from_sibling(layer, length - 1).wait_recv()

    def front_head(turn, first):
        for layer in head_layers:
            if first:

                @pl.when(core == 0)
                def _():
                    own(layer).wait()

                @pl.when(core == 1)
                def _():
                    cross(layer, turn).wait_recv()

            else:
                cross(layer, turn).wait_recv()
            across(layer, turn).start()

    @pl.when(role == 0)
    def _():
        for layer in layers:
            begin(layer)
        spread_mod()
        front_head(0, True)
        ring_turn(1, True)
        late = 2

        def turn_body(turn):
            ring_turn(turn, True)

            @pl.when(turn > late)
            def _():
                front_head(turn - late, False)

        each(2, length - 1, turn_body)
        ring_turn(length - 1, False)
        each(length - 1 - late, length, lambda turn: front_head(turn, False))
        ring_end()
        gathered_mod()

        def head_end(turn):
            for layer in head_layers:
                across(layer, turn).wait_send()
                from_sibling(layer, turn).wait_recv()

        each(0, length, head_end)

        @pl.when(core == 0)
        def _():
            for layer in head_layers:
                lend(layer).wait_send()

    @pl.when(role == 1)
    def _():
        spread_mod()
        for layer in head_layers:

            @pl.when(core == 1)
            def _():
                own(layer).wait()
                cross(layer, 0).start()

            @pl.when(core == 0)
            def _():
                lend(layer).wait_recv()

            onward(layer, 0).start()

        def head_turn(turn):
            for layer in head_layers:
                onward(layer, turn - 1).wait_recv()

                @pl.when(turn < length - 1)
                def _():
                    onward(layer, turn).start()

                cross(layer, turn).start()

        each(1, length, head_turn)
        for layer in layers:
            begin(layer)
        each(1, length - 1, lambda turn: ring_turn(turn, True))
        ring_turn(length - 1, False)
        ring_end()
        gathered_mod()

        def head_end(turn):
            for layer in head_layers:

                @pl.when(turn < length - 1)
                def _():
                    onward(layer, turn).wait_send()

                @pl.when((turn > 0) | (core == 1))
                def _():
                    cross(layer, turn).wait_send()

        each(0, length, head_end)

    @pl.when(core != role)
    def _():
        for layer in layers:
            swap_out(layer).wait_send()


def gather(shards, head_shards, mod_part, collective_id):
    members = lax.axis_size("dp")
    length, count, heads = members // 2, len(shards), len(head_shards)
    total = count + heads
    everything = list(shards) + list(head_shards)
    moved = sum(shard.size * 2 for shard in everything) * members
    inside = pl.BlockSpec(memory_space=pltpu.VMEM)
    results = pl.pallas_call(
        functools.partial(gather_kernel, length, count, heads),
        name="gather",
        out_shape=[jax.ShapeDtypeStruct((members,) + s.shape, s.dtype) for s in everything]
        + [jax.ShapeDtypeStruct((members,) + mod_part.shape[1:], mod_part.dtype)],
        in_specs=[inside] * (total + 1),
        out_specs=[ANY] * (total + 1),
        scratch_shapes=[
            DMA((total,)),
            DMA((total,)),
            DMA((total,)),
            DMA((total, length)),
            DMA((total, length)),
            DMA((total, length)),
            DMA((total, length)),
            DMA((heads, length)),
            DMA((heads, length)),
            DMA((members,)),
            DMA((members,)),
            DMA(()),
        ],
        compiler_params=pltpu.CompilerParams(
            collective_id=collective_id, has_side_effects=True, vmem_limit_bytes=VMEM_BYTES
        ),
        cost_estimate=pl.CostEstimate(flops=0, bytes_accessed=16 * moved, transcendentals=0),
    )(*everything, mod_part)
    return results[:count], results[count:total], results[total]


def tile_of(columns):
    for tile in (512, 384, 256, 128):
        if columns % tile == 0:
            return tile
    return columns


class Ring:
    def __init__(self, me, length, lefts, rights, scratch):
        count = len(lefts)
        self.me, self.length, self.layers = me, length, range(count)
        self.lefts, self.rights = lefts, rights
        self.left_all, self.right_all = scratch[:count], scratch[count : 2 * count]
        self.arrived, self.leaving = scratch[2 * count : 3 * count], scratch[3 * count : 4 * count]
        (
            self.own_sem, self.side_send, self.side_recv, self.ring_send, self.ring_recv,
        ) = scratch[4 * count : 4 * count + 5]

    @staticmethod
    def scratch(length, rows, columns, tokens):
        bf16, count = jnp.bfloat16, len(rows)
        return (
            [pltpu.VMEM((2, length, r, tokens), bf16) for r in rows]
            + [pltpu.VMEM((2, tokens, c), bf16) for c in columns]
            + [pltpu.VMEM((length - 1, r, c), bf16) for r, c in zip(rows, columns)]
            + [pltpu.VMEM((2, r, c), bf16) for r, c in zip(rows, columns)]
            + [
                DMA((count, 2)),
                DMA((count, 2)),
                DMA((count, 2)),
                DMA((count, 2)),
                DMA((count, length)),
            ]
        )

    def chunk(self, layer, slot, turn, add):
        spot = self.me["at"](-(turn + 1))
        columns = self.rights[layer].shape[1]
        tile = tile_of(columns)
        left, right = self.left_all[layer], self.right_all[layer]

        def body(index):
            start = pl.multiple_of(index * tile, tile)
            total = product(left[0, spot], right[0, :, pl.ds(start, tile)]) + product(
                left[1, spot], right[1, :, pl.ds(start, tile)]
            )
            if add:
                total = total + wide(self.arrived[layer][turn - 1, :, pl.ds(start, tile)])
            self.leaving[layer][slot, :, pl.ds(start, tile)] = narrow(total)

        each(0, columns // tile, body)

    def onward(self, layer, slot, turn):
        return remote(
            self.leaving[layer].at[slot],
            self.arrived[layer].at[turn],
            self.ring_send.at[layer, slot],
            self.ring_recv.at[layer, turn],
            self.me["onward"],
        )

    def inputs(self, layer):
        core, sibling = self.me["core"], self.me["sibling"]
        return [
            pltpu.make_async_copy(
                self.lefts[layer].at[:, core], self.left_all[layer].at[0], self.own_sem.at[layer, 0]
            ),
            pltpu.make_async_copy(
                self.rights[layer], self.right_all[layer].at[0], self.own_sem.at[layer, 1]
            ),
            remote(
                self.lefts[layer].at[:, 1 - core],
                self.left_all[layer].at[1],
                self.side_send.at[layer, 0],
                self.side_recv.at[layer, 0],
                sibling,
            ),
            remote(
                self.rights[layer],
                self.right_all[layer].at[1],
                self.side_send.at[layer, 1],
                self.side_recv.at[layer, 1],
                sibling,
            ),
        ]

    def run(self, finish):
        length = self.length
        for layer in self.layers:
            for copy in self.inputs(layer):
                copy.start()
        for layer in self.layers:
            for copy in self.inputs(layer):
                copy.wait()
            self.chunk(layer, 0, 0, False)
            self.onward(layer, 0, 0).start()

        def turn_body(turn):
            slot = lax.rem(turn, 2)
            for layer in self.layers:
                self.onward(layer, slot, turn - 1).wait_recv()

                @pl.when(turn >= 2)
                def _():
                    self.onward(layer, slot, turn).wait_send()

                self.chunk(layer, slot, turn, True)
                self.onward(layer, slot, turn).start()

        each(1, length - 1, turn_body)
        slot = (length - 1) % 2
        for layer in self.layers:
            self.onward(layer, slot, length - 2).wait_recv()
            if length >= 3:
                self.onward(layer, slot, length - 2).wait_send()
            self.chunk(layer, slot, length - 1, True)
            finish(layer, slot)
        for layer in self.layers:
            self.onward(layer, 1 - slot, length - 2).wait_send()


def ring_cost(length, rows, columns, tokens):
    work = sum(r * c for r, c in zip(rows, columns)) * length
    return pl.CostEstimate(flops=4 * work * tokens, bytes_accessed=64 * work, transcendentals=0)


def head_reduce_kernel(length, count, *refs):
    lefts, rights, outs = refs[:count], refs[count : 2 * count], refs[2 * count : 3 * count]
    scratch = refs[3 * count :]
    last_sem = scratch[-1]
    me = whereabouts(length)

    @pl.when(me["role"] == 0)
    def _():
        greet([me["onward"], me["before"], me["sibling"]])
        ring = Ring(me, length, lefts, rights, scratch[:-1])

        def last(layer, slot):
            return pltpu.make_async_copy(
                ring.leaving[layer].at[slot], outs[layer], last_sem.at[layer]
            )

        ring.run(lambda layer, slot: last(layer, slot).start())
        for layer in ring.layers:
            last(layer, (length - 1) % 2).wait()


def head_reduce(lefts, rights, collective_id):
    length, count = lax.axis_size("dp") // 2, len(lefts)
    rows = [left.shape[2] for left in lefts]
    columns = [right.shape[1] for right in rights]
    tokens = rights[0].shape[0]
    return pl.pallas_call(
        functools.partial(head_reduce_kernel, length, count),
        name="head_reduce",
        out_shape=[jax.ShapeDtypeStruct((r, c), jnp.bfloat16) for r, c in zip(rows, columns)],
        in_specs=[ANY] * (2 * count),
        out_specs=[ANY] * count,
        scratch_shapes=Ring.scratch(length, rows, columns, tokens) + [DMA((count,))],
        compiler_params=pltpu.CompilerParams(
            collective_id=collective_id, has_side_effects=True, vmem_limit_bytes=VMEM_BYTES
        ),
        cost_estimate=ring_cost(length, rows, columns, tokens),
    )(*lefts, *rights)


def reduce_kernel(length, count, heads, *refs):
    lefts, rights = refs[:count], refs[count : 2 * count]
    head_parts = refs[2 * count : 2 * count + heads]
    stream, mod, bias, head_sums = refs[2 * count + heads : 2 * count + heads + 4]
    refs = refs[2 * count + heads + 4 :]
    outs, head_outs = refs[:count], refs[count : count + heads]
    stream_out, mod_all, bias_all, head_all = refs[count + heads : count + heads + 4]
    scratch = refs[count + heads + 4 :]
    (
        last_send, last_recv, part_send, part_recv, stream_send, stream_recv, small_send,
        mod_recv, bias_recv, head_recv, keep_sem,
    ) = scratch[-11:]
    me = whereabouts(length)
    core, role, place = me["core"], me["role"], me["place"]
    members = 2 * length
    index, mine = 2 * place + role, 2 * place + core
    barrier = pltpu.get_barrier_semaphore()

    def greet_all(peer):
        other = (peer // members, lax.rem(peer, members))

        @pl.when((other[0] != core) | (other[1] != index))
        def _():
            pl.semaphore_signal(barrier, inc=1, device_id=other, device_id_type=MESH)

    each(0, 2 * members, greet_all)
    pl.semaphore_wait(barrier, 2 * members - 1)

    stream_copy = remote(stream, stream_out, stream_send, stream_recv, me["partner"])

    @pl.when(core != role)
    def _():
        stream_copy.start()

    def small(source, target, send, recv, device):
        return remote(source, target, send, recv, device)

    def mod_copy(peer):
        return small(
            mod, mod_all.at[mine], small_send.at[0, peer], mod_recv.at[mine], (role, peer)
        )

    def bias_copy(peer):
        return small(
            bias.at[peer], bias_all.at[mine], small_send.at[1, peer], bias_recv.at[mine],
            (role, peer),
        )

    def head_copy(peer):
        return small(
            head_sums.at[peer], head_all.at[mine], small_send.at[2, peer], head_recv.at[mine],
            (peer // members, lax.rem(peer, members)),
        )

    own_mod = pltpu.make_async_copy(mod, mod_all.at[mine], keep_sem.at[0])
    own_bias = pltpu.make_async_copy(bias.at[index], bias_all.at[mine], keep_sem.at[1])
    own_head = pltpu.make_async_copy(
        head_sums.at[core * members + index], head_all.at[mine], keep_sem.at[2]
    )

    def smalls(act_mod, act_head, act_own):
        def to_section(peer):
            @pl.when((core != role) | (peer != index))
            def _():
                act_mod(mod_copy(peer))
                act_mod(bias_copy(peer))

        each(0, members, to_section)

        @pl.when(core == role)
        def _():
            act_own(own_mod)
            act_own(own_bias)

        @pl.when(role == 0)
        def _():
            def to_all(peer):
                @pl.when(peer != core * members + index)
                def _():
                    act_head(head_copy(peer))

            each(0, 2 * members, to_all)
            act_own(own_head)

    def start(copy):
        copy.start()

    smalls(start, start, start)

    def part(layer, half):
        rows = head_outs[layer].shape[0]
        return head_parts[layer].at[pl.ds(half * rows, rows)]

    def kept(layer):
        return pltpu.make_async_copy(part(layer, 0), head_outs[layer], part_send.at[layer, 0])

    def handed(layer, half, device):
        return remote(
            part(layer, half), head_outs[layer], part_send.at[layer, half], part_recv.at[layer],
            device,
        )

    @pl.when((role == 0) & (core == 0))
    def _():
        for layer in range(heads):
            kept(layer).start()
            handed(layer, 1, me["sibling"]).start()

    @pl.when((role == 0) & (core == 1))
    def _():
        for layer in range(heads):
            handed(layer, 0, (0, 2 * place + 1)).start()
            handed(layer, 1, (1, 2 * place + 1)).start()

    ring = Ring(me, length, lefts, rights, scratch[:-11])

    def local_last(layer, slot):
        return pltpu.make_async_copy(ring.leaving[layer].at[slot], outs[layer], last_send.at[layer])

    def remote_last(layer, slot):
        return remote(
            ring.leaving[layer].at[slot], outs[layer], last_send.at[layer], last_recv.at[layer],
            me["partner"],
        )

    def finish(layer, slot):
        @pl.when(core == role)
        def _():
            local_last(layer, slot).start()

        @pl.when(core != role)
        def _():
            remote_last(layer, slot).start()

    ring.run(finish)

    @pl.when((role == 0) & (core == 0))
    def _():
        for layer in range(heads):
            kept(layer).wait()
            handed(layer, 1, me["sibling"]).wait_send()

    @pl.when((role == 0) & (core == 1))
    def _():
        for layer in range(heads):
            handed(layer, 0, (0, 2 * place + 1)).wait_send()
            handed(layer, 1, (1, 2 * place + 1)).wait_send()

    @pl.when((role == 1) | (core == 1))
    def _():
        for layer in range(heads):
            handed(layer, 0, me["sibling"]).wait_recv()

    @pl.when(core != role)
    def _():
        stream_copy.wait()

    smalls(lambda copy: copy.wait_send(), lambda copy: copy.wait_send(), lambda copy: copy.wait())

    def came(source):
        @pl.when((core != role) | (source != mine))
        def _():
            small(
                mod, mod_all.at[source], small_send.at[0, 0], mod_recv.at[source], me["sibling"]
            ).wait_recv()
            small(
                bias.at[0], bias_all.at[source], small_send.at[1, 0], bias_recv.at[source],
                me["sibling"],
            ).wait_recv()

        @pl.when((role != 0) | (source != mine))
        def _():
            small(
                head_sums.at[0], head_all.at[source], small_send.at[2, 0], head_recv.at[source],
                me["sibling"],
            ).wait_recv()

    each(0, members, came)
    slot = (length - 1) % 2
    for layer in ring.layers:

        @pl.when(core == role)
        def _():
            local_last(layer, slot).wait()

        @pl.when(core != role)
        def _():
            remote_last(layer, slot).wait()


def reduce(lefts, rights, head_parts, stream, mod, bias, head_sums, collective_id):
    members = lax.axis_size("dp")
    length, count, heads = members // 2, len(lefts), len(head_parts)
    rows = [left.shape[2] for left in lefts]
    columns = [right.shape[1] for right in rights]
    tokens = rights[0].shape[0]
    bf16 = jnp.bfloat16
    inside = pl.BlockSpec(memory_space=pltpu.VMEM)
    small = [mod.shape, bias.shape[1:], head_sums.shape[1:]]
    results = pl.pallas_call(
        functools.partial(reduce_kernel, length, count, heads),
        name="reduce",
        out_shape=[jax.ShapeDtypeStruct((r, c), bf16) for r, c in zip(rows, columns)]
        + [jax.ShapeDtypeStruct((h.shape[0] // 2, h.shape[1]), bf16) for h in head_parts]
        + [jax.ShapeDtypeStruct(stream.shape, stream.dtype)]
        + [
            jax.ShapeDtypeStruct((members,) + shape, array.dtype)
            for shape, array in zip(small, (mod, bias, head_sums))
        ],
        in_specs=[ANY] * (2 * count) + [inside] * heads + [ANY] + [inside] * 3,
        out_specs=[ANY] * (count + heads + 4),
        scratch_shapes=Ring.scratch(length, rows, columns, tokens)
        + [
            DMA((count,)),
            DMA((count,)),
            DMA((heads, 2)),
            DMA((heads,)),
            DMA(()),
            DMA(()),
            DMA((3, 2 * members)),
            DMA((members,)),
            DMA((members,)),
            DMA((members,)),
            DMA((3,)),
        ],
        compiler_params=pltpu.CompilerParams(
            collective_id=collective_id, has_side_effects=True, vmem_limit_bytes=VMEM_BYTES
        ),
        cost_estimate=ring_cost(length, rows, columns, tokens),
    )(*lefts, *rights, *head_parts, stream, mod, bias, head_sums)
    return (results[:count], results[count : count + heads]) + tuple(results[count + heads :])


def spread_kernel(members, given, taken, keep_sem, send_sem, recv_sem):
    core, index = lax.axis_index("section"), lax.axis_index("dp")
    here = core * members + index
    barrier = pltpu.get_barrier_semaphore()

    def others(act):
        def body(peer):
            @pl.when(peer != here)
            def _():
                act(peer, (peer // members, lax.rem(peer, members)))

        each(0, 2 * members, body)

    def copy(peer, device):
        return remote(given, taken.at[here], send_sem.at[peer], recv_sem.at[here], device)

    own = pltpu.make_async_copy(given, taken.at[here], keep_sem)
    own.start()
    others(
        lambda peer, device: pl.semaphore_signal(
            barrier, inc=1, device_id=device, device_id_type=MESH
        )
    )
    pl.semaphore_wait(barrier, 2 * members - 1)
    others(lambda peer, device: copy(peer, device).start())
    others(lambda peer, device: copy(peer, device).wait_send())
    others(
        lambda peer, device: remote(
            given, taken.at[peer], send_sem.at[peer], recv_sem.at[peer], device
        ).wait_recv()
    )
    own.wait()


def spread(block, collective_id):
    members = lax.axis_size("dp")
    return pl.pallas_call(
        functools.partial(spread_kernel, members),
        name="spread",
        out_shape=jax.ShapeDtypeStruct((2 * members,) + block.shape, block.dtype),
        in_specs=[pl.BlockSpec(memory_space=pltpu.VMEM)],
        out_specs=ANY,
        scratch_shapes=[DMA(()), DMA((2 * members,)), DMA((2 * members,))],
        compiler_params=pltpu.CompilerParams(collective_id=collective_id, has_side_effects=True),
    )(block)


def local_grad(function, primal, cotangent_in):
    return jax.vjp(function, primal)[1](cotangent_in)[0]


def column_sums(values):
    return jnp.sum(wide(values), 0)


def blocked_t(values, members):
    tokens, features = values.shape
    return values.T.reshape(members // 2, 2, features // members, tokens)


def normed_of(values):
    center = values - jnp.mean(values, -1, keepdims=True)
    inverse = lax.rsqrt(jnp.mean(center * center, -1, keepdims=True) + EPSILON)
    return center * inverse, inverse


def lane_window(head, head_size):
    start = head * head_size
    base = start // 128 * 128
    width = -(-(start + head_size - base) // 128) * 128
    return base, width, start - base


def head_only(block, inside, head_size):
    lanes = lax.broadcasted_iota(jnp.int32, block.shape, 1)
    keep = (lanes >= inside) & (lanes < inside + head_size)
    return jnp.where(keep, block, jnp.zeros_like(block))


def attend_kernel(
    head_count, hidden, pieces, pack_w, pack_b, out_w, out_b,
    input_out, packed_out, probs_out, mixed_out, attn_out, after_out, mixed_acc,
):
    channels = hidden.shape[1]
    head_size = channels // head_count
    scaling = head_size ** (-0.5)
    residual = wide(hidden[...])
    normed, _ = normed_of(residual)
    attn_input = narrow(normed * (1.0 + pieces[0, 1:2]) + pieces[0, 0:1])
    input_out[...] = attn_input
    packed_out[...] = narrow(product(attn_input, pack_w[...]) + pack_b[...])
    mixed_acc[...] = jnp.zeros_like(mixed_acc)
    for head in range(head_count):
        base, width, inside = lane_window(head, head_size)
        queries = packed_out[:, base : base + width]
        keys = head_only(packed_out[:, channels + base : channels + base + width], inside, head_size)
        values = head_only(
            packed_out[:, 2 * channels + base : 2 * channels + base + width], inside, head_size
        )
        scores = product_right_t(queries, keys) * scaling
        exponent = jnp.exp(scores - jnp.max(scores, -1, keepdims=True))
        probs = narrow(exponent * (1.0 / jnp.sum(exponent, -1, keepdims=True)))
        probs_out[0, head] = probs
        mixed_acc[:, base : base + width] += product(probs, values)
    mixed = narrow(mixed_acc[...])
    mixed_out[...] = mixed
    out = product(mixed, out_w[...]) + out_b[...]
    attn_out[...] = narrow(out)
    after_out[...] = residual + pieces[0, 2:3] * out


def rows_spec(seq_len, columns):
    return pl.BlockSpec((seq_len, columns), lambda i: (i, 0))


def fixed_spec(shape):
    zeros = (0,) * len(shape)
    return pl.BlockSpec(shape, lambda i: zeros, pipeline_mode=pl.Buffered(1))


def attend(hidden, pieces, pack_w, pack_b, out_w, out_b):
    tokens, channels = hidden.shape
    images = pieces.shape[0]
    seq = tokens // images
    bf16, f32 = jnp.bfloat16, jnp.float32
    work = tokens * channels * (4 * channels + 2 * seq)
    return pl.pallas_call(
        functools.partial(attend_kernel, HEADS),
        grid=(images,),
        name="attend",
        in_specs=[
            rows_spec(seq, channels),
            pl.BlockSpec((1,) + pieces.shape[1:], lambda i: (i, 0, 0)),
            fixed_spec(pack_w.shape),
            fixed_spec(pack_b.shape),
            fixed_spec(out_w.shape),
            fixed_spec(out_b.shape),
        ],
        out_specs=[
            rows_spec(seq, channels),
            rows_spec(seq, 3 * channels),
            pl.BlockSpec((1, HEADS, seq, seq), lambda i: (i, 0, 0, 0)),
            rows_spec(seq, channels),
            rows_spec(seq, channels),
            rows_spec(seq, channels),
        ],
        out_shape=[
            jax.ShapeDtypeStruct((tokens, channels), bf16),
            jax.ShapeDtypeStruct((tokens, 3 * channels), bf16),
            jax.ShapeDtypeStruct((images, HEADS, seq, seq), bf16),
            jax.ShapeDtypeStruct((tokens, channels), bf16),
            jax.ShapeDtypeStruct((tokens, channels), bf16),
            jax.ShapeDtypeStruct((tokens, channels), f32),
        ],
        scratch_shapes=[pltpu.VMEM((seq, channels), f32)],
        compiler_params=pltpu.CompilerParams(vmem_limit_bytes=VMEM_BYTES),
        cost_estimate=pl.CostEstimate(
            flops=2 * work, bytes_accessed=40 * 2**20, transcendentals=0
        ),
    )(hidden, pieces, pack_w, pack_b, out_w, out_b)


def per_image(values, images):
    return values.reshape(images, values.shape[0] // images, values.shape[1])


GELU_A, GELU_B = 0.7978845608028654, 0.044715


def mlp_kernel(
    after, pieces, up_w, up_b, down_w, down_b,
    input_out, act_out, slope_out, mlp_out, final_out, input_keep, total,
):
    step, steps = pl.program_id(0), pl.num_programs(0)
    images = pieces.shape[0]

    @pl.when(step == 0)
    def _():
        normed, _ = normed_of(per_image(after[...], images))
        rows = narrow(normed * (1.0 + pieces[:, 4:5]) + pieces[:, 3:4]).reshape(after.shape)
        input_keep[...] = rows
        input_out[...] = rows
        total[...] = jnp.zeros_like(total)

    pre = product(input_keep[...], up_w[...]) + up_b[...]
    square = pre * pre
    tanh = jnp.tanh(GELU_A * pre * (1.0 + GELU_B * square))
    half = 0.5 + 0.5 * tanh
    act = narrow(pre * half)
    act_out[...] = act
    slope_out[...] = narrow(
        half + pre * (0.5 - 0.5 * tanh * tanh) * (GELU_A + (3.0 * GELU_A * GELU_B) * square)
    )
    total[...] += product(act, down_w[...])

    @pl.when(step == steps - 1)
    def _():
        out = total[...] + down_b[...]
        mlp_out[...] = narrow(out)
        final = per_image(after[...], images) + pieces[:, 5:6] * per_image(out, images)
        final_out[...] = narrow(final * pieces[:, 6:7]).reshape(after.shape)


def feed_tile(width):
    return 1152 if width % 1152 == 0 else width


def mlp(after, pieces, up_w, up_b, down_w, down_b):
    tokens, channels = after.shape
    width = up_w.shape[1]
    tile = feed_tile(width)
    bf16, f32 = jnp.bfloat16, jnp.float32
    columns = pl.BlockSpec((tokens, tile), lambda i: (0, i))
    return pl.pallas_call(
        mlp_kernel,
        grid=(width // tile,),
        name="mlp",
        in_specs=[
            fixed_spec(after.shape),
            fixed_spec(pieces.shape),
            pl.BlockSpec((channels, tile), lambda i: (0, i)),
            pl.BlockSpec((1, tile), lambda i: (0, i)),
            pl.BlockSpec((tile, channels), lambda i: (i, 0)),
            fixed_spec(down_b.shape),
        ],
        out_specs=[
            fixed_spec((tokens, channels)),
            columns,
            columns,
            fixed_spec((tokens, channels)),
            fixed_spec((tokens, channels)),
        ],
        out_shape=[
            jax.ShapeDtypeStruct((tokens, channels), bf16),
            jax.ShapeDtypeStruct((tokens, width), bf16),
            jax.ShapeDtypeStruct((tokens, width), bf16),
            jax.ShapeDtypeStruct((tokens, channels), bf16),
            jax.ShapeDtypeStruct((tokens, channels), bf16),
        ],
        scratch_shapes=[pltpu.VMEM((tokens, channels), bf16), pltpu.VMEM((tokens, channels), f32)],
        compiler_params=pltpu.CompilerParams(vmem_limit_bytes=VMEM_BYTES),
        cost_estimate=pl.CostEstimate(
            flops=4 * tokens * channels * width, bytes_accessed=40 * 2**20, transcendentals=0
        ),
    )(after, pieces, up_w, up_b, down_w, down_b)


def sum_rows(values):
    return product(jnp.ones((8, values.shape[0]), jnp.bfloat16), values)


def layer_norm_back(grad_in, normed, inverse):
    return inverse * (
        grad_in
        - jnp.mean(grad_in, -1, keepdims=True)
        - normed * jnp.mean(grad_in * normed, -1, keepdims=True)
    )


def mlp_back_kernel(
    grad, after, pieces, slope, mlp_out, attn_out, up_w, down_w,
    grad_mlp_out, grad_pre_out, grad_after_out, grad_attn_out, sums_out, pre_sums, out_sums,
    total,
):
    step, steps = pl.program_id(0), pl.num_programs(0)
    images = pieces.shape[0]

    @pl.when(step == 0)
    def _():
        given = per_image(grad[...], images)
        rows = narrow(pieces[:, 5:6] * given).reshape(grad.shape)
        grad_mlp_out[...] = rows
        sums_out[:, 5] = jnp.sum(given * per_image(wide(mlp_out[...]), images), 1)
        out_sums[0] = sum_rows(rows)
        total[...] = jnp.zeros_like(total)

    grad_pre = narrow(wide(slope[...]) * product_right_t(grad_mlp_out[...], down_w[...]))
    grad_pre_out[...] = grad_pre
    pre_sums[...] = sum_rows(grad_pre)
    total[...] += product_right_t(grad_pre, up_w[...])

    @pl.when(step == steps - 1)
    def _():
        normed, inverse = normed_of(per_image(after[...], images))
        grad_min = per_image(total[...], images)
        sums_out[:, 3] = jnp.sum(grad_min, 1)
        sums_out[:, 4] = jnp.sum(grad_min * normed, 1)
        grad_after = per_image(grad[...], images) + layer_norm_back(
            grad_min * (1.0 + pieces[:, 4:5]), normed, inverse
        )
        grad_after_out[...] = grad_after.reshape(grad.shape)
        rows = narrow(pieces[:, 2:3] * grad_after).reshape(grad.shape)
        grad_attn_out[...] = rows
        sums_out[:, 2] = jnp.sum(grad_after * per_image(wide(attn_out[...]), images), 1)
        out_sums[1] = sum_rows(rows)


def mlp_back(grad, after, pieces, slope, mlp_out, attn_out, up_w, down_w):
    tokens, channels = after.shape
    images = pieces.shape[0]
    width = up_w.shape[1]
    tile = feed_tile(width)
    bf16, f32 = jnp.bfloat16, jnp.float32
    columns = pl.BlockSpec((tokens, tile), lambda i: (0, i))
    rows = fixed_spec((tokens, channels))
    return pl.pallas_call(
        mlp_back_kernel,
        grid=(width // tile,),
        name="mlp_back",
        in_specs=[
            rows,
            rows,
            fixed_spec(pieces.shape),
            columns,
            rows,
            rows,
            pl.BlockSpec((channels, tile), lambda i: (0, i)),
            pl.BlockSpec((tile, channels), lambda i: (i, 0)),
        ],
        out_specs=[
            rows,
            columns,
            rows,
            rows,
            fixed_spec((images, 8, channels)),
            pl.BlockSpec((8, tile), lambda i: (0, i)),
            fixed_spec((2, 8, channels)),
        ],
        out_shape=[
            jax.ShapeDtypeStruct((tokens, channels), bf16),
            jax.ShapeDtypeStruct((tokens, width), bf16),
            jax.ShapeDtypeStruct((tokens, channels), f32),
            jax.ShapeDtypeStruct((tokens, channels), bf16),
            jax.ShapeDtypeStruct((images, 8, channels), f32),
            jax.ShapeDtypeStruct((8, width), f32),
            jax.ShapeDtypeStruct((2, 8, channels), f32),
        ],
        scratch_shapes=[pltpu.VMEM((tokens, channels), f32)],
        compiler_params=pltpu.CompilerParams(vmem_limit_bytes=VMEM_BYTES),
        cost_estimate=pl.CostEstimate(
            flops=4 * tokens * channels * width, bytes_accessed=40 * 2**20, transcendentals=0
        ),
    )(grad, after, pieces, slope, mlp_out, attn_out, up_w, down_w)


def attend_back_kernel(
    head_count, hidden, pieces, packed, probs_in, grad_attn, grad_after, pack_w, out_w,
    grad_packed_out, grad_hidden_out, sums_out, pack_sums, acc, grad_mixed_keep,
):
    image = pl.program_id(0)
    channels = hidden.shape[1]
    head_size = channels // head_count
    scaling = head_size ** (-0.5)
    grad_mixed_keep[...] = narrow(product_right_t(grad_attn[...], out_w[...]))
    acc[...] = jnp.zeros_like(acc)
    for head in range(head_count):
        base, width, inside = lane_window(head, head_size)
        q_at, k_at, v_at = (slice(j * channels + base, j * channels + base + width) for j in range(3))
        queries = head_only(packed[:, q_at], inside, head_size)
        keys = head_only(packed[:, k_at], inside, head_size)
        grad_mixed = head_only(grad_mixed_keep[:, q_at], inside, head_size)
        probs = probs_in[0, head]
        grad_probs = product_right_t(grad_mixed, packed[:, v_at])
        probs_wide = wide(probs)
        weighted = probs_wide * grad_probs
        grad_scores = narrow(weighted - probs_wide * jnp.sum(weighted, -1, keepdims=True))
        acc[:, v_at] += product_left_t(probs, grad_mixed)
        acc[:, q_at] += product(grad_scores, keys) * scaling
        acc[:, k_at] += product_left_t(grad_scores, queries) * scaling
    grad_packed = narrow(acc[...])
    grad_packed_out[...] = grad_packed
    column_totals = sum_rows(grad_packed)

    @pl.when(image == 0)
    def _():
        pack_sums[...] = column_totals

    @pl.when(image > 0)
    def _():
        pack_sums[...] += column_totals

    grad_ain = product_right_t(grad_packed, pack_w[...])
    normed, inverse = normed_of(wide(hidden[...]))
    sums_out[0, 0:1] = jnp.sum(grad_ain, 0, keepdims=True)
    sums_out[0, 1:2] = jnp.sum(grad_ain * normed, 0, keepdims=True)
    grad_hidden_out[...] = narrow(
        grad_after[...] + layer_norm_back(grad_ain * (1.0 + pieces[0, 1:2]), normed, inverse)
    )


def attend_back(hidden, pieces, packed, probs, grad_attn, grad_after, pack_w, out_w):
    tokens, channels = hidden.shape
    images = pieces.shape[0]
    seq = tokens // images
    bf16, f32 = jnp.bfloat16, jnp.float32
    work = tokens * channels * (4 * channels + 5 * seq)
    rows = rows_spec(seq, channels)
    return pl.pallas_call(
        functools.partial(attend_back_kernel, HEADS),
        grid=(images,),
        name="attend_back",
        in_specs=[
            rows,
            pl.BlockSpec((1,) + pieces.shape[1:], lambda i: (i, 0, 0)),
            rows_spec(seq, 3 * channels),
            pl.BlockSpec((1, HEADS, seq, seq), lambda i: (i, 0, 0, 0)),
            rows,
            rows,
            fixed_spec(pack_w.shape),
            fixed_spec(out_w.shape),
        ],
        out_specs=[
            rows_spec(seq, 3 * channels),
            rows,
            pl.BlockSpec((1, 8, channels), lambda i: (i, 0, 0)),
            fixed_spec((8, 3 * channels)),
        ],
        out_shape=[
            jax.ShapeDtypeStruct((tokens, 3 * channels), bf16),
            jax.ShapeDtypeStruct((tokens, channels), bf16),
            jax.ShapeDtypeStruct((images, 8, channels), f32),
            jax.ShapeDtypeStruct((8, 3 * channels), f32),
        ],
        scratch_shapes=[
            pltpu.VMEM((seq, 3 * channels), f32),
            pltpu.VMEM((seq, channels), bf16),
        ],
        compiler_params=pltpu.CompilerParams(vmem_limit_bytes=VMEM_BYTES),
        cost_estimate=pl.CostEstimate(
            flops=2 * work, bytes_accessed=40 * 2**20, transcendentals=0
        ),
    )(hidden, pieces, packed, probs, grad_attn, grad_after, pack_w, out_w)


def block_forward(hidden, pieces, weights):
    pack_w, pack_b, out_w, out_b, up_w, up_b, down_w, down_b = weights
    attn_input, packed, probs, mixed, attn_out, after = attend(
        hidden, pieces, pack_w, pack_b, out_w, out_b
    )
    mlp_input, act, slope, mlp_out, final = mlp(after, pieces, up_w, up_b, down_w, down_b)
    return final, (attn_input, packed, probs, mixed, attn_out, after, mlp_input, act, slope, mlp_out)


def block_backward(hidden, saved_state, pieces, weights, grad):
    pack_w, pack_b, out_w, out_b, up_w, up_b, down_w, down_b = weights
    attn_input, packed, probs, mixed, attn_out, after, mlp_input, act, slope, mlp_out = saved_state
    grad_mlp, grad_pre, grad_after, grad_attn, high_sums, pre_sums, out_sums = mlp_back(
        grad, after, pieces, slope, mlp_out, attn_out, up_w, down_w
    )
    grad_packed, grad_hidden, low_sums, pack_sums = attend_back(
        hidden, pieces, packed, probs, grad_attn, grad_after, pack_w, out_w
    )
    images, channels = pieces.shape[0], hidden.shape[1]
    grad_mod = narrow(
        jnp.concatenate([low_sums[:, 0:2], high_sums[:, 2:6]], 1).reshape(images, 6 * channels)
    )
    pack_row = pack_sums[0]
    bias_grads = (
        jnp.concatenate([pack_row[:channels], pack_row[2 * channels :]]),
        out_sums[1, 0],
        pre_sums[0],
        out_sums[0, 0],
    )
    return grad_hidden, (grad_mlp, grad_pre, grad_attn, grad_packed), bias_grads, grad_mod


def head_pass(hidden_rows, target_rows, live_rows, head_weights, members):
    in_weight, in_bias, mid_weight, mid_bias, out_weight, out_bias = head_weights
    pre_first = product(hidden_rows, in_weight) + in_bias
    act_first = narrow(jax.nn.silu(pre_first))
    pre_second = product(act_first, mid_weight) + mid_bias
    act_second = narrow(jax.nn.silu(pre_second))
    feature = product(act_second, out_weight) + out_bias
    inverse_feature = lax.rsqrt(jnp.sum(feature * feature, -1, keepdims=True) + EPSILON)
    unit_feature = feature * inverse_feature
    target_float = wide(target_rows)
    unit_target = target_float * lax.rsqrt(
        jnp.sum(target_float * target_float, -1, keepdims=True) + EPSILON
    )
    cosine = jnp.sum(unit_feature * unit_target, -1)
    loss_part = 0.5 * jnp.sum(live_rows * (1.0 - cosine))
    grad_unit = -0.5 * live_rows[:, None] * unit_target
    grad_feature = narrow(
        inverse_feature
        * (grad_unit - unit_feature * jnp.sum(grad_unit * unit_feature, -1, keepdims=True))
    )
    grad_second = narrow(
        local_grad(jax.nn.silu, pre_second, product_right_t(grad_feature, out_weight))
    )
    grad_first = narrow(
        local_grad(jax.nn.silu, pre_first, product_right_t(grad_second, mid_weight))
    )
    grad_hidden = product_right_t(grad_first, in_weight)

    def in_halves(values):
        tokens, features = values.shape
        rows = features // (2 * members)
        cut = values.T.reshape(2, members, rows, tokens)
        return jnp.swapaxes(cut, 0, 1).reshape(members // 2, 2, 2 * rows, tokens)

    lefts = (in_halves(act_second), in_halves(act_first), in_halves(grad_first))
    rights = (grad_feature, grad_second, hidden_rows)
    sums = (column_sums(grad_first), column_sums(grad_second), column_sums(grad_feature))
    return (grad_hidden, loss_part, lefts, rights, sums)


def on_device(
    tokens_in,
    cotangent,
    targets,
    buckets,
    counts,
    time_table,
    modulate_weight,
    modulate_bias,
    qkv_weight,
    qv_bias,
    attn_weight,
    attn_bias,
    up_weight,
    up_bias,
    down_weight,
    down_bias,
    project_in_weight,
    project_in_bias,
    project_mid_weight,
    project_mid_bias,
    project_out_weight,
    project_out_bias,
):
    members = lax.axis_size("dp")
    core = lax.axis_index("section")
    index = lax.axis_index("dp")
    place, role = index // 2, index % 2
    is_first = role == 0
    own = 2 * place + core
    channels = tokens_in.shape[1]
    images = tokens_in.shape[0] // SEQ
    pairs_swap, pairs_up, pairs_back = [], [], []
    for pair in range(members // 2):
        low, high = 2 * pair, 2 * pair + 1
        pairs_swap += [(low, low), (members + low, high), (high, members + low), (members + high, members + high)]
        pairs_up += [(low, high), (members + low, members + high)]
        pairs_back += [(high, low), (members + high, members + low)]
    axes = ("section", "dp")

    def swap(values):
        return lax.ppermute(values, axes, pairs_swap)

    all_buckets = lax.all_gather(buckets, "dp", axis=0, tiled=True)
    one_hot = (
        all_buckets[:, None] == jnp.arange(time_table.shape[0], dtype=jnp.int32)[None, :]
    ).astype(jnp.float32)
    conditioning = jnp.dot(one_hot, time_table, precision=HIGHEST)
    silu_all = narrow(jax.nn.silu(conditioning))
    depth = modulate_weight.shape[1]
    silu_depth = lax.dynamic_slice_in_dim(silu_all, index * depth, depth, 1)
    mod_part = product(silu_depth, modulate_weight[0])
    share = modulate_bias.shape[1]
    bias_row = lax.dynamic_update_slice_in_dim(
        jnp.zeros((mod_part.shape[1],), jnp.float32), wide(modulate_bias[0]), index * share, 0
    )
    mod_part = (mod_part + bias_row[None]).reshape(members, images, 6 * channels)

    section_biases = (qv_bias[0], attn_bias[0], up_bias[0], down_bias[0])
    head_biases = (project_in_bias, project_mid_bias, project_out_bias)
    parts = section_biases + head_biases
    widths = [part.shape[0] for part in parts]
    lanes = 16 * 128
    packed_bias = jnp.concatenate(
        list(parts) + [jnp.zeros((lanes - sum(widths),), jnp.bfloat16)]
    ).reshape(16, 128)
    block_full, head_full, mod_all = gather(
        (packed_bias, qkv_weight[0], attn_weight[0], up_weight[0], down_weight[0], project_out_weight),
        (project_in_weight, project_mid_weight),
        mod_part,
        0,
    )
    all_bias, pack_weight, out_weight, first_weight, second_weight, head_last = block_full
    all_bias = all_bias.reshape(members, lanes)
    biases, offset = [], 0
    for width in widths:
        biases.append(wide(all_bias[:, offset : offset + width].reshape(-1)))
        offset += width
    pack_full = jnp.concatenate(
        [biases[0][:channels], jnp.zeros((channels,), jnp.float32), biases[0][channels:]]
    )

    def whole(values):
        return values.reshape(-1, values.shape[-1])

    block_weights = (
        whole(pack_weight),
        pack_full[None],
        whole(out_weight),
        biases[1][None],
        whole(first_weight),
        biases[2][None],
        whole(second_weight),
        biases[3][None],
    )
    head_weights = (
        whole(head_full[0]),
        biases[4],
        whole(head_full[1]),
        biases[5],
        whole(head_last),
        biases[6],
    )
    pieces = jnp.sum(mod_all, 0).reshape(images, 6, channels)

    own_counts = counts[own]
    image_live = (jnp.arange(images, dtype=jnp.int32) < own_counts).astype(jnp.float32)
    token_live = jnp.repeat(image_live, SEQ)
    out_scale = jnp.where(is_first, 1.0, image_live)
    scale_rows = jnp.broadcast_to(out_scale[:, None, None], (images, 2, channels))
    pieces = jnp.concatenate([pieces, scale_rows], 1)
    total_live = wide(jnp.sum(counts)) * SEQ
    payload = swap(jnp.where(is_first, cotangent, tokens_in))
    crossed = core != role
    hidden_first = jnp.where(crossed, payload, tokens_in)
    outer = jnp.where(crossed, payload, cotangent)
    own_targets = swap(targets)

    def zeros_of(function, *operands_in):
        shapes = jax.eval_shape(function, *operands_in)
        return jax.tree.map(lambda leaf: jnp.zeros(leaf.shape, leaf.dtype), shapes)

    def lefts_of(state):
        attn_input, mixed, mlp_input, act = state[0], state[3], state[6], state[7]
        return tuple(blocked_t(v, members) for v in (act, mlp_input, mixed, attn_input))

    first_out, saved_state = lax.cond(
        is_first,
        block_forward,
        lambda *operands_in: zeros_of(block_forward, *operands_in),
        hidden_first,
        pieces,
        block_weights,
    )
    hidden_second = lax.ppermute(first_out, axes, pairs_up)

    def do_head(first, target, live, state, head):
        return head_pass(first, target, live, head, members) + (lefts_of(state),)

    def do_second(second, mod, grad, live, block):
        final, state = block_forward(second, mod, block)
        outer_grad = wide(grad) * live[:, None]
        grad_input, rights, bias_grads, grad_mod = block_backward(
            second, state, mod, block, outer_grad
        )
        keep = (state[0], state[3], state[6], state[7])
        return grad_input, final, rights, bias_grads, grad_mod, keep

    def at_front(first, second, mod, grad, target, live, state, block, head):
        return (
            do_head(first, target, live, state, head),
            zeros_of(do_second, second, mod, grad, live, block),
        )

    def at_back(first, second, mod, grad, target, live, state, block, head):
        return (
            zeros_of(do_head, first, target, live, state, head),
            do_second(second, mod, grad, live, block),
        )

    head_result, second_result = lax.cond(
        is_first,
        at_front,
        at_back,
        first_out,
        hidden_second,
        pieces,
        outer,
        own_targets,
        token_live,
        saved_state,
        block_weights,
        head_weights,
    )
    grad_hidden, loss_part, head_lefts, head_rights, head_sums, first_lefts = head_result
    arrived_back = lax.ppermute(second_result[0], axes, pairs_back)
    head_parts = head_reduce(head_lefts, head_rights, 2)

    def do_first(hidden, state, mod, extra, back_grad, block, lefts, other):
        grad_input, rights, bias_grads, grad_mod = block_backward(
            hidden, state, mod, block, wide(back_grad) + extra
        )
        return grad_input, rights, bias_grads, grad_mod, lefts

    def keep_second(hidden, state, mod, extra, back_grad, block, lefts, other):
        attn_input, mixed, mlp_input, act = other[-1]
        return other[:-1] + (
            tuple(blocked_t(v, members) for v in (act, mlp_input, mixed, attn_input)),
        )

    stream, rights, bias_grads, grad_mod, lefts = lax.cond(
        is_first,
        do_first,
        keep_second,
        hidden_first,
        saved_state,
        pieces,
        grad_hidden,
        arrived_back,
        block_weights,
        first_lefts,
        second_result[1:],
    )
    bias_rows = jnp.concatenate([grads.reshape(members, -1) for grads in bias_grads], 1)
    bias_width = bias_rows.shape[1]
    bias_rows = jnp.pad(bias_rows, ((0, 0), (0, 1024 - bias_width))).reshape(members, 8, 128)
    in_sums, mid_sums, out_sums = head_sums
    devices = 2 * members
    out_width = out_sums.shape[0]
    head_rows = jnp.concatenate(
        [
            in_sums.reshape(devices, -1),
            mid_sums.reshape(devices, -1),
            jnp.broadcast_to(out_sums[None], (devices, out_width)),
            jnp.broadcast_to(loss_part[None, None], (devices, 1)),
        ],
        1,
    )
    head_width = head_rows.shape[1]
    head_rows = jnp.pad(head_rows, ((0, 0), (0, 1024 - head_width))).reshape(devices, 8, 128)
    mod_width = images * 6 * channels
    mod_lines = -(-mod_width // 2048) * 16
    mod_rows = jnp.pad(grad_mod.reshape(-1), (0, mod_lines * 128 - mod_width)).reshape(-1, 128)
    block_grads, head_grads, stream_in, mod_grads, bias_all, head_all = reduce(
        lefts, rights, head_parts, stream, mod_rows, bias_rows, head_rows, 3
    )
    down_grad, up_grad, attn_grad, qkv_grad = block_grads
    stream_own = jnp.where(crossed, stream_in, stream)
    mod_grad_all = mod_grads.reshape(members, -1)[:, :mod_width].reshape(-1, 6 * channels)
    silu_part = product_right_t(mod_grad_all, modulate_weight[0])
    lines = silu_part.shape[0]
    padded = jnp.pad(silu_part, ((0, 0), (0, 128 - depth)))
    silu_parts = spread(padded, 4)[:, :, :depth].reshape(2, members, lines, depth)
    mod_w_grad = product_left_t(silu_depth, mod_grad_all)
    mod_b_grad = lax.dynamic_slice_in_dim(column_sums(mod_grad_all), index * share, share, 0)
    silu_total = jnp.swapaxes(jnp.sum(silu_parts, 0), 0, 1).reshape(lines, channels)
    cond_grad = local_grad(jax.nn.silu, conditioning, silu_total)
    table_grad = jnp.dot(one_hot.T, cond_grad, precision=HIGHEST)

    bias_sums = jnp.sum(bias_all, 0).reshape(-1)
    bias_outs, offset = [], 0
    for part in section_biases:
        width = part.shape[0]
        bias_outs.append(bias_sums[offset : offset + width][None])
        offset += width
    sums = jnp.sum(head_all, 0).reshape(-1)
    head_share = in_sums.shape[0] // devices
    loss_value = sums[head_width - 1] / total_live
    return (
        stream_own[None],
        loss_value,
        table_grad,
        mod_w_grad[None],
        mod_b_grad[None],
        wide(qkv_grad)[None],
        bias_outs[0],
        wide(attn_grad)[None],
        bias_outs[1],
        wide(up_grad)[None],
        bias_outs[2],
        wide(down_grad)[None],
        bias_outs[3],
        wide(head_grads[2]).T,
        sums[:head_share],
        wide(head_grads[1]),
        sums[head_share : 2 * head_share],
        wide(head_grads[0]),
        sums[2 * head_share : 2 * head_share + out_width],
    )


def solution(mesh):
    in_specs = (
        P("dp", None),
        P("dp", None),
        P("dp", None),
        P("dp"),
        P(),
        P(),
        P("section", "dp", None),
        P("section", "dp"),
        P("section", "dp", None),
        P("section", "dp"),
        P("section", "dp", None),
        P("section", "dp"),
        P("section", "dp", None),
        P("section", "dp"),
        P("section", "dp", None),
        P("section", "dp"),
        P("dp", None),
        P("dp"),
        P("dp", None),
        P("dp"),
        P("dp", None),
        P("dp"),
    )
    out_specs = (
        P("section", "dp", None),
        P(),
        P(),
        P("section", "dp", None),
        P("section", "dp"),
        P("section", "dp", None),
        P("section", "dp"),
        P("section", "dp", None),
        P("section", "dp"),
        P("section", "dp", None),
        P("section", "dp"),
        P("section", "dp", None),
        P("section", "dp"),
        P(None, ("section", "dp")),
        P(("section", "dp")),
        P(("section", "dp"), None),
        P(("section", "dp")),
        P(("section", "dp"), None),
        P(),
    )
    return jax.shard_map(
        on_device, mesh=mesh, in_specs=in_specs, out_specs=out_specs, check_vma=False
    )
```

time: 1280 us -> 862 us (0.67)
  blocking collectives: 175 us -> 13.7 us
  matrix products: 110 us -> 10.9 us
  starting transfers between devices: 86.9 us -> 9.86 us
  local copies, waits for them, and re-layouts: 114 us -> 68.3 us
  waiting for transfers between devices: 9.93 us -> 45.1 us
  other arithmetic: 42.7 us -> 19.5 us
  Pallas kernels: 678 us -> 655 us
  between operations: 18.9 us -> 4.59 us
    all_gather x2 -> x0, blocking collectives: 110 us -> none  [the longest x1 67.3 us: on_device(): silu_parts = lax.all_gather(silu_part, axes, axis=0, tiled=False)]
    ppermute x5 -> x2, starting transfers between devices: 83.2 us -> 6.21 us  [swap(): return lax.ppermute(values, axes, pairs_swap)]
    psum x1 -> x0, blocking collectives: 50.9 us -> none  [on_device(): sums = lax.psum((mine, head_sums, loss_part), axes)]
    dot_general x5 -> x1, matrix products: 46.5 us -> 0.37 us  [product_right_t(): lax.dot_general(left_side, right_side, (((1,), (1,)), ((), ())), preferre...]
    dot_general x5 -> x1, matrix products: 39.7 us -> 0.29 us  [product(): return jnp.dot(left_side, right_side, preferred_element_type=jnp.float32)]
    cond x89 -> x15, local copies, waits for them, and re-layouts: 23.8 us -> 1.09 us
    pallas_call x4 -> x8, Pallas kernels: 678 us -> 655 us  [the longest x1 274 us: gather(): pl.pallas_call(functools.partial(gather_kernel, length, count, heads), na...]
    ppermute x5 -> x2, waiting for transfers between devices: 9.89 us -> 32.4 us  [swap(): return lax.ppermute(values, axes, pairs_swap)]
  transfers between devices with their start and end apart: 9 -> 4, of which waited for: 2 -> 2; matrix products, arithmetic and copies ran while one was open for 3% -> 2% of each run, Pallas kernels for 28% -> 32%
where the time goes in v2:
time: 862 us; the launch traced here: 850 us
  Pallas kernels  655 us (76%)
  local copies, waits for them, and re-layouts  68.3 us (8%)
  waiting for transfers between devices  45.1 us (5%)
  loops' own time  23.2 us (3%)
  other arithmetic  19.5 us (2%)
  blocking collectives  13.7 us (2%)
  matrix products  10.9 us (1%)
  starting transfers between devices  9.86 us (1%)
    pallas_call x1, Pallas kernels, gather(): pl.pallas_call(functools.partial(gather_kernel, length, count, heads), na...  274 us
    pallas_call x1, Pallas kernels, reduce(): pl.pallas_call(functools.partial(reduce_kernel, length, count, heads), na...  269 us
    another operation x28, local copies, waits for them, and re-layouts  44.8 us
    ppermute x2, waiting for transfers between devices, swap(): return lax.ppermute(values, axes, pairs_swap)  32.4 us
    pallas_call x1, Pallas kernels, mlp_back(): pl.pallas_call(mlp_back_kernel, grid=(width // tile,), name='mlp_back', i...  29 us
    pallas_call x1, Pallas kernels, attend_back(): pl.pallas_call(functools.partial(attend_back_kernel, HEADS), grid=(images...  26 us
    pallas_call x1, Pallas kernels, mlp(): pl.pallas_call(mlp_kernel, grid=(width // tile,), name='mlp', in_specs=[f...  23.2 us
    pallas_call x1, Pallas kernels, attend(): pl.pallas_call(functools.partial(attend_kernel, HEADS), grid=(images,), n...  18.8 us
  transfers between devices with their start and end apart: 4, of which 2 were waited for; matrix products, arithmetic and copies ran while one was open for 2% of the time, Pallas kernels for 32%

profile of v2, /device:TPU:10, one launch (start us, length us, event | category | flops | bytes accessed | tf_op | source)
XLA Modules:
  0.0 850.3 jit_solution(5177464596897704956)
XLA Ops:
  0.7 2.5 broadcast_select_fusion
  3.2 1.9 collective-permute-start
  6.7 13.7 %all-reduce.4 = s32[32]{0:T(128)S(1)} all-reduce(s32[32]{0:T(128)S(1)} %dynamic-update-slice), channel_id=1, replica_groups=mesh['section'=2,'dp'=16] {'dp'}, use_global_device_ids=true, to_apply=%add.4 | all-reduce | flops 32 | bytes 256
  20.4 4.0 add_divide_fusion.2
  27.8 273.7 %gather.1 = (bf16[16,16,128]{2,1,0:T(8,128)(2,1)}, bf16[16,72,3456]{2,1,0:T(8,128)(2,1)}, bf16[16,72,1152]{2,1,0:T(8,128)(2,1)}, bf16[16,72,4608]{2,1,0:T(8,128)...) custom-call(bf16[16,128]{1,0:T(8,128)(2,1)} %bitcast.200, ...), custom_call_target="tpu_custom_call" | custom-call | bytes 770703360 | tf_op jit(solution)/shard_map/gather/pallas_call | solution.py:391
  309.9 17.2 %conditional.3 = (bf16[512,1152]{1,0:T(8,128)(2,1)S(1)}, bf16[512,1152]{1,0:T(8,128)(2,1)}, bf16[512,3456]{1,0:T(8,128)(2,1)}, bf16[2,16,256,256]{3,2,1,0:T(8,12...) conditional(s32[]{:T(128)} %convert_element_type.172, () %tuple.44, ...), branch_computations={%region_1.2_spmd, %region_2.3_spmd} | conditional | flops 16911433728 | bytes 83886168 | solution.py:1451
  309.9 2.5 broadcast.137
  312.4 2.5 broadcast.137.clone
  314.9 2.5 broadcast.135
  317.4 2.0 broadcast.134
  319.3 1.6 broadcast.136
  328.4 4.3 collective-permute-start.2
  333.3 32.4 %collective-permute-done.2 = bf16[512,768]{1,0:T(8,128)(2,1)} collective-permute-done((bf16[512,768]{1,0:T(8,128)(2,1)}, bf16[512,768]{1,0:T(8,128)(2,1)}, u32[]{:S(2)}, u32[]{:S(2)}) %collective-permute-start.2) | collective-permute-done | bytes 786464 | tf_op jit(solution)/shard_map/ppermute | solution.py:1366
  365.7 134.9 %conditional.4 = (f32[512,1152]{1,0:T(8,128)S(1)}, f32[]{:T(128)}, bf16[8,2,128,512]{3,2,1,0:T(8,128)(2,1)}, bf16[8,2,128,512]{3,2,1,0:T(8,128)(2,1)}, bf16[8,2,...) conditional(s32[]{:T(128)} %convert_element_type.172, ...), branch_computations={%region_3.4_spmd, %region_4.13_spmd} | conditional | flops 34730663936 | bytes 276951040 | solution.py:1485
  366.9 18.8 %attend.3 = (bf16[512,1152]{1,0:T(8,128)(2,1)}, bf16[512,3456]{1,0:T(8,128)(2,1)}, bf16[2,16,256,256]{3,2,1,0:T(8,128)(2,1)}, bf16[512,1152]{1,0:T(8,128)(2,1)},...) custom-call(bf16[512,1152]{1,0:T(8,128)(2,1)} %copy-done.48, f32[2,8,1152]{2,1,0:T(8,128)} %get-tuple-element.204.pieces, ...), custom_call_target="tpu_custom_call" | custom-call | flops 6039797760 | bytes 41943040 | tf_op jit(solution)/shard_map/cond/branch_0_fun/attend/pallas_call | solution.py:945
  385.8 23.2 %mlp.3 = (bf16[512,1152]{1,0:T(8,128)(2,1)}, bf16[512,4608]{1,0:T(8,128)(2,1)}, bf16[512,4608]{1,0:T(8,128)(2,1)}, bf16[512,1152]{1,0:T(8,128)(2,1)}, bf16[512,1152]{1,0:T(8,128)(2,1)}) custom-call(f32[512,1152]{1,0:T(8,128)} %get-tuple-element.215.after, f32[2,8,1152]{2,1,0:T(8,128)S(1)} %copy-done.24, bf16[1152,4608]{1,0:T(8,128)(2,1)} %get-tuple-element.216.up_w, ...), custom_call_target="tpu_custom_call" | custom-call | flops 10871635968 | bytes 41943040 | tf_op jit(solution)/shard_map/cond/branch_0_fun/mlp/pallas_call | solution.py:1032
  409.1 1.8 convert_multiply_fusion.2.grad
  410.8 29.0 %mlp_back.2 = (bf16[512,1152]{1,0:T(8,128)(2,1)}, bf16[512,4608]{1,0:T(8,128)(2,1)}, f32[512,1152]{1,0:T(8,128)}, bf16[512,1152]{1,0:T(8,128)(2,1)}, f32[2,8,115...) custom-call(f32[512,1152]{1,0:T(8,128)} %convert_multiply_fusion.2.grad, ...), custom_call_target="tpu_custom_call" | custom-call | flops 10871635968 | bytes 41943040 | tf_op jit(solution)/shard_map/cond/branch_0_fun/mlp_back/pallas_call | solution.py:1124
  439.8 26.0 %attend_back.2 = (bf16[512,3456]{1,0:T(8,128)(2,1)}, bf16[512,1152]{1,0:T(8,128)(2,1)}, f32[2,8,1152]{2,1,0:T(8,128)}, f32[8,3456]{1,0:T(8,128)}) custom-call(bf16[512,1152]{1,0:T(8,128)(2,1)} %copy-done.48, f32[2,8,1152]{2,1,0:T(8,128)S(1)} %copy-done.24, bf16[512,3456]{1,0:T(8,128)(2,1)} %get-tuple-element.209.packed, ...), custom_call_target="tpu_custom_call" | custom-call | flops 6945767424 | bytes 41943040 | tf_op jit(solution)/shard_map/cond/branch_0_fun/attend_back/pallas_call | solution.py:1216
  470.5 2.6 broadcast.144
  477.6 1.6 broadcast.141
  500.7 2.4 collective-permute-start.3
  506.3 12.7 %collective-permute-done.3 = bf16[512,1152]{1,0:T(8,128)(2,1)} collective-permute-done((bf16[512,1152]{1,0:T(8,128)(2,1)}, bf16[512,1152]{1,0:T(8,128)(2,1)}, u32[]{:S(2)}, u32[]{:S(2)}) %collective-permute-start.3) | collective-permute-done | bytes 1179680 | tf_op jit(solution)/shard_map/ppermute | solution.py:1500
  518.9 20.3 %conditional.5 = (bf16[512,1152]{1,0:T(8,128)(2,1)}, bf16[512,1152]{1,0:T(8,128)(2,1)}, bf16[512,4608]{1,0:T(8,128)(2,1)}, bf16[512,1152]{1,0:T(8,128)(2,1)}, bf...) conditional(s32[]{:T(128)} %convert_element_type.172, ...), branch_computations={%region_13.14_spmd, %region_14.15_spmd} | conditional | flops 17818640384 | bytes 94761104 | solution.py:1515
  518.9 6.6 copy.102
  525.6 2.4 copy.103
  528.0 2.4 copy.104
  530.4 2.4 copy.105
  542.4 268.7 %reduce.26 = (bf16[288,1152]{1,0:T(8,128)(2,1)}, bf16[72,4608]{1,0:T(8,128)(2,1)}, bf16[72,1152]{1,0:T(8,128)(2,1)}, bf16[72,3456]{1,0:T(8,128)(2,1)}, bf16[64,7...) custom-call(bf16[8,2,288,512]{3,2,1,0:T(8,128)(2,1)} %get-tuple-elem, ...), custom_call_target="tpu_custom_call" | custom-call | flops 16307453952 | bytes 509607936 | tf_op jit(solution)/shard_map/reduce/pallas_call | solution.py:785
  812.9 1.7 convolution_bitcast_fusion
  818.3 15.3 %spread.1 = f32[32,32,128]{2,1,0:T(8,128)} custom-call(f32[32,128]{1,0:T(8,128)} %pad.19.given), custom_call_target="tpu_custom_call" | custom-call | tf_op jit(solution)/shard_map/spread/pallas_call | solution.py:855
  835.1 4.4 fusion.37
  (197 shorter events, 57.0 us)
Async XLA Ops:
  0.7 24.6 %copy-start = (bf16[1,72,6912]{2,1,0:T(8,128)(2,1)S(1)}, bf16[1,72,6912]{2,1,0:T(8,128)(2,1)}, u32[]{:S(2)}) copy-start(bf16[1,72,6912]{2,1,0:T(8,128)(2,1)} %param.34) | copy-start | bytes 2985988
  0.7 4.5 copy-start.51
  0.7 5.7 copy-start.49
  0.7 19.7 %copy-start.37 = (bf16[1,432]{1,0:T(2,128)(2,1)S(1)}, bf16[1,432]{1,0:T(2,128)(2,1)}, u32[]{:S(2)}) copy-start(bf16[1,432]{1,0:T(2,128)(2,1)} %param.35) | copy-start | bytes 2596
  3.2 305.2 %collective-permute-start = (bf16[512,1152]{1,0:T(8,128)(2,1)}, bf16[512,1152]{1,0:T(8,128)(2,1)S(1)}, u32[]{:S(2)}, u32[]{:S(2)}) collective-permute-start(bf16[512,1152]{1,0:T(8,128)(2,1)} %broadcast_select_fusion), channel_id=1, source_target_pairs={{0,0},{16,1},{1,16},{17,17},{2,2},{18,3},{3,18},{19,19},{4,4},{20,... | collective-permute-start | bytes 3538952 | tf_op jit(solution)/shard_map/ppermute | solution.py:1366
  20.4 4.1 copy-start.35
  24.6 3.2 copy-start.20
  27.8 279.2 %copy-start.50 = (s32[16]{0:T(128)S(1)}, s32[16]{0:T(128)}, u32[]{:S(2)}) copy-start(s32[16]{0:T(128)} %param.32) | copy-start | bytes 196
  27.8 280.6 %copy-start.3 = (bf16[512,1152]{1,0:T(8,128)(2,1)S(1)}, bf16[512,1152]{1,0:T(8,128)(2,1)}, u32[]{:S(2)}) copy-start(bf16[512,1152]{1,0:T(8,128)(2,1)} %param.28) | copy-start | bytes 3538948
  307.0 2.8 copy-start.31
  307.1 2.8 copy-start.33
  309.9 55.9 %copy-start.4 = (bf16[512,1152]{1,0:T(8,128)(2,1)S(1)}, bf16[512,1152]{1,0:T(8,128)(2,1)}, u32[]{:S(2)}) copy-start(bf16[512,1152]{1,0:T(8,128)(2,1)} %param.29) | copy-start | bytes 3538948
  309.9 55.9 %copy-start.32 = (f32[1,3456]{1,0:T(1,128)S(1)}, f32[1,3456]{1,0:T(1,128)}, u32[]{:S(2)}) copy-start(f32[1,3456]{1,0:T(1,128)} %broadcast_in_dim.99) | copy-start | bytes 41476
  309.9 55.9 %copy-start.34 = (f32[1,1152]{1,0:T(1,128)S(1)}, f32[1,1152]{1,0:T(1,128)}, u32[]{:S(2)}) copy-start(f32[1,1152]{1,0:T(1,128)} %reshape.333) | copy-start | bytes 13828
  327.1 38.7 %collective-permute-start.1 = (bf16[512,1152]{1,0:T(8,128)(2,1)S(1)}, bf16[512,1152]{1,0:T(8,128)(2,1)S(1)}, u32[]{:S(2)}, u32[]{:S(2)}) collective-permute-start(bf16[512,1152]{1,0:T(8,128)(2,1)S(1)} %get-tuple-element.396), channel_id=1, source_target_pairs={{0,1},{16,17},{2,3},{18,19},{4,5},{20,21},{6,7},{22,23},{8,9},{24,... | collective-permute-start | bytes 3538952 | tf_op jit(solution)/shard_map/ppermute | solution.py:1459
  328.4 37.4 %collective-permute-start.2 = (bf16[512,768]{1,0:T(8,128)(2,1)}, bf16[512,768]{1,0:T(8,128)(2,1)}, u32[]{:S(2)}, u32[]{:S(2)}) collective-permute-start(bf16[512,768]{1,0:T(8,128)(2,1)} %param.30), channel_id=1, source_target_pairs={{0,0},{16,1},{1,16},{17,17},{2,2},{18,3},{3,18},{19,19},{4,4},{20,... | collective-permute-start | bytes 2359304 | tf_op jit(solution)/shard_map/ppermute | solution.py:1366
  366.9 18.8 %copy-start.24 = (f32[2,8,1152]{2,1,0:T(8,128)S(1)}, f32[2,8,1152]{2,1,0:T(8,128)}, u32[]{:S(2)}) copy-start(f32[2,8,1152]{2,1,0:T(8,128)} %get-tuple-element.204.pieces) | copy-start | bytes 221188 | tf_op jit(solution)/shard_map/cond
  366.9 18.8 %copy-start.30 = (f32[1,4608]{1,0:T(1,128)S(1)}, f32[1,4608]{1,0:T(1,128)}, u32[]{:S(2)}) copy-start(f32[1,4608]{1,0:T(1,128)} %copy-done.29) | copy-start | bytes 55300 | tf_op jit(solution)/shard_map/cond
  385.8 23.3 %copy-start.6 = (bf16[512,1152]{1,0:T(8,128)(2,1)S(1)}, bf16[512,1152]{1,0:T(8,128)(2,1)}, u32[]{:S(2)}) copy-start(bf16[512,1152]{1,0:T(8,128)(2,1)} %get-tuple-element.212) | copy-start | bytes 3538948 | tf_op jit(solution)/shard_map/cond
  410.8 29.0 %copy-start.47 = (bf16[1152,1152]{1,0:T(8,128)(2,1)S(1)}, bf16[1152,1152]{1,0:T(8,128)(2,1)}, u32[]{:S(2)}) copy-start(bf16[1152,1152]{1,0:T(8,128)(2,1)} %get-tuple-element.207.out_w) | copy-start | bytes 7962628 | tf_op jit(solution)/shard_map/cond
  500.7 5.1 copy-start.27
  500.7 5.1 copy-start.28
  500.7 18.3 %collective-permute-start.3 = (bf16[512,1152]{1,0:T(8,128)(2,1)}, bf16[512,1152]{1,0:T(8,128)(2,1)}, u32[]{:S(2)}, u32[]{:S(2)}) collective-permute-start(bf16[512,1152]{1,0:T(8,128)(2,1)} %get-tuple-element.418), channel_id=1, source_target_pairs={{1,0},{17,16},{3,2},{19,18},{5,4},{21,20},{7,6},{23,22},{9,8},{25,... | collective-permute-start | bytes 3538952 | tf_op jit(solution)/shard_map/ppermute | solution.py:1500
  505.8 13.2 %copy-start.23 = (f32[2,8,1152]{2,1,0:T(8,128)S(1)}, f32[2,8,1152]{2,1,0:T(8,128)}, u32[]{:S(2)}) copy-start(f32[2,8,1152]{2,1,0:T(8,128)} %copy-done.22) | copy-start | bytes 221188
  812.4 4.0 copy-start.25
  812.8 22.2 %copy-start.14 = (f32[32,1152]{1,0:T(8,128)S(1)}, f32[32,1152]{1,0:T(8,128)}, u32[]{:S(2)}) copy-start(f32[32,1152]{1,0:T(8,128)} %copy-done.13) | copy-start | bytes 442372
  812.9 22.2 %copy-start.36 = (s32[32]{0:T(128)S(1)}, s32[32]{0:T(128)}, u32[]{:S(2)}) copy-start(s32[32]{0:T(128)} %copy-done.35) | copy-start | bytes 388
  835.1 5.1 copy-start.12
  839.5 3.0 copy-start.10
  842.5 3.1 copy-start.17
  843.8 2.6 copy-start.18
  843.8 3.3 copy-start.19
  (17 other events, 32.7 us)

commit v3 on v2

--- a/solution.py
+++ b/solution.py
@@ -101,19 +101,21 @@
 
 def gather_kernel(length, count, heads, *refs):
     total = count + heads
-    shards, mod_part = refs[:total], refs[total]
-    full, mod_all = refs[total + 1 : 2 * total + 1], refs[2 * total + 1]
+    shards, (mod_part, tokens, cotangent) = refs[:total], refs[total : total + 3]
+    refs = refs[total + 3 :]
+    full, (mod_all, rows_in) = refs[:total], refs[total : total + 2]
     (
         own_sem, swap_send, swap_recv, ring_send, ring_recv, side_send, side_recv,
-        cross_send, cross_recv, mod_send, mod_recv, mod_sem,
-    ) = refs[2 * total + 2 :]
+        cross_send, cross_recv, mod_send, mod_recv, mod_sem, rows_send, rows_recv, mod_pair, mod_in,
+        mod_sum,
+    ) = refs[total + 2 :]
     me = whereabouts(length)
     core, role, place, at = me["core"], me["role"], me["place"], me["at"]
     members = 2 * length
     index = 2 * place + role
     neighbour = (core, 2 * place + 1 - role)
     mine = 2 * place + core
-    layers, head_layers = range(count), range(count, total)
+    layers, shared, head_layers = range(count), range(count - 1), range(count, total)
 
     barrier = pltpu.get_barrier_semaphore()
 
@@ -181,13 +183,24 @@
 
     @pl.when(core == role)
     def _():
-        for layer in layers:
+        for layer in shared:
             own(layer).start()
 
+    @pl.when((core == 0) & (role == 0))
+    def _():
+        own(count - 1).start()
+
+    def rows_move(source):
+        return remote(source, rows_in, rows_send, rows_recv, me["partner"])
+
     @pl.when(core != role)
     def _():
-        for layer in layers:
+        for layer in shared:
             swap_out(layer).start()
+
+    @pl.when((core == 0) & (role == 1))
+    def _():
+        swap_out(count - 1).start()
 
     @pl.when(core == role)
     def _():
@@ -199,53 +212,55 @@
         for layer in head_layers:
             lend(layer).start()
 
-    def mod_target(peer):
-        return (lax.rem(peer, 2), 2 * (peer // 2) + core)
+    mod_move = remote(mod_part, mod_in, mod_pair.at[0], mod_pair.at[1], neighbour)
 
     def mod_copy(peer):
         return remote(
-            mod_part.at[peer], mod_all.at[index], mod_send.at[peer], mod_recv.at[index],
-            mod_target(peer),
-        )
-
-    def mod_is_own(peer):
-        return (core == role) & (peer == mine)
-
-    mod_own = pltpu.make_async_copy(mod_part.at[mine], mod_all.at[index], mod_sem)
+            mod_sum.at[peer], mod_all.at[place], mod_send.at[peer], mod_recv.at[place],
+            (lax.rem(peer, 2), 2 * (peer // 2) + core),
+        )
+
+    mod_own = pltpu.make_async_copy(mod_sum.at[mine], mod_all.at[place], mod_sem)
+
+    def others(act):
+        def body(peer):
+            @pl.when(peer != mine)
+            def _():
+                act(mod_copy(peer))
+
+        each(0, members, body)
+
+    @pl.when(core != role)
+    def _():
+        mod_move.start()
 
     def spread_mod():
-        def start(peer):
-            @pl.when(jnp.logical_not(mod_is_own(peer)))
-            def _():
-                mod_copy(peer).start()
-
-        each(0, members, start)
-
         @pl.when(core == role)
         def _():
+            mod_move.wait_recv()
+            mod_sum[...] = mod_part[...] + mod_in[...]
+            others(lambda copy: copy.start())
             mod_own.start()
 
     def gathered_mod():
         @pl.when(core == role)
         def _():
             mod_own.wait()
-
-        def sent(peer):
-            @pl.when(jnp.logical_not(mod_is_own(peer)))
-            def _():
-                mod_copy(peer).wait_send()
-
-        each(0, members, sent)
+            others(lambda copy: copy.wait_send())
+
+        @pl.when(core != role)
+        def _():
+            mod_move.wait_send()
 
         def came(source):
-            @pl.when(jnp.logical_not((core == role) & (source == index)))
+            @pl.when(jnp.logical_not((core == role) & (source == place)))
             def _():
                 remote(
-                    mod_part.at[0], mod_all.at[source], mod_send.at[0], mod_recv.at[source],
+                    mod_sum.at[0], mod_all.at[source], mod_send.at[0], mod_recv.at[source],
                     me["sibling"],
                 ).wait_recv()
 
-        each(0, members, came)
+        each(0, length, came)
 
     def begin(layer):
         @pl.when(core == role)
@@ -259,22 +274,22 @@
         onward(layer, 0).start()
         across(layer, 0).start()
 
-    def ring_turn(turn, more):
-        for layer in layers:
+    def ring_turn(turn, more, which):
+        for layer in which:
             onward(layer, turn - 1).wait_recv()
             if more:
                 onward(layer, turn).start()
             across(layer, turn).start()
 
-    def ring_end():
+    def ring_end(which):
         def end(turn):
-            for layer in layers:
+            for layer in which:
                 onward(layer, turn).wait_send()
                 across(layer, turn).wait_send()
                 from_sibling(layer, turn).wait_recv()
 
         each(0, length - 1, end)
-        for layer in layers:
+        for layer in which:
             across(layer, length - 1).wait_send()
             from_sibling(layer, length - 1).wait_recv()
 
@@ -298,22 +313,27 @@
     def _():
         for layer in layers:
             begin(layer)
+
+        @pl.when(core == 1)
+        def _():
+            rows_move(cotangent).start()
+
+        front_head(0, True)
+        ring_turn(1, True, layers)
         spread_mod()
-        front_head(0, True)
-        ring_turn(1, True)
         late = 2
 
         def turn_body(turn):
-            ring_turn(turn, True)
+            ring_turn(turn, True, layers)
 
             @pl.when(turn > late)
             def _():
                 front_head(turn - late, False)
 
         each(2, length - 1, turn_body)
-        ring_turn(length - 1, False)
+        ring_turn(length - 1, False, layers)
         each(length - 1 - late, length, lambda turn: front_head(turn, False))
-        ring_end()
+        ring_end(layers)
         gathered_mod()
 
         def head_end(turn):
@@ -330,13 +350,19 @@
 
     @pl.when(role == 1)
     def _():
-        spread_mod()
+        lag = 3
+
+        def cross_start(turn):
+            @pl.when((turn > 0) | (core == 1))
+            def _():
+                for layer in head_layers:
+                    cross(layer, turn).start()
+
         for layer in head_layers:
 
             @pl.when(core == 1)
             def _():
                 own(layer).wait()
-                cross(layer, 0).start()
 
             @pl.when(core == 0)
             def _():
@@ -352,14 +378,22 @@
                 def _():
                     onward(layer, turn).start()
 
-                cross(layer, turn).start()
+            @pl.when(turn >= lag)
+            def _():
+                cross_start(turn - lag)
 
         each(1, length, head_turn)
-        for layer in layers:
+        @pl.when(core == 0)
+        def _():
+            rows_move(tokens).start()
+
+        each(length - lag, length, cross_start)
+        spread_mod()
+        for layer in shared:
             begin(layer)
-        each(1, length - 1, lambda turn: ring_turn(turn, True))
-        ring_turn(length - 1, False)
-        ring_end()
+        each(1, length - 1, lambda turn: ring_turn(turn, True, shared))
+        ring_turn(length - 1, False, shared)
+        ring_end(shared)
         gathered_mod()
 
         def head_end(turn):
@@ -375,13 +409,18 @@
 
         each(0, length, head_end)
 
+    @pl.when((core == 0) & (role == 1))
+    def _():
+        swap_out(count - 1).wait_send()
+
     @pl.when(core != role)
     def _():
-        for layer in layers:
+        for layer in shared:
             swap_out(layer).wait_send()
-
-
-def gather(shards, head_shards, mod_part, collective_id):
+        rows_move(tokens).wait()
+
+
+def gather(shards, head_shards, mod_part, tokens, cotangent, collective_id):
     members = lax.axis_size("dp")
     length, count, heads = members // 2, len(shards), len(head_shards)
     total = count + heads
@@ -392,9 +431,10 @@
         functools.partial(gather_kernel, length, count, heads),
         name="gather",
         out_shape=[jax.ShapeDtypeStruct((members,) + s.shape, s.dtype) for s in everything]
-        + [jax.ShapeDtypeStruct((members,) + mod_part.shape[1:], mod_part.dtype)],
-        in_specs=[inside] * (total + 1),
-        out_specs=[ANY] * (total + 1),
+        + [jax.ShapeDtypeStruct((length,) + mod_part.shape[1:], mod_part.dtype)]
+        + [jax.ShapeDtypeStruct(tokens.shape, tokens.dtype)],
+        in_specs=[inside] * (total + 1) + [ANY] * 2,
+        out_specs=[ANY] * (total + 2),
         scratch_shapes=[
             DMA((total,)),
             DMA((total,)),
@@ -408,13 +448,18 @@
             DMA((members,)),
             DMA((members,)),
             DMA(()),
+            DMA(()),
+            DMA(()),
+            DMA((2,)),
+            pltpu.VMEM(mod_part.shape, mod_part.dtype),
+            pltpu.VMEM(mod_part.shape, mod_part.dtype),
         ],
         compiler_params=pltpu.CompilerParams(
             collective_id=collective_id, has_side_effects=True, vmem_limit_bytes=VMEM_BYTES
         ),
         cost_estimate=pl.CostEstimate(flops=0, bytes_accessed=16 * moved, transcendentals=0),
-    )(*everything, mod_part)
-    return results[:count], results[count:total], results[total]
+    )(*everything, mod_part, tokens, cotangent)
+    return (results[:count], results[count:total]) + tuple(results[total:])
 
 
 def tile_of(columns):
@@ -503,7 +548,7 @@
             ),
         ]
 
-    def run(self, finish):
+    def run(self, finish, midway=None, late=None):
         length = self.length
         for layer in self.layers:
             for copy in self.inputs(layer):
@@ -526,7 +571,14 @@
                 self.chunk(layer, slot, turn, True)
                 self.onward(layer, slot, turn).start()
 
-        each(1, length - 1, turn_body)
+        first, second = min(3, length - 1), max(min(3, length - 1), length - 2)
+        each(1, first, turn_body)
+        if midway:
+            midway()
+        each(first, second, turn_body)
+        if late:
+            late()
+        each(second, length - 1, turn_body)
         slot = (length - 1) % 2
         for layer in self.layers:
             self.onward(layer, slot, length - 2).wait_recv()
@@ -586,11 +638,13 @@
 def reduce_kernel(length, count, heads, *refs):
     lefts, rights = refs[:count], refs[count : 2 * count]
     head_parts = refs[2 * count : 2 * count + heads]
-    stream, mod, bias, head_sums = refs[2 * count + heads : 2 * count + heads + 4]
-    refs = refs[2 * count + heads + 4 :]
+    stream, mod, bias, head_sums, mod_weight = refs[2 * count + heads : 2 * count + heads + 5]
+    refs = refs[2 * count + heads + 5 :]
     outs, head_outs = refs[:count], refs[count : count + heads]
-    stream_out, mod_all, bias_all, head_all = refs[count + heads : count + heads + 4]
-    scratch = refs[count + heads + 4 :]
+    stream_out, bias_all, head_all, mod_rows, silu_all = refs[count + heads : count + heads + 5]
+    scratch = refs[count + heads + 5 :]
+    mod_all, silu_own, silu_keep, silu_send, silu_recv, silu_side = scratch[-6:]
+    scratch = scratch[:-6]
     (
         last_send, last_recv, part_send, part_recv, stream_send, stream_recv, small_send,
         mod_recv, bias_recv, head_recv, keep_sem,
@@ -717,7 +771,66 @@
         def _():
             remote_last(layer, slot).start()
 
-    ring.run(finish)
+    def silu_copy(peer):
+        return remote(
+            silu_own, silu_all.at[core, index], silu_send.at[peer], silu_recv.at[index],
+            (core, peer),
+        )
+
+    silu_kept = pltpu.make_async_copy(silu_own, silu_all.at[core, index], silu_keep)
+
+    def others(act):
+        def body(peer):
+            @pl.when(peer != index)
+            def _():
+                act(peer)
+
+        each(0, members, body)
+
+    def midway():
+        def mod_came(source):
+            @pl.when((core != role) | (source != mine))
+            def _():
+                small(
+                    mod, mod_all.at[source], small_send.at[0, 0], mod_recv.at[source],
+                    me["sibling"],
+                ).wait_recv()
+
+        each(0, members, mod_came)
+
+        @pl.when(core == role)
+        def _():
+            own_mod.wait()
+
+        images, depth = mod.shape[0], mod_weight.shape[0]
+        for source in range(members):
+            mod_rows[source * images : (source + 1) * images, :] = wide(mod_all[source])
+        silu_own[...] = jnp.zeros_like(silu_own)
+        silu_own[:, 0:depth] = product_right_t(narrow(mod_rows[...]), mod_weight[...])
+        silu_kept.start()
+        others(lambda peer: silu_copy(peer).start())
+
+    across = remote(
+        silu_all.at[core], silu_all.at[core], silu_side.at[0], silu_side.at[1], me["sibling"]
+    )
+
+    def late():
+        others(
+            lambda peer: remote(
+                silu_own, silu_all.at[core, peer], silu_send.at[peer], silu_recv.at[peer],
+                (core, peer),
+            ).wait_recv()
+        )
+        silu_kept.wait()
+        across.start()
+
+    ring.run(finish, midway, late)
+    others(lambda peer: silu_copy(peer).wait_send())
+    across.wait_send()
+    remote(
+        silu_all.at[1 - core], silu_all.at[1 - core], silu_side.at[0], silu_side.at[1],
+        me["sibling"],
+    ).wait_recv()
 
     @pl.when((role == 0) & (core == 0))
     def _():
@@ -740,14 +853,15 @@
     def _():
         stream_copy.wait()
 
-    smalls(lambda copy: copy.wait_send(), lambda copy: copy.wait_send(), lambda copy: copy.wait())
+    smalls(
+        lambda copy: copy.wait_send(),
+        lambda copy: copy.wait_send(),
+        lambda copy: None if copy is own_mod else copy.wait(),
+    )
 
     def came(source):
         @pl.when((core != role) | (source != mine))
         def _():
-            small(
-                mod, mod_all.at[source], small_send.at[0, 0], mod_recv.at[source], me["sibling"]
-            ).wait_recv()
             small(
                 bias.at[0], bias_all.at[source], small_send.at[1, 0], bias_recv.at[source],
                 me["sibling"],
@@ -773,7 +887,7 @@
             remote_last(layer, slot).wait()
 
 
-def reduce(lefts, rights, head_parts, stream, mod, bias, head_sums, collective_id):
+def reduce(lefts, rights, head_parts, stream, mod, bias, head_sums, mod_weight, collective_id):
     members = lax.axis_size("dp")
     length, count, heads = members // 2, len(lefts), len(head_parts)
     rows = [left.shape[2] for left in lefts]
@@ -781,7 +895,8 @@
     tokens = rights[0].shape[0]
     bf16 = jnp.bfloat16
     inside = pl.BlockSpec(memory_space=pltpu.VMEM)
-    small = [mod.shape, bias.shape[1:], head_sums.shape[1:]]
+    f32 = jnp.float32
+    lines = members * mod.shape[0]
     results = pl.pallas_call(
         functools.partial(reduce_kernel, length, count, heads),
         name="reduce",
@@ -789,11 +904,15 @@
         + [jax.ShapeDtypeStruct((h.shape[0] // 2, h.shape[1]), bf16) for h in head_parts]
         + [jax.ShapeDtypeStruct(stream.shape, stream.dtype)]
         + [
-            jax.ShapeDtypeStruct((members,) + shape, array.dtype)
-            for shape, array in zip(small, (mod, bias, head_sums))
+            jax.ShapeDtypeStruct((members,) + array.shape[1:], array.dtype)
+            for array in (bias, head_sums)
+        ]
+        + [
+            jax.ShapeDtypeStruct((lines, mod.shape[1]), f32),
+            jax.ShapeDtypeStruct((2, members, lines, 128), f32),
         ],
-        in_specs=[ANY] * (2 * count) + [inside] * heads + [ANY] + [inside] * 3,
-        out_specs=[ANY] * (count + heads + 4),
+        in_specs=[ANY] * (2 * count) + [inside] * heads + [ANY] + [inside] * 4,
+        out_specs=[ANY] * (count + heads + 3) + [inside, ANY],
         scratch_shapes=Ring.scratch(length, rows, columns, tokens)
         + [
             DMA((count,)),
@@ -807,60 +926,19 @@
             DMA((members,)),
             DMA((members,)),
             DMA((3,)),
+            pltpu.VMEM((members,) + mod.shape, mod.dtype),
+            pltpu.VMEM((lines, 128), f32),
+            DMA(()),
+            DMA((members,)),
+            DMA((members,)),
+            DMA((2,)),
         ],
         compiler_params=pltpu.CompilerParams(
             collective_id=collective_id, has_side_effects=True, vmem_limit_bytes=VMEM_BYTES
         ),
         cost_estimate=ring_cost(length, rows, columns, tokens),
-    )(*lefts, *rights, *head_parts, stream, mod, bias, head_sums)
+    )(*lefts, *rights, *head_parts, stream, mod, bias, head_sums, mod_weight)
     return (results[:count], results[count : count + heads]) + tuple(results[count + heads :])
-
-
-def spread_kernel(members, given, taken, keep_sem, send_sem, recv_sem):
-    core, index = lax.axis_index("section"), lax.axis_index("dp")
-    here = core * members + index
-    barrier = pltpu.get_barrier_semaphore()
-
-    def others(act):
-        def body(peer):
-            @pl.when(peer != here)
-            def _():
-                act(peer, (peer // members, lax.rem(peer, members)))
-
-        each(0, 2 * members, body)
-
-    def copy(peer, device):
-        return remote(given, taken.at[here], send_sem.at[peer], recv_sem.at[here], device)
-
-    own = pltpu.make_async_copy(given, taken.at[here], keep_sem)
-    own.start()
-    others(
-        lambda peer, device: pl.semaphore_signal(
-            barrier, inc=1, device_id=device, device_id_type=MESH
-        )
-    )
-    pl.semaphore_wait(barrier, 2 * members - 1)
-    others(lambda peer, device: copy(peer, device).start())
-    others(lambda peer, device: copy(peer, device).wait_send())
-    others(
-        lambda peer, device: remote(
-            given, taken.at[peer], send_sem.at[peer], recv_sem.at[peer], device
-        ).wait_recv()
-    )
-    own.wait()
-
-
-def spread(block, collective_id):
-    members = lax.axis_size("dp")
-    return pl.pallas_call(
-        functools.partial(spread_kernel, members),
-        name="spread",
-        out_shape=jax.ShapeDtypeStruct((2 * members,) + block.shape, block.dtype),
-        in_specs=[pl.BlockSpec(memory_space=pltpu.VMEM)],
-        out_specs=ANY,
-        scratch_shapes=[DMA(()), DMA((2 * members,)), DMA((2 * members,))],
-        compiler_params=pltpu.CompilerParams(collective_id=collective_id, has_side_effects=True),
-    )(block)
 
 
 def local_grad(function, primal, cotangent_in):
@@ -869,11 +947,6 @@
 
 def column_sums(values):
     return jnp.sum(wide(values), 0)
-
-
-def blocked_t(values, members):
-    tokens, features = values.shape
-    return values.T.reshape(members // 2, 2, features // members, tokens)
 
 
 def normed_of(values):
@@ -895,9 +968,16 @@
     return jnp.where(keep, block, jnp.zeros_like(block))
 
 
+def lay_shards(left, values):
+    rows = left.shape[2]
+    turned = values.T
+    for shard in range(values.shape[1] // rows):
+        left[shard // 2, shard % 2] = turned[shard * rows : (shard + 1) * rows]
+
+
 def attend_kernel(
     head_count, hidden, pieces, pack_w, pack_b, out_w, out_b,
-    input_out, packed_out, probs_out, mixed_out, attn_out, after_out, mixed_acc,
+    input_left, packed_out, probs_out, mixed_left, attn_out, after_out, mixed_acc,
 ):
     channels = hidden.shape[1]
     head_size = channels // head_count
@@ -905,7 +985,7 @@
     residual = wide(hidden[...])
     normed, _ = normed_of(residual)
     attn_input = narrow(normed * (1.0 + pieces[0, 1:2]) + pieces[0, 0:1])
-    input_out[...] = attn_input
+    lay_shards(input_left, attn_input)
     packed_out[...] = narrow(product(attn_input, pack_w[...]) + pack_b[...])
     mixed_acc[...] = jnp.zeros_like(mixed_acc)
     for head in range(head_count):
@@ -921,7 +1001,7 @@
         probs_out[0, head] = probs
         mixed_acc[:, base : base + width] += product(probs, values)
     mixed = narrow(mixed_acc[...])
-    mixed_out[...] = mixed
+    lay_shards(mixed_left, mixed)
     out = product(mixed, out_w[...]) + out_b[...]
     attn_out[...] = narrow(out)
     after_out[...] = residual + pieces[0, 2:3] * out
@@ -936,8 +1016,9 @@
     return pl.BlockSpec(shape, lambda i: zeros, pipeline_mode=pl.Buffered(1))
 
 
-def attend(hidden, pieces, pack_w, pack_b, out_w, out_b):
+def attend(hidden, pieces, pack_w, pack_b, out_w, out_b, members):
     tokens, channels = hidden.shape
+    left = (members // 2, 2, channels // members)
     images = pieces.shape[0]
     seq = tokens // images
     bf16, f32 = jnp.bfloat16, jnp.float32
@@ -955,18 +1036,18 @@
             fixed_spec(out_b.shape),
         ],
         out_specs=[
-            rows_spec(seq, channels),
+            pl.BlockSpec(left + (seq,), lambda i: (0, 0, 0, i)),
             rows_spec(seq, 3 * channels),
             pl.BlockSpec((1, HEADS, seq, seq), lambda i: (i, 0, 0, 0)),
-            rows_spec(seq, channels),
+            pl.BlockSpec(left + (seq,), lambda i: (0, 0, 0, i)),
             rows_spec(seq, channels),
             rows_spec(seq, channels),
         ],
         out_shape=[
-            jax.ShapeDtypeStruct((tokens, channels), bf16),
+            jax.ShapeDtypeStruct(left + (tokens,), bf16),
             jax.ShapeDtypeStruct((tokens, 3 * channels), bf16),
             jax.ShapeDtypeStruct((images, HEADS, seq, seq), bf16),
-            jax.ShapeDtypeStruct((tokens, channels), bf16),
+            jax.ShapeDtypeStruct(left + (tokens,), bf16),
             jax.ShapeDtypeStruct((tokens, channels), bf16),
             jax.ShapeDtypeStruct((tokens, channels), f32),
         ],
@@ -987,7 +1068,7 @@
 
 def mlp_kernel(
     after, pieces, up_w, up_b, down_w, down_b,
-    input_out, act_out, slope_out, mlp_out, final_out, input_keep, total,
+    input_left, act_left, slope_out, mlp_out, final_out, input_keep, total,
 ):
     step, steps = pl.program_id(0), pl.num_programs(0)
     images = pieces.shape[0]
@@ -997,7 +1078,7 @@
         normed, _ = normed_of(per_image(after[...], images))
         rows = narrow(normed * (1.0 + pieces[:, 4:5]) + pieces[:, 3:4]).reshape(after.shape)
         input_keep[...] = rows
-        input_out[...] = rows
+        lay_shards(input_left, rows)
         total[...] = jnp.zeros_like(total)
 
     pre = product(input_keep[...], up_w[...]) + up_b[...]
@@ -1005,7 +1086,7 @@
     tanh = jnp.tanh(GELU_A * pre * (1.0 + GELU_B * square))
     half = 0.5 + 0.5 * tanh
     act = narrow(pre * half)
-    act_out[...] = act
+    lay_shards(act_left, act)
     slope_out[...] = narrow(
         half + pre * (0.5 - 0.5 * tanh * tanh) * (GELU_A + (3.0 * GELU_A * GELU_B) * square)
     )
@@ -1023,12 +1104,15 @@
     return 1152 if width % 1152 == 0 else width
 
 
-def mlp(after, pieces, up_w, up_b, down_w, down_b):
+def mlp(after, pieces, up_w, up_b, down_w, down_b, members):
     tokens, channels = after.shape
     width = up_w.shape[1]
     tile = feed_tile(width)
     bf16, f32 = jnp.bfloat16, jnp.float32
     columns = pl.BlockSpec((tokens, tile), lambda i: (0, i))
+    left = (members // 2, 2, channels // members, tokens)
+    rows = width // members
+    act_block = (tile // (2 * rows), 2, rows, tokens)
     return pl.pallas_call(
         mlp_kernel,
         grid=(width // tile,),
@@ -1042,15 +1126,15 @@
             fixed_spec(down_b.shape),
         ],
         out_specs=[
-            fixed_spec((tokens, channels)),
-            columns,
+            fixed_spec(left),
+            pl.BlockSpec(act_block, lambda i: (i, 0, 0, 0)),
             columns,
             fixed_spec((tokens, channels)),
             fixed_spec((tokens, channels)),
         ],
         out_shape=[
-            jax.ShapeDtypeStruct((tokens, channels), bf16),
-            jax.ShapeDtypeStruct((tokens, width), bf16),
+            jax.ShapeDtypeStruct(left, bf16),
+            jax.ShapeDtypeStruct((members // 2, 2, rows, tokens), bf16),
             jax.ShapeDtypeStruct((tokens, width), bf16),
             jax.ShapeDtypeStruct((tokens, channels), bf16),
             jax.ShapeDtypeStruct((tokens, channels), bf16),
@@ -1250,18 +1334,24 @@
     )(hidden, pieces, packed, probs, grad_attn, grad_after, pack_w, out_w)
 
 
-def block_forward(hidden, pieces, weights):
+def block_forward(hidden, pieces, weights, members):
     pack_w, pack_b, out_w, out_b, up_w, up_b, down_w, down_b = weights
-    attn_input, packed, probs, mixed, attn_out, after = attend(
-        hidden, pieces, pack_w, pack_b, out_w, out_b
-    )
-    mlp_input, act, slope, mlp_out, final = mlp(after, pieces, up_w, up_b, down_w, down_b)
-    return final, (attn_input, packed, probs, mixed, attn_out, after, mlp_input, act, slope, mlp_out)
+    input_left, packed, probs, mixed_left, attn_out, after = attend(
+        hidden, pieces, pack_w, pack_b, out_w, out_b, members
+    )
+    rows_left, act_left, slope, mlp_out, final = mlp(
+        after, pieces, up_w, up_b, down_w, down_b, members
+    )
+    return (
+        final,
+        (packed, probs, attn_out, after, slope, mlp_out),
+        (act_left, rows_left, mixed_left, input_left),
+    )
 
 
 def block_backward(hidden, saved_state, pieces, weights, grad):
     pack_w, pack_b, out_w, out_b, up_w, up_b, down_w, down_b = weights
-    attn_input, packed, probs, mixed, attn_out, after, mlp_input, act, slope, mlp_out = saved_state
+    packed, probs, attn_out, after, slope, mlp_out = saved_state
     grad_mlp, grad_pre, grad_after, grad_attn, high_sums, pre_sums, out_sums = mlp_back(
         grad, after, pieces, slope, mlp_out, attn_out, up_w, down_w
     )
@@ -1272,54 +1362,176 @@
     grad_mod = narrow(
         jnp.concatenate([low_sums[:, 0:2], high_sums[:, 2:6]], 1).reshape(images, 6 * channels)
     )
-    pack_row = pack_sums[0]
+    pack_row = pack_sums[0:1]
     bias_grads = (
-        jnp.concatenate([pack_row[:channels], pack_row[2 * channels :]]),
-        out_sums[1, 0],
-        pre_sums[0],
-        out_sums[0, 0],
+        jnp.concatenate([pack_row[:, :channels], pack_row[:, 2 * channels :]], 1),
+        out_sums[1, 0:1],
+        pre_sums[0:1],
+        out_sums[0, 0:1],
     )
     return grad_hidden, (grad_mlp, grad_pre, grad_attn, grad_packed), bias_grads, grad_mod
 
 
-def head_pass(hidden_rows, target_rows, live_rows, head_weights, members):
-    in_weight, in_bias, mid_weight, mid_bias, out_weight, out_bias = head_weights
-    pre_first = product(hidden_rows, in_weight) + in_bias
-    act_first = narrow(jax.nn.silu(pre_first))
-    pre_second = product(act_first, mid_weight) + mid_bias
-    act_second = narrow(jax.nn.silu(pre_second))
-    feature = product(act_second, out_weight) + out_bias
-    inverse_feature = lax.rsqrt(jnp.sum(feature * feature, -1, keepdims=True) + EPSILON)
-    unit_feature = feature * inverse_feature
-    target_float = wide(target_rows)
-    unit_target = target_float * lax.rsqrt(
-        jnp.sum(target_float * target_float, -1, keepdims=True) + EPSILON
-    )
-    cosine = jnp.sum(unit_feature * unit_target, -1)
-    loss_part = 0.5 * jnp.sum(live_rows * (1.0 - cosine))
-    grad_unit = -0.5 * live_rows[:, None] * unit_target
-    grad_feature = narrow(
-        inverse_feature
-        * (grad_unit - unit_feature * jnp.sum(grad_unit * unit_feature, -1, keepdims=True))
-    )
-    grad_second = narrow(
-        local_grad(jax.nn.silu, pre_second, product_right_t(grad_feature, out_weight))
-    )
-    grad_first = narrow(
-        local_grad(jax.nn.silu, pre_first, product_right_t(grad_second, mid_weight))
-    )
-    grad_hidden = product_right_t(grad_first, in_weight)
-
-    def in_halves(values):
-        tokens, features = values.shape
-        rows = features // (2 * members)
-        cut = values.T.reshape(2, members, rows, tokens)
-        return jnp.swapaxes(cut, 0, 1).reshape(members // 2, 2, 2 * rows, tokens)
-
-    lefts = (in_halves(act_second), in_halves(act_first), in_halves(grad_first))
-    rights = (grad_feature, grad_second, hidden_rows)
-    sums = (column_sums(grad_first), column_sums(grad_second), column_sums(grad_feature))
-    return (grad_hidden, loss_part, lefts, rights, sums)
+def silu_parts(values):
+    gate = 0.5 + 0.5 * jnp.tanh(0.5 * values)
+    return values * gate, gate * (1.0 + values * (1.0 - gate))
+
+
+def head_kernel(
+    members, hidden_at, target_at, live, in_w_at, in_b, mid_w_at, mid_b, out_w_at, out_b,
+    grad_hidden_at, last_left_at, mid_left_at, in_left_at, grad_feature_at, grad_second_at,
+    in_sums, mid_sums, out_sums, loss_out,
+    hidden, target, in_w, mid_w, out_w,
+    grad_hidden_out, last_left, mid_left, in_left, grad_feature_out, grad_second_out,
+    act_first, slope_first, act_second, slope_second, grad_first_keep, come_sem, go_sem,
+):
+    width = in_w.shape[1]
+    tile = 512 if width % 512 == 0 else width
+    tiles = [slice(start, start + tile) for start in range(0, width, tile)]
+    rows = width // (2 * members)
+    pairs_in = ((hidden_at, hidden), (in_w_at, in_w), (mid_w_at, mid_w), (out_w_at, out_w), (target_at, target))
+    come = [
+        pltpu.make_async_copy(there, here, come_sem.at[i]) for i, (there, here) in enumerate(pairs_in)
+    ]
+    pairs_out = (
+        (grad_hidden_out, grad_hidden_at),
+        (last_left, last_left_at),
+        (mid_left, mid_left_at),
+        (in_left, in_left_at),
+        (grad_feature_out, grad_feature_at),
+        (grad_second_out, grad_second_at),
+    )
+    go = [
+        pltpu.make_async_copy(here, there, go_sem.at[i]) for i, (here, there) in enumerate(pairs_out)
+    ]
+
+    def lay(left, values, start):
+        turned = values.T
+        for offset in range(0, values.shape[1], rows):
+            shard = (start + offset) // rows
+            half, index = shard // members, shard % members
+            left[index // 2, index % 2, half * rows : (half + 1) * rows] = turned[
+                offset : offset + rows
+            ]
+
+    @pl.when(lax.rem(lax.axis_index("dp"), 2) == 0)
+    def _():
+        for copy in come:
+            copy.start()
+        come[0].wait()
+        come[1].wait()
+        for at in tiles:
+            act, slope = silu_parts(product(hidden[...], in_w[:, at]) + in_b[:, at])
+            act_first[:, at] = narrow(act)
+            slope_first[:, at] = narrow(slope)
+        come[2].wait()
+        for at in tiles:
+            act, slope = silu_parts(product(act_first[...], mid_w[:, at]) + mid_b[:, at])
+            act_second[:, at] = narrow(act)
+            slope_second[:, at] = narrow(slope)
+            lay(mid_left, act_first[:, at], at.start)
+        go[2].start()
+        come[3].wait()
+        come[4].wait()
+        feature = product(act_second[...], out_w[...]) + out_b[...]
+        inverse = lax.rsqrt(jnp.sum(feature * feature, -1, keepdims=True) + EPSILON)
+        unit = feature * inverse
+        aim = wide(target[...])
+        aim = aim * lax.rsqrt(jnp.sum(aim * aim, -1, keepdims=True) + EPSILON)
+        alive = live[:, 0:1]
+        cosine = jnp.sum(unit * aim, -1, keepdims=True)
+        loss_out[...] = jnp.broadcast_to(
+            0.5 * jnp.sum(alive * (1.0 - cosine), axis=(0, 1), keepdims=True), loss_out.shape
+        )
+        grad_unit = (-0.5 * alive) * aim
+        grad_feature = narrow(
+            inverse * (grad_unit - unit * jnp.sum(grad_unit * unit, -1, keepdims=True))
+        )
+        grad_feature_out[...] = grad_feature
+        go[4].start()
+        out_sums[...] = sum_rows(grad_feature)
+        for at in tiles:
+            grad_second = narrow(
+                wide(slope_second[:, at]) * product_right_t(grad_feature, out_w[at, :])
+            )
+            grad_second_out[:, at] = grad_second
+            mid_sums[:, at] = sum_rows(grad_second)
+            lay(last_left, act_second[:, at], at.start)
+        go[1].start()
+        go[5].start()
+        for at in tiles:
+            grad_first = narrow(
+                wide(slope_first[:, at]) * product_right_t(grad_second_out[...], mid_w[at, :])
+            )
+            grad_first_keep[:, at] = grad_first
+            in_sums[:, at] = sum_rows(grad_first)
+            part = product_right_t(grad_first, in_w[:, at])
+            if at.start == 0:
+                grad_hidden_out[...] = part
+            else:
+                grad_hidden_out[...] += part
+            lay(in_left, grad_first_keep[:, at], at.start)
+        go[0].start()
+        go[3].start()
+        for copy in go:
+            copy.wait()
+
+
+def head_pass(hidden, target, live, head_weights, members):
+    tokens, channels = hidden.shape
+    width, features = head_weights[2].shape[0], target.shape[1]
+    bf16, f32 = jnp.bfloat16, jnp.float32
+    left = ((members // 2, 2, width // members, tokens), bf16)
+    live_lanes = jnp.broadcast_to(live[:, None], (tokens, 128))
+    in_w, in_b, mid_w, mid_b, out_w, out_b = head_weights
+    inside = pl.BlockSpec(memory_space=pltpu.VMEM)
+    work = tokens * (channels * width + width * width + width * features)
+    big = [
+        ((tokens, channels), f32),
+        left,
+        left,
+        left,
+        ((tokens, features), bf16),
+        ((tokens, width), bf16),
+    ]
+    small = [((8, width), f32), ((8, width), f32), ((8, features), f32), ((8, 128), f32)]
+    results = pl.pallas_call(
+        functools.partial(head_kernel, members),
+        name="head",
+        in_specs=[ANY, ANY, inside, ANY, inside, ANY, inside, ANY, inside],
+        out_specs=[ANY] * 6 + [inside] * 4,
+        out_shape=[jax.ShapeDtypeStruct(*leaf) for leaf in big + small],
+        scratch_shapes=[
+            pltpu.VMEM(array.shape, array.dtype) for array in (hidden, target, in_w, mid_w, out_w)
+        ]
+        + [pltpu.VMEM(*leaf) for leaf in big]
+        + [pltpu.VMEM((tokens, width), bf16)] * 5
+        + [DMA((5,)), DMA((6,))],
+        compiler_params=pltpu.CompilerParams(vmem_limit_bytes=VMEM_BYTES),
+        cost_estimate=pl.CostEstimate(
+            flops=4 * work, bytes_accessed=40 * 2**20, transcendentals=0
+        ),
+    )(hidden, target, live_lanes, in_w, in_b[None], mid_w, mid_b[None], out_w, out_b[None])
+    grad_hidden, last_left, mid_left, in_left, grad_feature, grad_second = results[:6]
+    in_sums, mid_sums, out_sums, loss = results[6:]
+    return (
+        grad_hidden,
+        loss[0:1],
+        (last_left, mid_left, in_left),
+        (grad_feature, grad_second),
+        (in_sums[0:1], mid_sums[0:1], out_sums[0:1]),
+    )
+
+
+def hollow(shapes):
+    leaves, form = jax.tree.flatten(shapes)
+    results = pl.pallas_call(
+        lambda *refs: None,
+        name="hollow",
+        out_shape=[jax.ShapeDtypeStruct(leaf.shape, leaf.dtype) for leaf in leaves],
+        out_specs=[ANY if leaf.ndim else pl.BlockSpec(memory_space=pltpu.SMEM) for leaf in leaves],
+    )()
+    return jax.tree.unflatten(form, list(results))
 
 
 def on_device(
@@ -1354,16 +1566,13 @@
     own = 2 * place + core
     channels = tokens_in.shape[1]
     images = tokens_in.shape[0] // SEQ
-    pairs_swap, pairs_up, pairs_back = [], [], []
+    pairs_up, pairs_back, pairs_swap = [], [], []
     for pair in range(members // 2):
         low, high = 2 * pair, 2 * pair + 1
-        pairs_swap += [(low, low), (members + low, high), (high, members + low), (members + high, members + high)]
+        pairs_swap += [(high, members + low)]
         pairs_up += [(low, high), (members + low, members + high)]
         pairs_back += [(high, low), (members + high, members + low)]
     axes = ("section", "dp")
-
-    def swap(values):
-        return lax.ppermute(values, axes, pairs_swap)
 
     all_buckets = lax.all_gather(buckets, "dp", axis=0, tiled=True)
     one_hot = (
@@ -1388,10 +1597,19 @@
     packed_bias = jnp.concatenate(
         list(parts) + [jnp.zeros((lanes - sum(widths),), jnp.bfloat16)]
     ).reshape(16, 128)
-    block_full, head_full, mod_all = gather(
-        (packed_bias, qkv_weight[0], attn_weight[0], up_weight[0], down_weight[0], project_out_weight),
+    block_full, head_full, mod_all, rows_in = gather(
+        (
+            packed_bias,
+            qkv_weight[0],
+            attn_weight[0],
+            up_weight[0],
+            down_weight[0],
+            project_out_weight,
+        ),
         (project_in_weight, project_mid_weight),
         mod_part,
+        tokens_in,
+        cotangent,
         0,
     )
     all_bias, pack_weight, out_weight, first_weight, second_weight, head_last = block_full
@@ -1434,85 +1652,71 @@
     scale_rows = jnp.broadcast_to(out_scale[:, None, None], (images, 2, channels))
     pieces = jnp.concatenate([pieces, scale_rows], 1)
     total_live = wide(jnp.sum(counts)) * SEQ
-    payload = swap(jnp.where(is_first, cotangent, tokens_in))
     crossed = core != role
-    hidden_first = jnp.where(crossed, payload, tokens_in)
-    outer = jnp.where(crossed, payload, cotangent)
-    own_targets = swap(targets)
-
-    def zeros_of(function, *operands_in):
-        shapes = jax.eval_shape(function, *operands_in)
-        return jax.tree.map(lambda leaf: jnp.zeros(leaf.shape, leaf.dtype), shapes)
-
-    def lefts_of(state):
-        attn_input, mixed, mlp_input, act = state[0], state[3], state[6], state[7]
-        return tuple(blocked_t(v, members) for v in (act, mlp_input, mixed, attn_input))
-
-    first_out, saved_state = lax.cond(
+    targets_out, rows_in = lax.optimization_barrier((targets, rows_in))
+    hidden_first = jnp.where(crossed, rows_in, tokens_in)
+    outer = jnp.where(crossed, rows_in, cotangent)
+    own_targets = jnp.where(crossed, lax.ppermute(targets_out, axes, pairs_swap), targets)
+
+    def unused(function, *operands_in):
+        return hollow(jax.eval_shape(function, *operands_in))
+
+    def forward(hidden, mod, block):
+        return block_forward(hidden, mod, block, members)
+
+    first_out, saved_state, first_lefts = lax.cond(
         is_first,
-        block_forward,
-        lambda *operands_in: zeros_of(block_forward, *operands_in),
+        forward,
+        lambda *operands_in: unused(forward, *operands_in),
         hidden_first,
         pieces,
         block_weights,
     )
     hidden_second = lax.ppermute(first_out, axes, pairs_up)
 
-    def do_head(first, target, live, state, head):
-        return head_pass(first, target, live, head, members) + (lefts_of(state),)
-
     def do_second(second, mod, grad, live, block):
-        final, state = block_forward(second, mod, block)
+        final, state, lefts = forward(second, mod, block)
         outer_grad = wide(grad) * live[:, None]
         grad_input, rights, bias_grads, grad_mod = block_backward(
             second, state, mod, block, outer_grad
         )
-        keep = (state[0], state[3], state[6], state[7])
-        return grad_input, final, rights, bias_grads, grad_mod, keep
-
-    def at_front(first, second, mod, grad, target, live, state, block, head):
-        return (
-            do_head(first, target, live, state, head),
-            zeros_of(do_second, second, mod, grad, live, block),
-        )
-
-    def at_back(first, second, mod, grad, target, live, state, block, head):
-        return (
-            zeros_of(do_head, first, target, live, state, head),
-            do_second(second, mod, grad, live, block),
-        )
-
-    head_result, second_result = lax.cond(
+        return grad_input, final, rights, bias_grads, grad_mod, lefts
+
+    head_result = head_pass(first_out, own_targets, token_live, head_weights, members)
+    head_lefts, head_rights = head_result[2:4]
+    head_parts = head_reduce(head_lefts, head_rights + (first_out,), 2)
+    hidden_second, head_result, head_parts = lax.optimization_barrier(
+        (hidden_second, head_result, head_parts)
+    )
+    grad_hidden, loss_part, head_lefts, head_rights, head_sums = head_result
+    second_result = lax.cond(
         is_first,
-        at_front,
-        at_back,
-        first_out,
+        lambda *operands_in: unused(do_second, *operands_in),
+        do_second,
         hidden_second,
         pieces,
         outer,
-        own_targets,
         token_live,
-        saved_state,
         block_weights,
-        head_weights,
-    )
-    grad_hidden, loss_part, head_lefts, head_rights, head_sums, first_lefts = head_result
-    arrived_back = lax.ppermute(second_result[0], axes, pairs_back)
-    head_parts = head_reduce(head_lefts, head_rights, 2)
-
-    def do_first(hidden, state, mod, extra, back_grad, block, lefts, other):
-        grad_input, rights, bias_grads, grad_mod = block_backward(
-            hidden, state, mod, block, wide(back_grad) + extra
-        )
-        return grad_input, rights, bias_grads, grad_mod, lefts
-
-    def keep_second(hidden, state, mod, extra, back_grad, block, lefts, other):
-        attn_input, mixed, mlp_input, act = other[-1]
-        return other[:-1] + (
-            tuple(blocked_t(v, members) for v in (act, mlp_input, mixed, attn_input)),
-        )
-
-    stream, rights, bias_grads, grad_mod, lefts = lax.cond(
+    )
+    send_back = second_result[0]
+    arrived_back = lax.ppermute(send_back, axes, pairs_back)
+    lefts = lax.cond(
+        is_first,
+        lambda one, other: one,
+        lambda one, other: other,
+        first_lefts,
+        second_result[-1],
+    )
+    arrived_back, lefts = lax.optimization_barrier((arrived_back, lefts))
+
+    def do_first(hidden, state, mod, extra, back_grad, block, other):
+        return block_backward(hidden, state, mod, block, wide(back_grad) + extra)
+
+    def keep_second(hidden, state, mod, extra, back_grad, block, other):
+        return other
+
+    stream, rights, bias_grads, grad_mod = lax.cond(
         is_first,
         do_first,
         keep_second,
@@ -1522,42 +1726,42 @@
         grad_hidden,
         arrived_back,
         block_weights,
-        first_lefts,
-        second_result[1:],
+        second_result[1:-1],
     )
     bias_rows = jnp.concatenate([grads.reshape(members, -1) for grads in bias_grads], 1)
     bias_width = bias_rows.shape[1]
     bias_rows = jnp.pad(bias_rows, ((0, 0), (0, 1024 - bias_width))).reshape(members, 8, 128)
     in_sums, mid_sums, out_sums = head_sums
     devices = 2 * members
-    out_width = out_sums.shape[0]
+    out_width = out_sums.shape[1]
     head_rows = jnp.concatenate(
         [
             in_sums.reshape(devices, -1),
             mid_sums.reshape(devices, -1),
-            jnp.broadcast_to(out_sums[None], (devices, out_width)),
-            jnp.broadcast_to(loss_part[None, None], (devices, 1)),
+            jnp.broadcast_to(out_sums, (devices, out_width)),
+            jnp.broadcast_to(loss_part[:, 0:1], (devices, 1)),
         ],
         1,
     )
     head_width = head_rows.shape[1]
     head_rows = jnp.pad(head_rows, ((0, 0), (0, 1024 - head_width))).reshape(devices, 8, 128)
-    mod_width = images * 6 * channels
-    mod_lines = -(-mod_width // 2048) * 16
-    mod_rows = jnp.pad(grad_mod.reshape(-1), (0, mod_lines * 128 - mod_width)).reshape(-1, 128)
-    block_grads, head_grads, stream_in, mod_grads, bias_all, head_all = reduce(
-        lefts, rights, head_parts, stream, mod_rows, bias_rows, head_rows, 3
+    block_grads, head_grads, stream_in, bias_all, head_all, mod_wide, silu_all_terms = reduce(
+        lefts,
+        rights,
+        head_parts,
+        stream,
+        grad_mod,
+        bias_rows,
+        head_rows,
+        modulate_weight[0],
+        3,
     )
     down_grad, up_grad, attn_grad, qkv_grad = block_grads
     stream_own = jnp.where(crossed, stream_in, stream)
-    mod_grad_all = mod_grads.reshape(members, -1)[:, :mod_width].reshape(-1, 6 * channels)
-    silu_part = product_right_t(mod_grad_all, modulate_weight[0])
-    lines = silu_part.shape[0]
-    padded = jnp.pad(silu_part, ((0, 0), (0, 128 - depth)))
-    silu_parts = spread(padded, 4)[:, :, :depth].reshape(2, members, lines, depth)
-    mod_w_grad = product_left_t(silu_depth, mod_grad_all)
-    mod_b_grad = lax.dynamic_slice_in_dim(column_sums(mod_grad_all), index * share, share, 0)
-    silu_total = jnp.swapaxes(jnp.sum(silu_parts, 0), 0, 1).reshape(lines, channels)
+    mod_w_grad = product_left_t(silu_depth, narrow(mod_wide))
+    mod_b_grad = lax.dynamic_slice_in_dim(jnp.sum(mod_wide, 0), index * share, share, 0)
+    silu_total = jnp.sum(silu_all_terms[:, :, :, :depth], 0)
+    silu_total = jnp.swapaxes(silu_total, 0, 1).reshape(-1, channels)
     cond_grad = local_grad(jax.nn.silu, conditioning, silu_total)
     table_grad = jnp.dot(one_hot.T, cond_grad, precision=HIGHEST)
 
@@ -1568,7 +1772,7 @@
         bias_outs.append(bias_sums[offset : offset + width][None])
         offset += width
     sums = jnp.sum(head_all, 0).reshape(-1)
-    head_share = in_sums.shape[0] // devices
+    head_share = in_sums.shape[1] // devices
     loss_value = sums[head_width - 1] / total_live
     return (
         stream_own[None],

time: 862 us -> 759 us (0.88)
  Pallas kernels: 655 us -> 605 us
  local copies, waits for them, and re-layouts: 68.3 us -> 37.9 us
  waiting for transfers between devices: 45.1 us -> 27.2 us
  loops' own time: 23.2 us -> 8.11 us
  other arithmetic: 19.5 us -> 31.4 us
    another operation x28 -> x0, local copies, waits for them, and re-layouts: 44.8 us -> none
    ppermute x3 -> x2, waiting for transfers between devices: 45.1 us -> 16.5 us  [the longest x1 16.5 us: on_device(): arrived_back = lax.ppermute(send_back, axes, pairs_back)]
    pallas_call x1, Pallas kernels: 274 us -> 251 us  [gather(): pl.pallas_call(functools.partial(gather_kernel, length, count, heads), na...]
    pallas_call x1, Pallas kernels: 269 us -> 248 us  [reduce(): pl.pallas_call(functools.partial(reduce_kernel, length, count, heads), na...]
    another operation x2 -> x3, loops' own time: 16.8 us -> 0.86 us  [the longest x1 0.67 us: on_device(): lax.cond(is_first, lambda *operands_in: unused(do_second, *operands_in),...]
    ppermute x1, waiting for transfers between devices: 0.01 us -> 10.7 us  [on_device(): hidden_second = lax.ppermute(first_out, axes, pairs_up)]
    pallas_call x1 -> x2, Pallas kernels: 15.3 us -> 5.5 us  [the longest x1 5.5 us: head_pass(): pl.pallas_call(functools.partial(head_kernel, members), name='head', in_s...]
  transfers between devices with their start and end apart: 4 -> 3, of which waited for: 2 -> 2; matrix products, arithmetic and copies ran while one was open for 2% -> 5% of each run, Pallas kernels for 32% -> 1%
where the time goes in v3:
time: 759 us; the launch traced here: 752 us
  Pallas kernels  605 us (80%)
  local copies, waits for them, and re-layouts  37.9 us (5%)
  other arithmetic  31.4 us (4%)
  waiting for transfers between devices  27.2 us (4%)
  blocking collectives  13.6 us (2%)
  starting transfers between devices  12.9 us (2%)
  matrix products  11.9 us (2%)
  loops' own time  8.11 us (1%)
    pallas_call x1, Pallas kernels, gather(): pl.pallas_call(functools.partial(gather_kernel, length, count, heads), na...  251 us
    pallas_call x1, Pallas kernels, reduce(): pl.pallas_call(functools.partial(reduce_kernel, length, count, heads), na...  248 us
    pallas_call x1, Pallas kernels, mlp_back(): pl.pallas_call(mlp_back_kernel, grid=(width // tile,), name='mlp_back', i...  29 us
    pallas_call x1, Pallas kernels, attend_back(): pl.pallas_call(functools.partial(attend_back_kernel, HEADS), grid=(images...  26.2 us
    pallas_call x1, Pallas kernels, mlp(): pl.pallas_call(mlp_kernel, grid=(width // tile,), name='mlp', in_specs=[f...  25 us
    pallas_call x1, Pallas kernels, attend(): pl.pallas_call(functools.partial(attend_kernel, HEADS), grid=(images,), n...  18.9 us
    ppermute x1, waiting for transfers between devices, on_device(): arrived_back = lax.ppermute(send_back, axes, pairs_back)  16.5 us
  transfers between devices with their start and end apart: 3, of which 2 were waited for; matrix products, arithmetic and copies ran while one was open for 5% of the time, Pallas kernels for 1%

profile of v3, /device:TPU:10, one launch (start us, length us, event | category | flops | bytes accessed | tf_op | source)
XLA Modules:
  0.0 751.9 jit_solution(1725819091037611945)
XLA Ops:
  4.8 13.6 %all-reduce.2 = s32[32]{0:T(128)S(1)} all-reduce(s32[32]{0:T(128)S(1)} %dynamic-update-slice), channel_id=1, replica_groups=mesh['section'=2,'dp'=16] {'dp'}, use_global_device_ids=true, to_apply=%add.2 | all-reduce | flops 32 | bytes 256
  19.1 4.1 add_divide_fusion
  24.3 1.4 reshape.224.refs_8_
  26.5 251.0 %gather.1 = (bf16[16,16,128]{2,1,0:T(8,128)(2,1)}, bf16[16,72,3456]{2,1,0:T(8,128)(2,1)}, bf16[16,72,1152]{2,1,0:T(8,128)(2,1)}, bf16[16,72,4608]{2,1,0:T(8,128)...) custom-call(bf16[16,128]{1,0:T(8,128)(2,1)} %bitcast.105, ...), custom_call_target="tpu_custom_call" | custom-call | bytes 770703360 | tf_op jit(solution)/shard_map/gather/pallas_call | solution.py:430
  277.5 2.2 collective-permute-start.1
  282.5 1.8 reduce_sum.54
  284.3 1.5 reshape.225
  287.1 1.4 slice.134
  288.5 1.4 slice.132
  293.0 1.5 pad_maximum_fusion.2
  295.8 1.4 reshape.244
  297.2 1.4 reshape.245
  303.6 1.4 slice_convert_fusion.7
  305.0 2.1 broadcast_select_fusion.1.target_at
  308.0 5.5 head.1
  315.5 1.4 slice.143
  318.8 10.7 %collective-permute-done = bf16[512,1152]{1,0:T(8,128)(2,1)} collective-permute-done((bf16[512,1152]{1,0:T(8,128)(2,1)}, bf16[512,1152]{1,0:T(8,128)(2,1)}, u32[]{:S(2)}, u32[]{:S(2)}) %collective-permute-start) | collective-permute-done | bytes 1179680 | tf_op jit(solution)/shard_map/ppermute | solution.py:1675
  329.6 108.3 %conditional.5 = ((bf16[512,1152]{1,0:T(8,128)(2,1)}, bf16[512,1152]{1,0:T(8,128)(2,1)}, bf16[512,1152]{1,0:T(8,128)(2,1)}, bf16[512,4608]{1,0:T(8,128)(2,1)}, b...) conditional(s32[]{:T(128)} %convert_element_type.136, ...), branch_computations={%region_3.4_spmd, %region_4.5_spmd} | conditional | flops 34730663936 | bytes 183371936 | solution.py:1692
  329.8 18.9 %attend.3 = (bf16[8,2,72,512]{3,2,1,0:T(8,128)(2,1)}, bf16[512,3456]{1,0:T(8,128)(2,1)}, bf16[2,16,256,256]{3,2,1,0:T(8,128)(2,1)}, bf16[8,2,72,512]{3,2,1,0:T(8...) custom-call(bf16[512,1152]{1,0:T(8,128)(2,1)} %get-tuple-element.159.hidden, ...), custom_call_target="tpu_custom_call" | custom-call | flops 6039797760 | bytes 41943040 | tf_op jit(solution)/shard_map/cond/branch_0_fun/attend/pallas_call | solution.py:1026
  348.6 1.7 convert_multiply_fusion.grad
  350.4 25.0 %mlp.3 = (bf16[8,2,72,512]{3,2,1,0:T(8,128)(2,1)}, bf16[8,2,288,512]{3,2,1,0:T(8,128)(2,1)}, bf16[512,4608]{1,0:T(8,128)(2,1)}, bf16[512,1152]{1,0:T(8,128)(2,1)}, bf16[512,1152]{1,0:T(8,128)(2,1)}) custom-call(f32[512,1152]{1,0:T(8,128)} %get-tuple-element.171.after, f32[2,8,1152]{2,1,0:T(8,128)S(1)} %get-tuple-element.160.pieces, ...), custom_call_target="tpu_custom_call" | custom-call | flops 10871635968 | bytes 41943040 | tf_op jit(solution)/shard_map/cond/branch_0_fun/mlp/pallas_call | solution.py:1116
  375.4 29.0 %mlp_back.2 = (bf16[512,1152]{1,0:T(8,128)(2,1)}, bf16[512,4608]{1,0:T(8,128)(2,1)}, f32[512,1152]{1,0:T(8,128)}, bf16[512,1152]{1,0:T(8,128)(2,1)}, f32[2,8,115...) custom-call(f32[512,1152]{1,0:T(8,128)} %convert_multiply_fusion.grad, ...), custom_call_target="tpu_custom_call" | custom-call | flops 10871635968 | bytes 41943040 | tf_op jit(solution)/shard_map/cond/branch_0_fun/mlp_back/pallas_call | solution.py:1208
  404.4 26.2 %attend_back.2 = (bf16[512,3456]{1,0:T(8,128)(2,1)}, bf16[512,1152]{1,0:T(8,128)(2,1)}, f32[2,8,1152]{2,1,0:T(8,128)}, f32[8,3456]{1,0:T(8,128)}) custom-call(bf16[512,1152]{1,0:T(8,128)(2,1)} %get-tuple-element.159.hidden, f32[2,8,1152]{2,1,0:T(8,128)S(1)} %get-tuple-element.160.pieces, bf16[512,3456]{1,0:T(8,128)(2,1)} %get-tuple-element.165.packed, ...), custom_call_target="tpu_custom_call" | custom-call | flops 6945767424 | bytes 41943040 | tf_op jit(solution)/shard_map/cond/branch_0_fun/attend_back/pallas_call | solution.py:1300
  432.0 1.4 slice_bitcast_fusion
  433.4 1.5 slice.93
  437.8 9.4 %collective-permute-start.2 = (bf16[512,1152]{1,0:T(8,128)(2,1)}, bf16[512,1152]{1,0:T(8,128)(2,1)}, u32[]{:S(2)}, u32[]{:S(2)}) collective-permute-start(bf16[512,1152]{1,0:T(8,128)(2,1)} %get-tuple-element.367), channel_id=1, source_target_pairs={{1,0},{17,16},{3,2},{19,18},{5,4},{21,20},{7,6},{23,22},{9,8},{25,... | collective-permute-start | bytes 3538952 | tf_op jit(solution)/shard_map/ppermute | solution.py:1703
  449.7 1.4 reduce.18
  454.0 16.5 %collective-permute-done.2 = bf16[512,1152]{1,0:T(8,128)(2,1)} collective-permute-done((bf16[512,1152]{1,0:T(8,128)(2,1)}, bf16[512,1152]{1,0:T(8,128)(2,1)}, u32[]{:S(2)}, u32[]{:S(2)}) %collective-permute-start.2) | collective-permute-done | bytes 1179680 | tf_op jit(solution)/shard_map/ppermute | solution.py:1703
  470.6 8.1 %conditional.7 = (bf16[512,1152]{1,0:T(8,128)(2,1)}, bf16[512,1152]{1,0:T(8,128)(2,1)}, bf16[512,4608]{1,0:T(8,128)(2,1)}, bf16[512,1152]{1,0:T(8,128)(2,1)}, bf...) conditional(s32[]{:T(128)} %convert_element_type.136, ...), branch_computations={%region_7.8_spmd, %region_8.9_spmd} | conditional | flops 17818640384 | bytes 99793064 | solution.py:1719
  481.1 248.4 %reduce.20 = (bf16[288,1152]{1,0:T(8,128)(2,1)}, bf16[72,4608]{1,0:T(8,128)(2,1)}, bf16[72,1152]{1,0:T(8,128)(2,1)}, bf16[72,3456]{1,0:T(8,128)(2,1)}, bf16[64,7...) custom-call(bf16[8,2,288,512]{3,2,1,0:T(8,128)(2,1)} %get-tuple-elem, ...), custom_call_target="tpu_custom_call" | custom-call | flops 16307453952 | bytes 509607936 | tf_op jit(solution)/shard_map/reduce/pallas_call | solution.py:900
  729.6 3.0 convolution_bitcast_fusion
  737.9 4.4 fusion.3
  (165 shorter events, 48.8 us)
Async XLA Ops:
  18.4 4.8 copy-start.34
  19.1 4.8 copy-start.9
  24.2 1.5 copy-start.38
  24.2 1.5 copy-start.39
  24.3 1.5 copy-start.40
  24.3 2.2 copy-start.1
  26.5 263.4 %copy-start = (bf16[512,1152]{1,0:T(8,128)(2,1)S(1)}, bf16[512,1152]{1,0:T(8,128)(2,1)}, u32[]{:S(2)}) copy-start(bf16[512,1152]{1,0:T(8,128)(2,1)} %refs_9_.1) | copy-start | bytes 3538948
  277.5 27.5 %collective-permute-start.1 = (bf16[512,768]{1,0:T(8,128)(2,1)}, bf16[512,768]{1,0:T(8,128)(2,1)}, u32[]{:S(2)}, u32[]{:S(2)}) collective-permute-start(bf16[512,768]{1,0:T(8,128)(2,1)} %param.32), channel_id=1, source_target_pairs={{1,16},{3,18},{5,20},{7,22},{9,24},{11,26},{13,28},{15,30}} | collective-permute-start | bytes 2359304 | tf_op jit(solution)/shard_map/ppermute | solution.py:1659
  299.5 30.0 %collective-permute-start = (bf16[512,1152]{1,0:T(8,128)(2,1)}, bf16[512,1152]{1,0:T(8,128)(2,1)}, u32[]{:S(2)}, u32[]{:S(2)}) collective-permute-start(bf16[512,1152]{1,0:T(8,128)(2,1)} %get-tuple-element.348.hidden_at.refs_5_), channel_id=1, source_target_pairs={{0,1},{16,17},{2,3},{18,19},{4,5},{20,21},{6,7},{22,23},{8,9},{24,... | collective-permute-start | bytes 3538952 | tf_op jit(solution)/shard_map/ppermute | solution.py:1675
  305.0 2.1 copy-start.30
  318.3 11.2 %copy-start.37 = (f32[2]{0:T(128)S(1)}, f32[2]{0:T(128)}, u32[]{:S(2)}) copy-start(f32[2]{0:T(128)} %copy-done.36) | copy-start | bytes 28
  318.3 11.3 %copy-start.21 = (f32[2,8,1152]{2,1,0:T(8,128)S(1)}, f32[2,8,1152]{2,1,0:T(8,128)}, u32[]{:S(2)}) copy-start(f32[2,8,1152]{2,1,0:T(8,128)} %pad_maximum_fusion.2) | copy-start | bytes 221188
  318.3 11.3 %copy-start.27 = (f32[1,4608]{1,0:T(1,128)S(1)}, f32[1,4608]{1,0:T(1,128)}, u32[]{:S(2)}) copy-start(f32[1,4608]{1,0:T(1,128)} %reshape.245) | copy-start | bytes 55300
  318.3 11.3 %copy-start.29 = (f32[1,3456]{1,0:T(1,128)S(1)}, f32[1,3456]{1,0:T(1,128)}, u32[]{:S(2)}) copy-start(f32[1,3456]{1,0:T(1,128)} %broadcast_in_dim.102) | copy-start | bytes 41476
  318.3 11.3 %copy-start.31 = (f32[1,1152]{1,0:T(1,128)S(1)}, f32[1,1152]{1,0:T(1,128)}, u32[]{:S(2)}) copy-start(f32[1,1152]{1,0:T(1,128)} %reshape.244) | copy-start | bytes 13828
  318.3 11.3 %copy-start.32 = (f32[1,1152]{1,0:T(1,128)S(1)}, f32[1,1152]{1,0:T(1,128)}, u32[]{:S(2)}) copy-start(f32[1,1152]{1,0:T(1,128)} %reshape.246) | copy-start | bytes 13828
  375.4 29.0 %copy-start.43 = (bf16[1152,1152]{1,0:T(8,128)(2,1)S(1)}, bf16[1152,1152]{1,0:T(8,128)(2,1)}, u32[]{:S(2)}) copy-start(bf16[1152,1152]{1,0:T(8,128)(2,1)} %get-tuple-element.163.out_w) | copy-start | bytes 7962628 | tf_op jit(solution)/shard_map/cond
  437.8 32.7 %collective-permute-start.2 = (bf16[512,1152]{1,0:T(8,128)(2,1)}, bf16[512,1152]{1,0:T(8,128)(2,1)}, u32[]{:S(2)}, u32[]{:S(2)}) collective-permute-start(bf16[512,1152]{1,0:T(8,128)(2,1)} %get-tuple-element.367), channel_id=1, source_target_pairs={{1,0},{17,16},{3,2},{19,18},{5,4},{21,20},{7,6},{23,22},{9,8},{25,... | collective-permute-start | bytes 3538952 | tf_op jit(solution)/shard_map/ppermute | solution.py:1703
  454.0 16.5 %copy-start.3 = (f32[512,1152]{1,0:T(8,128)S(1)}, f32[512,1152]{1,0:T(8,128)}, u32[]{:S(2)}) copy-start(f32[512,1152]{1,0:T(8,128)} %get-tuple-element.395) | copy-start | bytes 7077892
  454.0 16.5 %copy-start.26 = (f32[1,1152]{1,0:T(1,128)S(1)}, f32[1,1152]{1,0:T(1,128)}, u32[]{:S(2)}) copy-start(f32[1,1152]{1,0:T(1,128)} %get-tuple-element.385) | copy-start | bytes 13828
  729.6 3.1 copy-start.2
  729.6 3.2 copy-start.25
  729.6 4.4 copy-start.24
  729.6 6.2 copy-start.7
  729.6 6.2 copy-start.8
  737.9 5.1 copy-start.15
  742.3 1.7 copy-start.18
  742.3 2.4 copy-start.11
  744.0 2.5 copy-start.10
  745.9 1.7 copy-start.19
  746.4 1.9 copy-start.16
  746.5 2.7 copy-start.20
  (8 other events, 8.6 us)

commit v4 on v3

--- a/solution.py
+++ b/solution.py
@@ -99,16 +99,17 @@
     lax.fori_loop(first, last, step, 0)
 
 
-def gather_kernel(length, count, heads, *refs):
+def gather_kernel(length, count, heads, widths, *refs):
     total = count + heads
     shards, (mod_part, tokens, cotangent) = refs[:total], refs[total : total + 3]
     refs = refs[total + 3 :]
-    full, (mod_all, rows_in) = refs[:total], refs[total : total + 2]
+    full, (mod_all, rows_in, block_bias, head_bias) = refs[:total], refs[total : total + 4]
     (
         own_sem, swap_send, swap_recv, ring_send, ring_recv, side_send, side_recv,
         cross_send, cross_recv, mod_send, mod_recv, mod_sem, rows_send, rows_recv, mod_pair, mod_in,
         mod_sum,
-    ) = refs[total + 2 :]
+        bias_in, bias_sem,
+    ) = refs[total + 4 :]
     me = whereabouts(length)
     core, role, place, at = me["core"], me["role"], me["place"], me["at"]
     members = 2 * length
@@ -409,6 +410,27 @@
 
         each(0, length, head_end)
 
+    fetch = pltpu.make_async_copy(full[0], bias_in, bias_sem)
+    fetch.start()
+    fetch.wait()
+    block_bias[...] = jnp.zeros_like(block_bias)
+    channels = tokens.shape[1]
+    for shard in range(members):
+        block = wide(bias_in[shard])
+        line, start = 0, 0
+        for part, width in enumerate(widths):
+            if part == 4:
+                start = 0
+            target = block_bias if part < 4 else head_bias
+            first = start + shard * width
+            if part == 0 and first >= channels:
+                first += channels
+            for offset in range(0, width, 128):
+                size = min(128, width - offset)
+                target[:, first + offset : first + offset + size] = block[line : line + 1, :size]
+                line += 1
+            start += members * width + (channels if part == 0 else 0)
+
     @pl.when((core == 0) & (role == 1))
     def _():
         swap_out(count - 1).wait_send()
@@ -420,7 +442,7 @@
         rows_move(tokens).wait()
 
 
-def gather(shards, head_shards, mod_part, tokens, cotangent, collective_id):
+def gather(shards, head_shards, mod_part, tokens, cotangent, widths, collective_id):
     members = lax.axis_size("dp")
     length, count, heads = members // 2, len(shards), len(head_shards)
     total = count + heads
@@ -428,13 +450,17 @@
     moved = sum(shard.size * 2 for shard in everything) * members
     inside = pl.BlockSpec(memory_space=pltpu.VMEM)
     results = pl.pallas_call(
-        functools.partial(gather_kernel, length, count, heads),
+        functools.partial(gather_kernel, length, count, heads, widths),
         name="gather",
         out_shape=[jax.ShapeDtypeStruct((members,) + s.shape, s.dtype) for s in everything]
         + [jax.ShapeDtypeStruct((length,) + mod_part.shape[1:], mod_part.dtype)]
-        + [jax.ShapeDtypeStruct(tokens.shape, tokens.dtype)],
+        + [
+            jax.ShapeDtypeStruct(tokens.shape, tokens.dtype),
+            jax.ShapeDtypeStruct((1, members * sum(widths[:4]) + tokens.shape[1]), jnp.float32),
+            jax.ShapeDtypeStruct((1, members * sum(widths[4:])), jnp.float32),
+        ],
         in_specs=[inside] * (total + 1) + [ANY] * 2,
-        out_specs=[ANY] * (total + 2),
+        out_specs=[ANY] * (total + 2) + [inside] * 2,
         scratch_shapes=[
             DMA((total,)),
             DMA((total,)),
@@ -453,6 +479,8 @@
             DMA((2,)),
             pltpu.VMEM(mod_part.shape, mod_part.dtype),
             pltpu.VMEM(mod_part.shape, mod_part.dtype),
+            pltpu.VMEM((members,) + shards[0].shape, shards[0].dtype),
+            DMA(()),
         ],
         compiler_params=pltpu.CompilerParams(
             collective_id=collective_id, has_side_effects=True, vmem_limit_bytes=VMEM_BYTES
@@ -470,10 +498,10 @@
 
 
 class Ring:
-    def __init__(self, me, length, lefts, rights, scratch):
-        count = len(lefts)
+    def __init__(self, me, length, variants, scratch):
+        count = len(variants[0][1])
         self.me, self.length, self.layers = me, length, range(count)
-        self.lefts, self.rights = lefts, rights
+        self.variants = variants
         self.left_all, self.right_all = scratch[:count], scratch[count : 2 * count]
         self.arrived, self.leaving = scratch[2 * count : 3 * count], scratch[3 * count : 4 * count]
         (
@@ -481,7 +509,7 @@
         ) = scratch[4 * count : 4 * count + 5]
 
     @staticmethod
-    def scratch(length, rows, columns, tokens):
+    def scratch(length, rows, columns, tokens, parts):
         bf16, count = jnp.bfloat16, len(rows)
         return (
             [pltpu.VMEM((2, length, r, tokens), bf16) for r in rows]
@@ -489,9 +517,9 @@
             + [pltpu.VMEM((length - 1, r, c), bf16) for r, c in zip(rows, columns)]
             + [pltpu.VMEM((2, r, c), bf16) for r, c in zip(rows, columns)]
             + [
-                DMA((count, 2)),
-                DMA((count, 2)),
-                DMA((count, 2)),
+                DMA((count, 2 * parts)),
+                DMA((count, 2 * parts)),
+                DMA((count, 2 * parts)),
                 DMA((count, 2)),
                 DMA((count, length)),
             ]
@@ -499,9 +527,9 @@
 
     def chunk(self, layer, slot, turn, add):
         spot = self.me["at"](-(turn + 1))
-        columns = self.rights[layer].shape[1]
+        left, right = self.left_all[layer], self.right_all[layer]
+        columns = right.shape[2]
         tile = tile_of(columns)
-        left, right = self.left_all[layer], self.right_all[layer]
 
         def body(index):
             start = pl.multiple_of(index * tile, tile)
@@ -523,39 +551,54 @@
             self.me["onward"],
         )
 
-    def inputs(self, layer):
+    def inputs(self, layer, lefts, rights):
         core, sibling = self.me["core"], self.me["sibling"]
-        return [
-            pltpu.make_async_copy(
-                self.lefts[layer].at[:, core], self.left_all[layer].at[0], self.own_sem.at[layer, 0]
-            ),
-            pltpu.make_async_copy(
-                self.rights[layer], self.right_all[layer].at[0], self.own_sem.at[layer, 1]
-            ),
-            remote(
-                self.lefts[layer].at[:, 1 - core],
-                self.left_all[layer].at[1],
-                self.side_send.at[layer, 0],
-                self.side_recv.at[layer, 0],
-                sibling,
-            ),
-            remote(
-                self.rights[layer],
-                self.right_all[layer].at[1],
-                self.side_send.at[layer, 1],
-                self.side_recv.at[layer, 1],
-                sibling,
-            ),
-        ]
+        left_all, right_all = self.left_all[layer], self.right_all[layer]
+        copies, sem, start = [], 0, 0
+
+        def both(mine, own_to, other, other_to):
+            nonlocal sem
+            at = (layer, sem)
+            sem += 1
+            copies.append(pltpu.make_async_copy(mine, own_to, self.own_sem.at[at]))
+            copies.append(
+                remote(other, other_to, self.side_send.at[at], self.side_recv.at[at], sibling)
+            )
+
+        for part in lefts[layer]:
+            lanes = pl.ds(start, part.shape[3])
+            both(
+                part.at[:, core],
+                left_all.at[0, :, :, lanes],
+                part.at[:, 1 - core],
+                left_all.at[1, :, :, lanes],
+            )
+            start += part.shape[3]
+        start = 0
+        for part in rights[layer]:
+            rows = pl.ds(start, part.shape[0])
+            both(part, right_all.at[0, rows], part, right_all.at[1, rows])
+            start += part.shape[0]
+        return copies
+
+    def fetch(self, layer, act):
+        for predicate, lefts, rights in self.variants:
+
+            def body():
+                for copy in self.inputs(layer, lefts, rights):
+                    act(copy)
+
+            if predicate is None:
+                body()
+            else:
+                pl.when(predicate)(body)
 
     def run(self, finish, midway=None, late=None):
         length = self.length
         for layer in self.layers:
-            for copy in self.inputs(layer):
-                copy.start()
+            self.fetch(layer, lambda copy: copy.start())
         for layer in self.layers:
-            for copy in self.inputs(layer):
-                copy.wait()
+            self.fetch(layer, lambda copy: copy.wait())
             self.chunk(layer, 0, 0, False)
             self.onward(layer, 0, 0).start()
 
@@ -604,7 +647,7 @@
     @pl.when(me["role"] == 0)
     def _():
         greet([me["onward"], me["before"], me["sibling"]])
-        ring = Ring(me, length, lefts, rights, scratch[:-1])
+        ring = Ring(me, length, [(None, [[v] for v in lefts], [[v] for v in rights])], scratch[:-1])
 
         def last(layer, slot):
             return pltpu.make_async_copy(
@@ -627,7 +670,7 @@
         out_shape=[jax.ShapeDtypeStruct((r, c), jnp.bfloat16) for r, c in zip(rows, columns)],
         in_specs=[ANY] * (2 * count),
         out_specs=[ANY] * count,
-        scratch_shapes=Ring.scratch(length, rows, columns, tokens) + [DMA((count,))],
+        scratch_shapes=Ring.scratch(length, rows, columns, tokens, 1) + [DMA((count,))],
         compiler_params=pltpu.CompilerParams(
             collective_id=collective_id, has_side_effects=True, vmem_limit_bytes=VMEM_BYTES
         ),
@@ -635,11 +678,12 @@
     )(*lefts, *rights)
 
 
-def reduce_kernel(length, count, heads, *refs):
-    lefts, rights = refs[:count], refs[count : 2 * count]
-    head_parts = refs[2 * count : 2 * count + heads]
-    stream, mod, bias, head_sums, mod_weight = refs[2 * count + heads : 2 * count + heads + 5]
-    refs = refs[2 * count + heads + 5 :]
+def reduce_kernel(length, form, count, heads, *refs):
+    operands = form.num_leaves
+    fronts, backs, head_parts, mod, bias, head_sums, mod_weight = jax.tree.unflatten(
+        form, refs[:operands]
+    )
+    refs = refs[operands:]
     outs, head_outs = refs[:count], refs[count : count + heads]
     stream_out, bias_all, head_all, mod_rows, silu_all = refs[count + heads : count + heads + 5]
     scratch = refs[count + heads + 5 :]
@@ -665,11 +709,30 @@
     each(0, 2 * members, greet_all)
     pl.semaphore_wait(barrier, 2 * members - 1)
 
-    stream_copy = remote(stream, stream_out, stream_send, stream_recv, me["partner"])
-
-    @pl.when(core != role)
-    def _():
-        stream_copy.start()
+    unit = fronts[2][0].shape[0]
+
+    def streams(act):
+        for there, parts in ((0, fronts[2]), (1, backs[2])):
+
+            @pl.when((role == there) & (core != role))
+            def _():
+                cuts = [
+                    part.at[pl.ds(start, unit)]
+                    for part in parts
+                    for start in range(0, part.shape[0], unit)
+                ]
+                for i, cut in enumerate(cuts):
+                    act(
+                        remote(
+                            cut,
+                            stream_out.at[pl.ds(i * unit, unit)],
+                            stream_send.at[i],
+                            stream_recv.at[i],
+                            me["partner"],
+                        )
+                    )
+
+    streams(lambda copy: copy.start())
 
     def small(source, target, send, recv, device):
         return remote(source, target, send, recv, device)
@@ -751,7 +814,8 @@
             handed(layer, 0, (0, 2 * place + 1)).start()
             handed(layer, 1, (1, 2 * place + 1)).start()
 
-    ring = Ring(me, length, lefts, rights, scratch[:-11])
+    variants = [(role == 0,) + tuple(fronts[:2]), (role == 1,) + tuple(backs[:2])]
+    ring = Ring(me, length, variants, scratch[:-11])
 
     def local_last(layer, slot):
         return pltpu.make_async_copy(ring.leaving[layer].at[slot], outs[layer], last_send.at[layer])
@@ -849,10 +913,7 @@
         for layer in range(heads):
             handed(layer, 0, me["sibling"]).wait_recv()
 
-    @pl.when(core != role)
-    def _():
-        stream_copy.wait()
-
+    streams(lambda copy: copy.wait())
     smalls(
         lambda copy: copy.wait_send(),
         lambda copy: copy.wait_send(),
@@ -887,22 +948,29 @@
             remote_last(layer, slot).wait()
 
 
-def reduce(lefts, rights, head_parts, stream, mod, bias, head_sums, mod_weight, collective_id):
+def reduce(fronts, backs, head_parts, mod, bias, head_sums, mod_weight, collective_id):
     members = lax.axis_size("dp")
+    lefts, rights, streams = fronts
     length, count, heads = members // 2, len(lefts), len(head_parts)
-    rows = [left.shape[2] for left in lefts]
-    columns = [right.shape[1] for right in rights]
-    tokens = rights[0].shape[0]
+    rows = [left[0].shape[2] for left in lefts]
+    columns = [right[0].shape[1] for right in rights]
+    parts = len(rights[0])
+    tokens = parts * rights[0][0].shape[0]
     bf16 = jnp.bfloat16
     inside = pl.BlockSpec(memory_space=pltpu.VMEM)
+    stream_shape = (tokens, streams[0].shape[1])
+    operands, form = jax.tree.flatten(
+        (fronts, backs, head_parts, mod, bias, head_sums, mod_weight)
+    )
+    outer = len(operands) - heads - 4
     f32 = jnp.float32
     lines = members * mod.shape[0]
     results = pl.pallas_call(
-        functools.partial(reduce_kernel, length, count, heads),
+        functools.partial(reduce_kernel, length, form, count, heads),
         name="reduce",
         out_shape=[jax.ShapeDtypeStruct((r, c), bf16) for r, c in zip(rows, columns)]
         + [jax.ShapeDtypeStruct((h.shape[0] // 2, h.shape[1]), bf16) for h in head_parts]
-        + [jax.ShapeDtypeStruct(stream.shape, stream.dtype)]
+        + [jax.ShapeDtypeStruct(stream_shape, bf16)]
         + [
             jax.ShapeDtypeStruct((members,) + array.shape[1:], array.dtype)
             for array in (bias, head_sums)
@@ -911,16 +979,16 @@
             jax.ShapeDtypeStruct((lines, mod.shape[1]), f32),
             jax.ShapeDtypeStruct((2, members, lines, 128), f32),
         ],
-        in_specs=[ANY] * (2 * count) + [inside] * heads + [ANY] + [inside] * 4,
+        in_specs=[ANY] * outer + [inside] * (heads + 4),
         out_specs=[ANY] * (count + heads + 3) + [inside, ANY],
-        scratch_shapes=Ring.scratch(length, rows, columns, tokens)
+        scratch_shapes=Ring.scratch(length, rows, columns, tokens, parts)
         + [
             DMA((count,)),
             DMA((count,)),
             DMA((heads, 2)),
             DMA((heads,)),
-            DMA(()),
-            DMA(()),
+            DMA((parts,)),
+            DMA((parts,)),
             DMA((3, 2 * members)),
             DMA((members,)),
             DMA((members,)),
@@ -937,7 +1005,7 @@
             collective_id=collective_id, has_side_effects=True, vmem_limit_bytes=VMEM_BYTES
         ),
         cost_estimate=ring_cost(length, rows, columns, tokens),
-    )(*lefts, *rights, *head_parts, stream, mod, bias, head_sums, mod_weight)
+    )(*operands)
     return (results[:count], results[count : count + heads]) + tuple(results[count + heads :])
 
 
@@ -1011,16 +1079,30 @@
     return pl.BlockSpec((seq_len, columns), lambda i: (i, 0))
 
 
+def block_at(shape, index):
+    return pl.BlockSpec(shape, lambda i: index, pipeline_mode=pl.Buffered(1))
+
+
 def fixed_spec(shape):
-    zeros = (0,) * len(shape)
-    return pl.BlockSpec(shape, lambda i: zeros, pipeline_mode=pl.Buffered(1))
-
-
-def attend(hidden, pieces, pack_w, pack_b, out_w, out_b, members):
+    return block_at(shape, (0,) * len(shape))
+
+
+def image_rows(array, image):
+    if image is None:
+        return fixed_spec(array.shape)
+    return block_at((SEQ, array.shape[1]), (image if array.shape[0] > SEQ else 0, 0))
+
+
+def image_steps(array, image):
+    base = 0 if image is None or array.shape[0] <= SEQ else image
+    return pl.BlockSpec((SEQ, array.shape[1]), lambda i: (base + i, 0))
+
+
+def attend(hidden, pieces, pack_w, out_w, bias, members, image):
     tokens, channels = hidden.shape
     left = (members // 2, 2, channels // members)
-    images = pieces.shape[0]
-    seq = tokens // images
+    images, seq = tokens // SEQ, SEQ
+    lowest = image or 0
     bf16, f32 = jnp.bfloat16, jnp.float32
     work = tokens * channels * (4 * channels + 2 * seq)
     return pl.pallas_call(
@@ -1029,11 +1111,11 @@
         name="attend",
         in_specs=[
             rows_spec(seq, channels),
-            pl.BlockSpec((1,) + pieces.shape[1:], lambda i: (i, 0, 0)),
+            pl.BlockSpec((1,) + pieces.shape[1:], lambda i: (lowest + i, 0, 0)),
             fixed_spec(pack_w.shape),
-            fixed_spec(pack_b.shape),
+            block_at((1, 3 * channels), (0, 0)),
             fixed_spec(out_w.shape),
-            fixed_spec(out_b.shape),
+            block_at((1, channels), (0, 3)),
         ],
         out_specs=[
             pl.BlockSpec(left + (seq,), lambda i: (0, 0, 0, i)),
@@ -1056,7 +1138,7 @@
         cost_estimate=pl.CostEstimate(
             flops=2 * work, bytes_accessed=40 * 2**20, transcendentals=0
         ),
-    )(hidden, pieces, pack_w, pack_b, out_w, out_b)
+    )(hidden, pieces, pack_w, bias, out_w, bias)
 
 
 def per_image(values, images):
@@ -1104,7 +1186,7 @@
     return 1152 if width % 1152 == 0 else width
 
 
-def mlp(after, pieces, up_w, up_b, down_w, down_b, members):
+def mlp(after, pieces, up_w, down_w, bias, members, image):
     tokens, channels = after.shape
     width = up_w.shape[1]
     tile = feed_tile(width)
@@ -1119,11 +1201,11 @@
         name="mlp",
         in_specs=[
             fixed_spec(after.shape),
-            fixed_spec(pieces.shape),
+            block_at((tokens // SEQ,) + pieces.shape[1:], (image or 0, 0, 0)),
             pl.BlockSpec((channels, tile), lambda i: (0, i)),
-            pl.BlockSpec((1, tile), lambda i: (0, i)),
+            pl.BlockSpec((1, tile), lambda i: (0, 4 * channels // tile + i)),
             pl.BlockSpec((tile, channels), lambda i: (i, 0)),
-            fixed_spec(down_b.shape),
+            block_at((1, channels), (0, 4 + width // channels)),
         ],
         out_specs=[
             fixed_spec(left),
@@ -1144,7 +1226,7 @@
         cost_estimate=pl.CostEstimate(
             flops=4 * tokens * channels * width, bytes_accessed=40 * 2**20, transcendentals=0
         ),
-    )(after, pieces, up_w, up_b, down_w, down_b)
+    )(after, pieces, up_w, bias, down_w, bias)
 
 
 def sum_rows(values):
@@ -1159,8 +1241,16 @@
     )
 
 
+def added_grad(grad, extra, pieces):
+    return per_image(wide(grad[...]) + extra[...], pieces.shape[0])
+
+
+def scaled_grad(grad, extra, pieces):
+    return per_image(wide(grad[...]), pieces.shape[0]) * pieces[:, 6:7]
+
+
 def mlp_back_kernel(
-    grad, after, pieces, slope, mlp_out, attn_out, up_w, down_w,
+    given_grad, grad, extra, after, pieces, slope, mlp_out, attn_out, up_w, down_w,
     grad_mlp_out, grad_pre_out, grad_after_out, grad_attn_out, sums_out, pre_sums, out_sums,
     total,
 ):
@@ -1169,7 +1259,7 @@
 
     @pl.when(step == 0)
     def _():
-        given = per_image(grad[...], images)
+        given = given_grad(grad, extra, pieces)
         rows = narrow(pieces[:, 5:6] * given).reshape(grad.shape)
         grad_mlp_out[...] = rows
         sums_out[:, 5] = jnp.sum(given * per_image(wide(mlp_out[...]), images), 1)
@@ -1187,7 +1277,7 @@
         grad_min = per_image(total[...], images)
         sums_out[:, 3] = jnp.sum(grad_min, 1)
         sums_out[:, 4] = jnp.sum(grad_min * normed, 1)
-        grad_after = per_image(grad[...], images) + layer_norm_back(
+        grad_after = given_grad(grad, extra, pieces) + layer_norm_back(
             grad_min * (1.0 + pieces[:, 4:5]), normed, inverse
         )
         grad_after_out[...] = grad_after.reshape(grad.shape)
@@ -1197,25 +1287,26 @@
         out_sums[1] = sum_rows(rows)
 
 
-def mlp_back(grad, after, pieces, slope, mlp_out, attn_out, up_w, down_w):
-    tokens, channels = after.shape
-    images = pieces.shape[0]
-    width = up_w.shape[1]
+def mlp_back(given_grad, grad, extra, after, pieces, slope, mlp_out, attn_out, up_w, down_w, image):
+    tokens = after.shape[0] if image is None else SEQ
+    images, channels, width = tokens // SEQ, after.shape[1], up_w.shape[1]
     tile = feed_tile(width)
     bf16, f32 = jnp.bfloat16, jnp.float32
     columns = pl.BlockSpec((tokens, tile), lambda i: (0, i))
+    slope_row = image if image and slope.shape[0] > SEQ else 0
     rows = fixed_spec((tokens, channels))
     return pl.pallas_call(
-        mlp_back_kernel,
+        functools.partial(mlp_back_kernel, given_grad),
         grid=(width // tile,),
         name="mlp_back",
         in_specs=[
-            rows,
-            rows,
-            fixed_spec(pieces.shape),
-            columns,
-            rows,
-            rows,
+            image_rows(grad, image),
+            image_rows(extra, image),
+            image_rows(after, image),
+            block_at((images,) + pieces.shape[1:], (image or 0, 0, 0)),
+            pl.BlockSpec((tokens, tile), lambda i: (slope_row, i)),
+            image_rows(mlp_out, image),
+            image_rows(attn_out, image),
             pl.BlockSpec((channels, tile), lambda i: (0, i)),
             pl.BlockSpec((tile, channels), lambda i: (i, 0)),
         ],
@@ -1242,14 +1333,13 @@
         cost_estimate=pl.CostEstimate(
             flops=4 * tokens * channels * width, bytes_accessed=40 * 2**20, transcendentals=0
         ),
-    )(grad, after, pieces, slope, mlp_out, attn_out, up_w, down_w)
+    )(grad, extra, after, pieces, slope, mlp_out, attn_out, up_w, down_w)
 
 
 def attend_back_kernel(
     head_count, hidden, pieces, packed, probs_in, grad_attn, grad_after, pack_w, out_w,
     grad_packed_out, grad_hidden_out, sums_out, pack_sums, acc, grad_mixed_keep,
 ):
-    image = pl.program_id(0)
     channels = hidden.shape[1]
     head_size = channels // head_count
     scaling = head_size ** (-0.5)
@@ -1273,11 +1363,11 @@
     grad_packed_out[...] = grad_packed
     column_totals = sum_rows(grad_packed)
 
-    @pl.when(image == 0)
+    @pl.when(pl.program_id(0) == 0)
     def _():
         pack_sums[...] = column_totals
 
-    @pl.when(image > 0)
+    @pl.when(pl.program_id(0) > 0)
     def _():
         pack_sums[...] += column_totals
 
@@ -1290,30 +1380,30 @@
     )
 
 
-def attend_back(hidden, pieces, packed, probs, grad_attn, grad_after, pack_w, out_w):
-    tokens, channels = hidden.shape
-    images = pieces.shape[0]
-    seq = tokens // images
+def attend_back(hidden, pieces, packed, probs, grad_attn, grad_after, pack_w, out_w, image):
+    tokens = hidden.shape[0] if image is None else SEQ
+    images, channels, seq = tokens // SEQ, hidden.shape[1], SEQ
+    lowest = image or 0
+    probs_at = lowest if probs.shape[0] > 1 else 0
     bf16, f32 = jnp.bfloat16, jnp.float32
     work = tokens * channels * (4 * channels + 5 * seq)
-    rows = rows_spec(seq, channels)
     return pl.pallas_call(
         functools.partial(attend_back_kernel, HEADS),
         grid=(images,),
         name="attend_back",
         in_specs=[
-            rows,
-            pl.BlockSpec((1,) + pieces.shape[1:], lambda i: (i, 0, 0)),
-            rows_spec(seq, 3 * channels),
-            pl.BlockSpec((1, HEADS, seq, seq), lambda i: (i, 0, 0, 0)),
-            rows,
-            rows,
+            image_steps(hidden, image),
+            pl.BlockSpec((1,) + pieces.shape[1:], lambda i: (lowest + i, 0, 0)),
+            image_steps(packed, image),
+            pl.BlockSpec((1, HEADS, seq, seq), lambda i: (probs_at + i, 0, 0, 0)),
+            image_steps(grad_attn, image),
+            image_steps(grad_after, image),
             fixed_spec(pack_w.shape),
             fixed_spec(out_w.shape),
         ],
         out_specs=[
             rows_spec(seq, 3 * channels),
-            rows,
+            rows_spec(seq, channels),
             pl.BlockSpec((1, 8, channels), lambda i: (i, 0, 0)),
             fixed_spec((8, 3 * channels)),
         ],
@@ -1334,13 +1424,13 @@
     )(hidden, pieces, packed, probs, grad_attn, grad_after, pack_w, out_w)
 
 
-def block_forward(hidden, pieces, weights, members):
-    pack_w, pack_b, out_w, out_b, up_w, up_b, down_w, down_b = weights
+def block_forward(hidden, pieces, weights, members, image=None):
+    pack_w, out_w, up_w, down_w, bias = weights
     input_left, packed, probs, mixed_left, attn_out, after = attend(
-        hidden, pieces, pack_w, pack_b, out_w, out_b, members
+        hidden, pieces, pack_w, out_w, bias, members, image
     )
     rows_left, act_left, slope, mlp_out, final = mlp(
-        after, pieces, up_w, up_b, down_w, down_b, members
+        after, pieces, up_w, down_w, bias, members, image
     )
     return (
         final,
@@ -1349,27 +1439,17 @@
     )
 
 
-def block_backward(hidden, saved_state, pieces, weights, grad):
-    pack_w, pack_b, out_w, out_b, up_w, up_b, down_w, down_b = weights
+def block_backward(hidden, saved_state, pieces, weights, given_grad, grad, extra, image):
+    pack_w, out_w, up_w, down_w, _ = weights
     packed, probs, attn_out, after, slope, mlp_out = saved_state
     grad_mlp, grad_pre, grad_after, grad_attn, high_sums, pre_sums, out_sums = mlp_back(
-        grad, after, pieces, slope, mlp_out, attn_out, up_w, down_w
+        given_grad, grad, extra, after, pieces, slope, mlp_out, attn_out, up_w, down_w, image
     )
     grad_packed, grad_hidden, low_sums, pack_sums = attend_back(
-        hidden, pieces, packed, probs, grad_attn, grad_after, pack_w, out_w
-    )
-    images, channels = pieces.shape[0], hidden.shape[1]
-    grad_mod = narrow(
-        jnp.concatenate([low_sums[:, 0:2], high_sums[:, 2:6]], 1).reshape(images, 6 * channels)
-    )
-    pack_row = pack_sums[0:1]
-    bias_grads = (
-        jnp.concatenate([pack_row[:, :channels], pack_row[:, 2 * channels :]], 1),
-        out_sums[1, 0:1],
-        pre_sums[0:1],
-        out_sums[0, 0:1],
-    )
-    return grad_hidden, (grad_mlp, grad_pre, grad_attn, grad_packed), bias_grads, grad_mod
+        hidden, pieces, packed, probs, grad_attn, grad_after, pack_w, out_w, image
+    )
+    rights = (grad_mlp, grad_pre, grad_attn, grad_packed)
+    return grad_hidden, rights, (low_sums, high_sums, pack_sums, pre_sums, out_sums)
 
 
 def silu_parts(values):
@@ -1590,16 +1670,16 @@
     mod_part = (mod_part + bias_row[None]).reshape(members, images, 6 * channels)
 
     section_biases = (qv_bias[0], attn_bias[0], up_bias[0], down_bias[0])
-    head_biases = (project_in_bias, project_mid_bias, project_out_bias)
-    parts = section_biases + head_biases
-    widths = [part.shape[0] for part in parts]
-    lanes = 16 * 128
-    packed_bias = jnp.concatenate(
-        list(parts) + [jnp.zeros((lanes - sum(widths),), jnp.bfloat16)]
-    ).reshape(16, 128)
-    block_full, head_full, mod_all, rows_in = gather(
+    biases = section_biases + (project_in_bias, project_mid_bias, project_out_bias)
+    widths = [part.shape[0] for part in biases]
+    lines = [
+        jnp.pad(part, (0, -part.shape[0] % 128)).reshape(-1, 128) for part in biases
+    ]
+    bias_block = jnp.concatenate(lines)
+    bias_block = jnp.pad(bias_block, ((0, -bias_block.shape[0] % 16), (0, 0)))
+    block_full, head_full, mod_all, rows_in, block_bias, head_bias = gather(
         (
-            packed_bias,
+            bias_block,
             qkv_weight[0],
             attn_weight[0],
             up_weight[0],
@@ -1610,38 +1690,32 @@
         mod_part,
         tokens_in,
         cotangent,
+        widths,
         0,
     )
-    all_bias, pack_weight, out_weight, first_weight, second_weight, head_last = block_full
-    all_bias = all_bias.reshape(members, lanes)
-    biases, offset = [], 0
-    for width in widths:
-        biases.append(wide(all_bias[:, offset : offset + width].reshape(-1)))
-        offset += width
-    pack_full = jnp.concatenate(
-        [biases[0][:channels], jnp.zeros((channels,), jnp.float32), biases[0][channels:]]
-    )
+    _, pack_weight, out_weight, first_weight, second_weight, head_last = block_full
+    head_ends = [members * width for width in widths[4:]]
+    head_bias = [
+        head_bias[0, sum(head_ends[:i]) : sum(head_ends[: i + 1])] for i in range(len(head_ends))
+    ]
 
     def whole(values):
         return values.reshape(-1, values.shape[-1])
 
     block_weights = (
         whole(pack_weight),
-        pack_full[None],
         whole(out_weight),
-        biases[1][None],
         whole(first_weight),
-        biases[2][None],
         whole(second_weight),
-        biases[3][None],
+        block_bias,
     )
     head_weights = (
         whole(head_full[0]),
-        biases[4],
+        head_bias[0],
         whole(head_full[1]),
-        biases[5],
+        head_bias[1],
         whole(head_last),
-        biases[6],
+        head_bias[2],
     )
     pieces = jnp.sum(mod_all, 0).reshape(images, 6, channels)
 
@@ -1674,60 +1748,82 @@
     )
     hidden_second = lax.ppermute(first_out, axes, pairs_up)
 
-    def do_second(second, mod, grad, live, block):
-        final, state, lefts = forward(second, mod, block)
-        outer_grad = wide(grad) * live[:, None]
-        grad_input, rights, bias_grads, grad_mod = block_backward(
-            second, state, mod, block, outer_grad
-        )
-        return grad_input, final, rights, bias_grads, grad_mod, lefts
-
     head_result = head_pass(first_out, own_targets, token_live, head_weights, members)
-    head_lefts, head_rights = head_result[2:4]
-    head_parts = head_reduce(head_lefts, head_rights + (first_out,), 2)
-    hidden_second, head_result, head_parts = lax.optimization_barrier(
-        (hidden_second, head_result, head_parts)
-    )
+    hidden_second, head_result = lax.optimization_barrier((hidden_second, head_result))
     grad_hidden, loss_part, head_lefts, head_rights, head_sums = head_result
-    second_result = lax.cond(
+
+    def do_second(rows, mod, grad, block):
+        final, state, lefts = block_forward(rows, mod, block, members)
+        grad_rows, rights, sums_of = block_backward(
+            rows, state, mod, block, scaled_grad, grad, grad, None
+        )
+        cut = tuple(grad_rows[i * SEQ : (i + 1) * SEQ] for i in range(images))
+        return cut, final, rights, sums_of, lefts
+
+    second = lax.cond(
         is_first,
         lambda *operands_in: unused(do_second, *operands_in),
         do_second,
         hidden_second,
         pieces,
         outer,
-        token_live,
         block_weights,
     )
-    send_back = second_result[0]
-    arrived_back = lax.ppermute(send_back, axes, pairs_back)
-    lefts = lax.cond(
-        is_first,
-        lambda one, other: one,
-        lambda one, other: other,
-        first_lefts,
-        second_result[-1],
-    )
-    arrived_back, lefts = lax.optimization_barrier((arrived_back, lefts))
-
-    def do_first(hidden, state, mod, extra, back_grad, block, other):
-        return block_backward(hidden, state, mod, block, wide(back_grad) + extra)
-
-    def keep_second(hidden, state, mod, extra, back_grad, block, other):
-        return other
-
-    stream, rights, bias_grads, grad_mod = lax.cond(
-        is_first,
-        do_first,
-        keep_second,
-        hidden_first,
-        saved_state,
-        pieces,
-        grad_hidden,
-        arrived_back,
-        block_weights,
-        second_result[1:-1],
-    )
+    returning = [lax.ppermute(rows, axes, pairs_back) for rows in second[0]]
+    head_lefts, head_rights, kept = lax.optimization_barrier((head_lefts, head_rights, second[1]))
+    second = (second[0], kept) + second[2:]
+    head_parts = head_reduce(head_lefts, head_rights + (first_out,), 2)
+    returning[0], head_parts = lax.optimization_barrier((returning[0], head_parts))
+    first = []
+    for i in range(images):
+
+        def do_first(rows, state, mod, extra, grad, block, i=i):
+            return block_backward(rows, state, mod, block, added_grad, grad, extra, i)
+
+        if i:
+            returning[i], gone = lax.optimization_barrier((returning[i], first[i - 1][0]))
+            first[i - 1] = (gone,) + first[i - 1][1:]
+        first.append(
+            lax.cond(
+                is_first,
+                do_first,
+                lambda *operands_in: unused(do_first, *operands_in),
+                hidden_first,
+                saved_state,
+                pieces,
+                grad_hidden,
+                returning[i],
+                block_weights,
+            )
+        )
+    sums_first = [result[2] for result in first]
+    low_sums, high_sums = (
+        jnp.where(is_first, jnp.concatenate([sums_of[j] for sums_of in sums_first]), second[3][j])
+        for j in range(2)
+    )
+    pack_row, pre_row, out_rows = (
+        jnp.where(is_first, sum(sums_of[j] for sums_of in sums_first), second[3][j])[..., 0:1, :]
+        for j in range(2, 5)
+    )
+    grad_mod = narrow(
+        jnp.concatenate([low_sums[:, 0:2], high_sums[:, 2:6]], 1).reshape(images, 6 * channels)
+    )
+    bias_grads = (
+        jnp.concatenate([pack_row[:, :channels], pack_row[:, 2 * channels :]], 1),
+        out_rows[1],
+        pre_row,
+        out_rows[0],
+    )
+
+    def by_layer(results):
+        return [list(parts_of) for parts_of in zip(*results)]
+
+    fronts = (
+        [[left] for left in first_lefts],
+        by_layer([result[1] for result in first]),
+        [result[0] for result in first],
+    )
+    backs = ([[left] for left in second[4]], [[right] for right in second[2]], [second[1]])
     bias_rows = jnp.concatenate([grads.reshape(members, -1) for grads in bias_grads], 1)
     bias_width = bias_rows.shape[1]
     bias_rows = jnp.pad(bias_rows, ((0, 0), (0, 1024 - bias_width))).reshape(members, 8, 128)
@@ -1746,10 +1842,9 @@
     head_width = head_rows.shape[1]
     head_rows = jnp.pad(head_rows, ((0, 0), (0, 1024 - head_width))).reshape(devices, 8, 128)
     block_grads, head_grads, stream_in, bias_all, head_all, mod_wide, silu_all_terms = reduce(
-        lefts,
-        rights,
+        fronts,
+        backs,
         head_parts,
-        stream,
         grad_mod,
         bias_rows,
         head_rows,
@@ -1757,6 +1852,7 @@
         3,
     )
     down_grad, up_grad, attn_grad, qkv_grad = block_grads
+    stream = jnp.where(is_first, jnp.concatenate(fronts[2]), jnp.concatenate(backs[2]))
     stream_own = jnp.where(crossed, stream_in, stream)
     mod_w_grad = product_left_t(silu_depth, narrow(mod_wide))
     mod_b_grad = lax.dynamic_slice_in_dim(jnp.sum(mod_wide, 0), index * share, share, 0)

time: 759 us -> 738 us (0.972)
  Pallas kernels: 605 us -> 616 us
  local copies, waits for them, and re-layouts: 37.9 us -> 27.5 us
    ppermute x1 -> x2, waiting for transfers between devices: 16.5 us -> 13.9 us  [on_device(): returning = [lax.ppermute(rows, axes, pairs_back) for rows in second[0]]]
  transfers between devices with their start and end apart: 3 -> 4, of which waited for: 2 -> 3; matrix products, arithmetic and copies ran while one was open for 5% -> 3% of each run, Pallas kernels for 1% -> 1%
where the time goes in v4:
time: 738 us; the launch traced here: 732 us
  Pallas kernels  616 us (83%)
  other arithmetic  30.3 us (4%)
  local copies, waits for them, and re-layouts  27.5 us (4%)
  waiting for transfers between devices  19.9 us (3%)
  blocking collectives  13.6 us (2%)
  matrix products  11.9 us (2%)
  starting transfers between devices  7.72 us (1%)
    pallas_call x1, Pallas kernels, gather(): pl.pallas_call(functools.partial(gather_kernel, length, count, heads, wid...  253 us
    pallas_call x1, Pallas kernels, reduce(): pl.pallas_call(functools.partial(reduce_kernel, length, form, count, head...  252 us
    pallas_call x1, Pallas kernels, mlp_back(): pl.pallas_call(functools.partial(mlp_back_kernel, given_grad), grid=(widt...  30.2 us
    pallas_call x1, Pallas kernels, attend_back(): pl.pallas_call(functools.partial(attend_back_kernel, HEADS), grid=(images...  26.7 us
    pallas_call x1, Pallas kernels, mlp(): pl.pallas_call(mlp_kernel, grid=(width // tile,), name='mlp', in_specs=[f...  25 us
    pallas_call x1, Pallas kernels, attend(): pl.pallas_call(functools.partial(attend_kernel, HEADS), grid=(images,), n...  18.9 us
  transfers between devices with their start and end apart: 4, of which 3 were waited for; matrix products, arithmetic and copies ran while one was open for 3% of the time, Pallas kernels for 1%

profile of v4, /device:TPU:10, one launch (start us, length us, event | category | flops | bytes accessed | tf_op | source)
XLA Modules:
  0.0 732.1 jit_solution(11004559326315122818)
XLA Ops:
  2.8 1.2 dynamic-slice
  5.5 13.6 %all-reduce.8 = s32[32]{0:T(128)S(1)} all-reduce(s32[32]{0:T(128)S(1)} %dynamic-update-slice), channel_id=1, replica_groups=mesh['section'=2,'dp'=16] {'dp'}, use_global_device_ids=true, to_apply=%add.8 | all-reduce | flops 32 | bytes 256
  19.8 4.1 add_divide_fusion
  25.1 1.4 reshape.138.refs_8_
  27.3 252.6 %gather.1 = (bf16[16,16,128]{2,1,0:T(8,128)(2,1)}, bf16[16,72,3456]{2,1,0:T(8,128)(2,1)}, bf16[16,72,1152]{2,1,0:T(8,128)(2,1)}, bf16[16,72,4608]{2,1,0:T(8,128)...) custom-call(bf16[16,128]{1,0:T(8,128)(2,1)} %pad.36.refs_0_, ...), custom_call_target="tpu_custom_call" | custom-call | bytes 770703360 | tf_op jit(solution)/shard_map/gather/pallas_call | solution.py:452
  279.9 2.2 collective-permute-start.1
  286.6 1.3 collective-permute-start
  289.3 1.2 slice.91.out_b
  291.2 1.3 fusion.22
  292.5 2.1 broadcast_select_fusion.2.target_at
  295.5 9.7 %head.1 = (f32[512,1152]{1,0:T(8,128)}, bf16[8,2,128,512]{3,2,1,0:T(8,128)(2,1)}, bf16[8,2,128,512]{3,2,1,0:T(8,128)(2,1)}, bf16[8,2,128,512]{3,2,1,0:T(8,128)(2...) custom-call(bf16[512,1152]{1,0:T(8,128)(2,1)} %get-tuple-element.331, ...), custom_call_target="tpu_custom_call" | custom-call | flops 16642998272 | bytes 41943040 | tf_op jit(solution)/shard_map/head/pallas_call | solution.py:1578
  306.4 1.4 slice.93
  307.8 1.4 slice.94
  309.3 1.3 slice.95
  310.6 6.0 collective-permute-done
  316.6 106.1 %conditional.5 = ((bf16[256,1152]{1,0:T(8,128)(2,1)}, bf16[256,1152]{1,0:T(8,128)(2,1)}, bf16[512,1152]{1,0:T(8,128)(2,1)}, bf16[512,1152]{1,0:T(8,128)(2,1)}, b...) conditional(s32[]{:T(128)} %convert_element_type.54, ...), branch_computations={%region_3.4_spmd, %region_4.5_spmd} | conditional | flops 34729426944 | bytes 173670528 | solution.py:1763
  316.6 18.9 %attend.3 = (bf16[8,2,72,512]{3,2,1,0:T(8,128)(2,1)}, bf16[512,3456]{1,0:T(8,128)(2,1)}, bf16[2,16,256,256]{3,2,1,0:T(8,128)(2,1)}, bf16[8,2,72,512]{3,2,1,0:T(8...) custom-call(bf16[512,1152]{1,0:T(8,128)(2,1)} %get-tuple-element.110.hidden, ...), custom_call_target="tpu_custom_call" | custom-call | flops 6039797760 | bytes 41943040 | tf_op jit(solution)/shard_map/cond/branch_0_fun/attend/pallas_call | solution.py:1108
  335.5 2.4 broadcast_select_fusion.grad.extra
  337.9 25.0 %mlp.3 = (bf16[8,2,72,512]{3,2,1,0:T(8,128)(2,1)}, bf16[8,2,288,512]{3,2,1,0:T(8,128)(2,1)}, bf16[512,4608]{1,0:T(8,128)(2,1)}, bf16[512,1152]{1,0:T(8,128)(2,1)}, bf16[512,1152]{1,0:T(8,128)(2,1)}) custom-call(f32[512,1152]{1,0:T(8,128)} %get-tuple-element.120.after, f32[2,8,1152]{2,1,0:T(8,128)S(1)} %get-tuple-element.111.pieces, ...), custom_call_target="tpu_custom_call" | custom-call | flops 10871635968 | bytes 41943040 | tf_op jit(solution)/shard_map/cond/branch_0_fun/mlp/pallas_call | solution.py:1198
  362.9 30.2 %mlp_back.3 = (bf16[512,1152]{1,0:T(8,128)(2,1)}, bf16[512,4608]{1,0:T(8,128)(2,1)}, f32[512,1152]{1,0:T(8,128)}, bf16[512,1152]{1,0:T(8,128)(2,1)}, f32[2,8,115...) custom-call(bf16[512,1152]{1,0:T(8,128)(2,1)} %broadcast_select_fusion.grad.extra, ...), custom_call_target="tpu_custom_call" | custom-call | flops 10871635968 | bytes 41943040 | tf_op jit(solution)/shard_map/cond/branch_0_fun/mlp_back/pallas_call | solution.py:1298
  393.2 26.7 %attend_back.3 = (bf16[512,3456]{1,0:T(8,128)(2,1)}, bf16[512,1152]{1,0:T(8,128)(2,1)}, f32[2,8,1152]{2,1,0:T(8,128)}, f32[8,3456]{1,0:T(8,128)}) custom-call(bf16[512,1152]{1,0:T(8,128)(2,1)} %get-tuple-element.110.hidden, f32[2,8,1152]{2,1,0:T(8,128)S(1)} %get-tuple-element.111.pieces, bf16[512,3456]{1,0:T(8,128)(2,1)} %get-tuple-element.115.packed, ...), custom_call_target="tpu_custom_call" | custom-call | flops 6945767424 | bytes 41943040 | tf_op jit(solution)/shard_map/cond/branch_0_fun/attend_back/pallas_call | solution.py:1390
  419.9 2.3 fusion.20
  422.7 2.1 collective-permute-start.2
  424.8 2.1 collective-permute-start.3
  427.4 1.4 reduce.18
  429.5 1.4 reduce.19
  434.9 3.2 collective-permute-done.2
  438.2 10.7 %collective-permute-done.3 = bf16[256,1152]{1,0:T(8,128)(2,1)} collective-permute-done((bf16[256,1152]{1,0:T(8,128)(2,1)}, bf16[256,1152]{1,0:T(8,128)(2,1)}, u32[]{:S(2)}, u32[]{:S(2)}) %collective-permute-start.3) | collective-permute-done | bytes 589856 | tf_op jit(solution)/shard_map/ppermute | solution.py:1772
  456.1 252.1 %reduce.20 = (bf16[288,1152]{1,0:T(8,128)(2,1)}, bf16[72,4608]{1,0:T(8,128)(2,1)}, bf16[72,1152]{1,0:T(8,128)(2,1)}, bf16[72,3456]{1,0:T(8,128)(2,1)}, bf16[64,7...) custom-call(bf16[8,2,288,512]{3,2,1,0:T(8,128)(2,1)} %get-tuple-elem, ...), custom_call_target="tpu_custom_call" | custom-call | flops 16307453952 | bytes 509607936 | tf_op jit(solution)/shard_map/reduce/pallas_call | solution.py:968
  708.2 3.0 convolution_bitcast_fusion
  714.3 2.7 fusion.1
  718.0 4.4 fusion.5
  (138 shorter events, 37.3 us)
Async XLA Ops:
  19.1 4.8 copy-start.23
  19.8 5.0 copy-start.10
  23.9 0.7 copy-start.13
  25.1 1.5 copy-start.27
  25.1 1.5 copy-start.28
  25.1 1.5 copy-start.25
  25.1 1.5 copy-start.26
  25.1 2.1 copy-start.1
  27.3 256.0 %copy-start = (bf16[512,1152]{1,0:T(8,128)(2,1)S(1)}, bf16[512,1152]{1,0:T(8,128)(2,1)}, u32[]{:S(2)}) copy-start(bf16[512,1152]{1,0:T(8,128)(2,1)} %refs_9_.1) | copy-start | bytes 3538948
  279.9 4.6 copy-start.2
  279.9 12.6 %collective-permute-start.1 = (bf16[512,768]{1,0:T(8,128)(2,1)}, bf16[512,768]{1,0:T(8,128)(2,1)}, u32[]{:S(2)}, u32[]{:S(2)}) collective-permute-start(bf16[512,768]{1,0:T(8,128)(2,1)} %param.32), channel_id=1, source_target_pairs={{1,16},{3,18},{5,20},{7,22},{9,24},{11,26},{13,28},{15,30}} | collective-permute-start | bytes 2359304 | tf_op jit(solution)/shard_map/ppermute | solution.py:1733
  283.3 1.2 copy-start.31
  286.6 30.0 %collective-permute-start = (bf16[512,1152]{1,0:T(8,128)(2,1)}, bf16[512,1152]{1,0:T(8,128)(2,1)}, u32[]{:S(2)}, u32[]{:S(2)}) collective-permute-start(bf16[512,1152]{1,0:T(8,128)(2,1)} %get-tuple-element.331.hidden_at.refs_5_), channel_id=1, source_target_pairs={{0,1},{16,17},{2,3},{18,19},{4,5},{20,21},{6,7},{22,23},{8,9},{24,... | collective-permute-start | bytes 3538952 | tf_op jit(solution)/shard_map/ppermute | solution.py:1749
  295.5 21.1 %copy-start.4 = (f32[2,8,1152]{2,1,0:T(8,128)S(1)}, f32[2,8,1152]{2,1,0:T(8,128)}, u32[]{:S(2)}) copy-start(f32[2,8,1152]{2,1,0:T(8,128)} %pad_maximum_fusion) | copy-start | bytes 221188
  295.5 21.1 %copy-start.29 = (f32[1,10368]{1,0:T(1,128)S(1)}, f32[1,10368]{1,0:T(1,128)}, u32[]{:S(2)}) copy-start(f32[1,10368]{1,0:T(1,128)} %get-tuple-element.323) | copy-start | bytes 124420
  422.7 15.4 %collective-permute-start.2 = (bf16[256,1152]{1,0:T(8,128)(2,1)}, bf16[256,1152]{1,0:T(8,128)(2,1)}, u32[]{:S(2)}, u32[]{:S(2)}) collective-permute-start(bf16[256,1152]{1,0:T(8,128)(2,1)} %get-tuple-element.348), channel_id=1, source_target_pairs={{1,0},{17,16},{3,2},{19,18},{5,4},{21,20},{7,6},{23,22},{9,8},{25,... | collective-permute-start | bytes 1769480 | tf_op jit(solution)/shard_map/ppermute | solution.py:1772
  424.8 24.2 %collective-permute-start.3 = (bf16[256,1152]{1,0:T(8,128)(2,1)}, bf16[256,1152]{1,0:T(8,128)(2,1)}, u32[]{:S(2)}, u32[]{:S(2)}) collective-permute-start(bf16[256,1152]{1,0:T(8,128)(2,1)} %get-tuple-element.372), channel_id=1, source_target_pairs={{1,0},{17,16},{3,2},{19,18},{5,4},{21,20},{7,6},{23,22},{9,8},{25,... | collective-permute-start | bytes 1769480 | tf_op jit(solution)/shard_map/ppermute | solution.py:1772
  449.1 6.9 copy-start.9
  708.2 3.1 copy-start.3
  708.2 3.2 copy-start.22
  708.2 4.4 copy-start.21
  708.2 6.1 copy-start.8
  714.3 2.7 copy-start.15
  717.0 0.9 copy-start.14
  717.0 0.9 copy-start.24
  718.0 5.1 copy-start.16
  722.4 1.7 copy-start.18
  722.4 2.4 copy-start.12
  724.1 2.5 copy-start.11
  726.0 1.7 copy-start.19
  726.0 2.5 copy-start.17
  726.6 2.7 copy-start.20

commit v5 on v4

--- a/solution.py
+++ b/solution.py
@@ -593,10 +593,12 @@
             else:
                 pl.when(predicate)(body)
 
-    def run(self, finish, midway=None, late=None):
+    def run(self, finish, early=None, midway=None, late=None):
         length = self.length
         for layer in self.layers:
             self.fetch(layer, lambda copy: copy.start())
+        if early:
+            early()
         for layer in self.layers:
             self.fetch(layer, lambda copy: copy.wait())
             self.chunk(layer, 0, 0, False)
@@ -678,17 +680,16 @@
     )(*lefts, *rights)
 
 
-def reduce_kernel(length, form, count, heads, *refs):
+def reduce_kernel(length, form, count, heads, widths, *refs):
     operands = form.num_leaves
-    fronts, backs, head_parts, mod, bias, head_sums, mod_weight = jax.tree.unflatten(
-        form, refs[:operands]
-    )
+    fronts, backs, head_parts, head_sums, mod_weight = jax.tree.unflatten(form, refs[:operands])
     refs = refs[operands:]
     outs, head_outs = refs[:count], refs[count : count + heads]
     stream_out, bias_all, head_all, mod_rows, silu_all = refs[count + heads : count + heads + 5]
     scratch = refs[count + heads + 5 :]
     mod_all, silu_own, silu_keep, silu_send, silu_recv, silu_side = scratch[-6:]
-    scratch = scratch[:-6]
+    mod, bias, bias_line = scratch[-9:-6]
+    scratch = scratch[:-9]
     (
         last_send, last_recv, part_send, part_recv, stream_send, stream_recv, small_send,
         mod_recv, bias_recv, head_recv, keep_sem,
@@ -787,7 +788,43 @@
     def start(copy):
         copy.start()
 
-    smalls(start, start, start)
+    def gather_sums(entries):
+        lows = [low[i] for low, *_ in entries for i in range(low.shape[0])]
+        highs = [high[i] for _, high, *_ in entries for i in range(high.shape[0])]
+        channels = lows[0].shape[1]
+        for piece in range(6):
+            rows = [v[piece : piece + 1] for v in (lows if piece < 2 else highs)]
+            mod[:, piece * channels : (piece + 1) * channels] = narrow(jnp.concatenate(rows, 0))
+
+        def total(read):
+            return sum(read(entry) for entry in entries)
+
+        wide_pre = entries[0][3].shape[1]
+        bias_line[:, 0:channels] = total(lambda e: e[2][0:1, 0:channels])
+        bias_line[:, channels : 2 * channels] = total(lambda e: e[2][0:1, 2 * channels :])
+        bias_line[:, 2 * channels : 3 * channels] = total(lambda e: e[4][1, 0:1])
+        bias_line[:, 3 * channels : 3 * channels + wide_pre] = total(lambda e: e[3][0:1])
+        bias_line[:, 3 * channels + wide_pre :] = total(lambda e: e[4][0, 0:1])
+
+    def early():
+        @pl.when(role == 0)
+        def _():
+            gather_sums(fronts[3])
+
+        @pl.when(role == 1)
+        def _():
+            gather_sums(backs[3])
+
+        for shard in range(members):
+            line, start_at = 0, 0
+            for width in widths:
+                for offset in range(0, width, 128):
+                    size = min(128, width - offset)
+                    first = start_at + shard * width + offset
+                    bias[shard, line : line + 1, 0:size] = bias_line[:, first : first + size]
+                    line += 1
+                start_at += members * width
+        smalls(start, start, start)
 
     def part(layer, half):
         rows = head_outs[layer].shape[0]
@@ -888,7 +925,7 @@
         silu_kept.wait()
         across.start()
 
-    ring.run(finish, midway, late)
+    ring.run(finish, early, midway, late)
     others(lambda peer: silu_copy(peer).wait_send())
     across.wait_send()
     remote(
@@ -948,9 +985,9 @@
             remote_last(layer, slot).wait()
 
 
-def reduce(fronts, backs, head_parts, mod, bias, head_sums, mod_weight, collective_id):
+def reduce(fronts, backs, head_parts, head_sums, mod_weight, widths, collective_id):
     members = lax.axis_size("dp")
-    lefts, rights, streams = fronts
+    lefts, rights, streams, image_sums = fronts
     length, count, heads = members // 2, len(lefts), len(head_parts)
     rows = [left[0].shape[2] for left in lefts]
     columns = [right[0].shape[1] for right in rights]
@@ -959,27 +996,33 @@
     bf16 = jnp.bfloat16
     inside = pl.BlockSpec(memory_space=pltpu.VMEM)
     stream_shape = (tokens, streams[0].shape[1])
-    operands, form = jax.tree.flatten(
-        (fronts, backs, head_parts, mod, bias, head_sums, mod_weight)
-    )
-    outer = len(operands) - heads - 4
+    operands, form = jax.tree.flatten((fronts, backs, head_parts, head_sums, mod_weight))
+
+    def side_specs(side):
+        return jax.tree.map(lambda _: ANY, side[:3]) + (jax.tree.map(lambda _: inside, side[3]),)
+
+    specs = side_specs(fronts) + side_specs(backs)
+    specs = jax.tree.leaves(specs, is_leaf=lambda leaf: isinstance(leaf, pl.BlockSpec))
+    images = sum(sums_of[0].shape[0] for sums_of in image_sums)
+    mod_shape = (images, 6 * image_sums[0][0].shape[2])
+    bias_shape = (members, 8, 128)
     f32 = jnp.float32
-    lines = members * mod.shape[0]
+    lines = members * images
     results = pl.pallas_call(
-        functools.partial(reduce_kernel, length, form, count, heads),
+        functools.partial(reduce_kernel, length, form, count, heads, widths),
         name="reduce",
         out_shape=[jax.ShapeDtypeStruct((r, c), bf16) for r, c in zip(rows, columns)]
         + [jax.ShapeDtypeStruct((h.shape[0] // 2, h.shape[1]), bf16) for h in head_parts]
         + [jax.ShapeDtypeStruct(stream_shape, bf16)]
         + [
-            jax.ShapeDtypeStruct((members,) + array.shape[1:], array.dtype)
-            for array in (bias, head_sums)
+            jax.ShapeDtypeStruct(bias_shape, f32),
+            jax.ShapeDtypeStruct((members,) + head_sums.shape[1:], f32),
         ]
         + [
-            jax.ShapeDtypeStruct((lines, mod.shape[1]), f32),
+            jax.ShapeDtypeStruct((lines, mod_shape[1]), f32),
             jax.ShapeDtypeStruct((2, members, lines, 128), f32),
         ],
-        in_specs=[ANY] * outer + [inside] * (heads + 4),
+        in_specs=specs + [inside] * (heads + 2),
         out_specs=[ANY] * (count + heads + 3) + [inside, ANY],
         scratch_shapes=Ring.scratch(length, rows, columns, tokens, parts)
         + [
@@ -994,7 +1037,10 @@
             DMA((members,)),
             DMA((members,)),
             DMA((3,)),
-            pltpu.VMEM((members,) + mod.shape, mod.dtype),
+            pltpu.VMEM(mod_shape, bf16),
+            pltpu.VMEM(bias_shape, f32),
+            pltpu.VMEM((1, members * sum(widths)), f32),
+            pltpu.VMEM((members,) + mod_shape, bf16),
             pltpu.VMEM((lines, 128), f32),
             DMA(()),
             DMA((members,)),
@@ -1460,10 +1506,11 @@
 def head_kernel(
     members, hidden_at, target_at, live, in_w_at, in_b, mid_w_at, mid_b, out_w_at, out_b,
     grad_hidden_at, last_left_at, mid_left_at, in_left_at, grad_feature_at, grad_second_at,
-    in_sums, mid_sums, out_sums, loss_out,
+    device_rows,
     hidden, target, in_w, mid_w, out_w,
     grad_hidden_out, last_left, mid_left, in_left, grad_feature_out, grad_second_out,
-    act_first, slope_first, act_second, slope_second, grad_first_keep, come_sem, go_sem,
+    act_first, slope_first, act_second, slope_second, grad_first_keep, in_sums, mid_sums,
+    come_sem, go_sem,
 ):
     width = in_w.shape[1]
     tile = 512 if width % 512 == 0 else width
@@ -1520,16 +1567,14 @@
         aim = aim * lax.rsqrt(jnp.sum(aim * aim, -1, keepdims=True) + EPSILON)
         alive = live[:, 0:1]
         cosine = jnp.sum(unit * aim, -1, keepdims=True)
-        loss_out[...] = jnp.broadcast_to(
-            0.5 * jnp.sum(alive * (1.0 - cosine), axis=(0, 1), keepdims=True), loss_out.shape
-        )
+        loss = 0.5 * jnp.sum(alive * (1.0 - cosine), axis=(0, 1), keepdims=True)
         grad_unit = (-0.5 * alive) * aim
         grad_feature = narrow(
             inverse * (grad_unit - unit * jnp.sum(grad_unit * unit, -1, keepdims=True))
         )
         grad_feature_out[...] = grad_feature
         go[4].start()
-        out_sums[...] = sum_rows(grad_feature)
+        out_sums = sum_rows(grad_feature)
         for at in tiles:
             grad_second = narrow(
                 wide(slope_second[:, at]) * product_right_t(grad_feature, out_w[at, :])
@@ -1553,6 +1598,18 @@
             lay(in_left, grad_first_keep[:, at], at.start)
         go[0].start()
         go[3].start()
+        share, devices = width // (2 * members), 2 * members
+        device_rows[...] = jnp.zeros_like(device_rows)
+        for device in range(devices):
+            lanes = slice(device * share, (device + 1) * share)
+            device_rows[device, 0:1, 0:share] = in_sums[0:1, lanes]
+            device_rows[device, 0:1, share : 2 * share] = mid_sums[0:1, lanes]
+        count = out_sums.shape[1] // 128
+        for line in range(count):
+            device_rows[:, 1 + line, :] = jnp.broadcast_to(
+                out_sums[0:1, line * 128 : (line + 1) * 128], (devices, 128)
+            )
+        device_rows[:, 1 + count, :] = jnp.broadcast_to(loss, (devices, 128))
         for copy in go:
             copy.wait()
 
@@ -1574,33 +1631,77 @@
         ((tokens, features), bf16),
         ((tokens, width), bf16),
     ]
-    small = [((8, width), f32), ((8, width), f32), ((8, features), f32), ((8, 128), f32)]
+    small = [((2 * members, 2 + features // 128, 128), f32)]
     results = pl.pallas_call(
         functools.partial(head_kernel, members),
         name="head",
         in_specs=[ANY, ANY, inside, ANY, inside, ANY, inside, ANY, inside],
-        out_specs=[ANY] * 6 + [inside] * 4,
+        out_specs=[ANY] * 6 + [inside],
         out_shape=[jax.ShapeDtypeStruct(*leaf) for leaf in big + small],
         scratch_shapes=[
             pltpu.VMEM(array.shape, array.dtype) for array in (hidden, target, in_w, mid_w, out_w)
         ]
         + [pltpu.VMEM(*leaf) for leaf in big]
         + [pltpu.VMEM((tokens, width), bf16)] * 5
+        + [pltpu.VMEM((8, width), f32)] * 2
         + [DMA((5,)), DMA((6,))],
         compiler_params=pltpu.CompilerParams(vmem_limit_bytes=VMEM_BYTES),
         cost_estimate=pl.CostEstimate(
             flops=4 * work, bytes_accessed=40 * 2**20, transcendentals=0
         ),
     )(hidden, target, live_lanes, in_w, in_b[None], mid_w, mid_b[None], out_w, out_b[None])
-    grad_hidden, last_left, mid_left, in_left, grad_feature, grad_second = results[:6]
-    in_sums, mid_sums, out_sums, loss = results[6:]
+    grad_hidden, last_left, mid_left, in_left, grad_feature, grad_second, device_rows = results
     return (
         grad_hidden,
-        loss[0:1],
         (last_left, mid_left, in_left),
         (grad_feature, grad_second),
-        (in_sums[0:1], mid_sums[0:1], out_sums[0:1]),
-    )
+        device_rows,
+    )
+
+
+def trade_kernel(members, given, taken, send_sem, recv_sem):
+    core, index = lax.axis_index("section"), lax.axis_index("dp")
+    barrier = pltpu.get_barrier_semaphore()
+
+    def others(act):
+        def body(peer):
+            @pl.when(peer != index)
+            def _():
+                act(peer)
+
+        each(0, members, body)
+
+    def copy(peer):
+        return remote(given, taken.at[index], send_sem.at[peer], recv_sem.at[index], (core, peer))
+
+    others(
+        lambda peer: pl.semaphore_signal(
+            barrier, inc=1, device_id=(core, peer), device_id_type=MESH
+        )
+    )
+    pl.semaphore_wait(barrier, members - 1)
+    others(lambda peer: copy(peer).start())
+    taken[index] = given[...]
+    others(
+        lambda peer: remote(
+            given, taken.at[peer], send_sem.at[peer], recv_sem.at[peer], (core, peer)
+        ).wait_recv()
+    )
+    others(lambda peer: copy(peer).wait_send())
+
+
+def trade(block, collective_id):
+    members = lax.axis_size("dp")
+    inside = pl.BlockSpec(memory_space=pltpu.VMEM)
+    return pl.pallas_call(
+        functools.partial(trade_kernel, members),
+        name="trade",
+        out_shape=jax.ShapeDtypeStruct((members,) + block.shape, block.dtype),
+        in_specs=[inside],
+        out_specs=inside,
+        scratch_shapes=[DMA((members,)), DMA((members,))],
+        compiler_params=pltpu.CompilerParams(collective_id=collective_id, has_side_effects=True),
+    )(block)
 
 
 def hollow(shapes):
@@ -1654,7 +1755,8 @@
         pairs_back += [(high, low), (members + high, members + low)]
     axes = ("section", "dp")
 
-    all_buckets = lax.all_gather(buckets, "dp", axis=0, tiled=True)
+    bucket_block = jnp.broadcast_to(jnp.pad(buckets, (0, 128 - images))[None], (8, 128))
+    all_buckets = trade(bucket_block, 1)[:, 0, :images].reshape(-1)
     one_hot = (
         all_buckets[:, None] == jnp.arange(time_table.shape[0], dtype=jnp.int32)[None, :]
     ).astype(jnp.float32)
@@ -1730,6 +1832,7 @@
     targets_out, rows_in = lax.optimization_barrier((targets, rows_in))
     hidden_first = jnp.where(crossed, rows_in, tokens_in)
     outer = jnp.where(crossed, rows_in, cotangent)
+    outer = lax.optimization_barrier(outer)
     own_targets = jnp.where(crossed, lax.ppermute(targets_out, axes, pairs_swap), targets)
 
     def unused(function, *operands_in):
@@ -1750,7 +1853,7 @@
 
     head_result = head_pass(first_out, own_targets, token_live, head_weights, members)
     hidden_second, head_result = lax.optimization_barrier((hidden_second, head_result))
-    grad_hidden, loss_part, head_lefts, head_rights, head_sums = head_result
+    grad_hidden, head_lefts, head_rights, head_rows = head_result
 
     def do_second(rows, mod, grad, block):
         final, state, lefts = block_forward(rows, mod, block, members)
@@ -1796,25 +1899,6 @@
                 block_weights,
             )
         )
-    sums_first = [result[2] for result in first]
-    low_sums, high_sums = (
-        jnp.where(is_first, jnp.concatenate([sums_of[j] for sums_of in sums_first]), second[3][j])
-        for j in range(2)
-    )
-    pack_row, pre_row, out_rows = (
-        jnp.where(is_first, sum(sums_of[j] for sums_of in sums_first), second[3][j])[..., 0:1, :]
-        for j in range(2, 5)
-    )
-    grad_mod = narrow(
-        jnp.concatenate([low_sums[:, 0:2], high_sums[:, 2:6]], 1).reshape(images, 6 * channels)
-    )
-    bias_grads = (
-        jnp.concatenate([pack_row[:, :channels], pack_row[:, 2 * channels :]], 1),
-        out_rows[1],
-        pre_row,
-        out_rows[0],
-    )
-
     def by_layer(results):
         return [list(parts_of) for parts_of in zip(*results)]
 
@@ -1822,33 +1906,21 @@
         [[left] for left in first_lefts],
         by_layer([result[1] for result in first]),
         [result[0] for result in first],
-    )
-    backs = ([[left] for left in second[4]], [[right] for right in second[2]], [second[1]])
-    bias_rows = jnp.concatenate([grads.reshape(members, -1) for grads in bias_grads], 1)
-    bias_width = bias_rows.shape[1]
-    bias_rows = jnp.pad(bias_rows, ((0, 0), (0, 1024 - bias_width))).reshape(members, 8, 128)
-    in_sums, mid_sums, out_sums = head_sums
-    devices = 2 * members
-    out_width = out_sums.shape[1]
-    head_rows = jnp.concatenate(
-        [
-            in_sums.reshape(devices, -1),
-            mid_sums.reshape(devices, -1),
-            jnp.broadcast_to(out_sums, (devices, out_width)),
-            jnp.broadcast_to(loss_part[:, 0:1], (devices, 1)),
-        ],
-        1,
-    )
-    head_width = head_rows.shape[1]
-    head_rows = jnp.pad(head_rows, ((0, 0), (0, 1024 - head_width))).reshape(devices, 8, 128)
+        [result[2] for result in first],
+    )
+    backs = (
+        [[left] for left in second[4]],
+        [[right] for right in second[2]],
+        [second[1]],
+        [second[3]],
+    )
     block_grads, head_grads, stream_in, bias_all, head_all, mod_wide, silu_all_terms = reduce(
         fronts,
         backs,
         head_parts,
-        grad_mod,
-        bias_rows,
         head_rows,
         modulate_weight[0],
+        widths[:4],
         3,
     )
     down_grad, up_grad, attn_grad, qkv_grad = block_grads
@@ -1861,15 +1933,15 @@
     cond_grad = local_grad(jax.nn.silu, conditioning, silu_total)
     table_grad = jnp.dot(one_hot.T, cond_grad, precision=HIGHEST)
 
-    bias_sums = jnp.sum(bias_all, 0).reshape(-1)
-    bias_outs, offset = [], 0
-    for part in section_biases:
-        width = part.shape[0]
-        bias_outs.append(bias_sums[offset : offset + width][None])
-        offset += width
-    sums = jnp.sum(head_all, 0).reshape(-1)
-    head_share = in_sums.shape[1] // devices
-    loss_value = sums[head_width - 1] / total_live
+    bias_sums = jnp.sum(bias_all, 0)
+    bias_outs, line = [], 0
+    for width in widths[:4]:
+        count = -(-width // 128)
+        bias_outs.append(bias_sums[line : line + count].reshape(1, -1)[:, :width])
+        line += count
+    sums = jnp.sum(head_all, 0)
+    head_share = head_grads[1].shape[0]
+    loss_value = sums[-1, 0] / total_live
     return (
         stream_own[None],
         loss_value,
@@ -1885,11 +1957,11 @@
         wide(down_grad)[None],
         bias_outs[3],
         wide(head_grads[2]).T,
-        sums[:head_share],
+        sums[0, :head_share],
         wide(head_grads[1]),
-        sums[head_share : 2 * head_share],
+        sums[0, head_share : 2 * head_share],
         wide(head_grads[0]),
-        sums[2 * head_share : 2 * head_share + out_width],
+        sums[1:-1].reshape(-1),
     )
 
 

time: 738 us -> 725 us (0.982)
  blocking collectives: 13.6 us -> 0 us
  waiting for transfers between devices: 19.9 us -> 33 us
  other arithmetic: 30.3 us -> 18.6 us
  local copies, waits for them, and re-layouts: 27.5 us -> 16.9 us
  Pallas kernels: 616 us -> 626 us
    unnamed x1 -> x0, blocking collectives: 13.6 us -> none
    pallas_call x0 -> x1, Pallas kernels: none -> 9.28 us  [trade(): pl.pallas_call(functools.partial(trade_kernel, members), name='trade', ou...]
    ppermute x2, waiting for transfers between devices: 13.9 us -> 21.4 us  [on_device(): returning = [lax.ppermute(rows, axes, pairs_back) for rows in second[0]]]
  transfers between devices with their start and end apart: 4 -> 4, of which waited for: 3 -> 3; matrix products, arithmetic and copies ran while one was open for 3% -> 2% of each run, Pallas kernels for 1% -> 1%
where the time goes in v5:
time: 725 us; the launch traced here: 719 us
  Pallas kernels  626 us (86%)
  waiting for transfers between devices  33 us (5%)
  other arithmetic  18.6 us (3%)
  local copies, waits for them, and re-layouts  16.9 us (2%)
  matrix products  11.8 us (2%)
  starting transfers between devices  7.71 us (1%)
    pallas_call x1, Pallas kernels, gather(): pl.pallas_call(functools.partial(gather_kernel, length, count, heads, wid...  253 us
    pallas_call x1, Pallas kernels, reduce(): pl.pallas_call(functools.partial(reduce_kernel, length, form, count, head...  253 us
    pallas_call x1, Pallas kernels, mlp_back(): pl.pallas_call(functools.partial(mlp_back_kernel, given_grad), grid=(widt...  30.4 us
    pallas_call x1, Pallas kernels, attend_back(): pl.pallas_call(functools.partial(attend_back_kernel, HEADS), grid=(images...  26.7 us
    pallas_call x1, Pallas kernels, mlp(): pl.pallas_call(mlp_kernel, grid=(width // tile,), name='mlp', in_specs=[f...  25 us
    ppermute x2, waiting for transfers between devices, on_device(): returning = [lax.ppermute(rows, axes, pairs_back) for rows in second[0]]  21.4 us
    pallas_call x1, Pallas kernels, attend(): pl.pallas_call(functools.partial(attend_kernel, HEADS), grid=(images,), n...  18.9 us
  transfers between devices with their start and end apart: 4, of which 3 were waited for; matrix products, arithmetic and copies ran while one was open for 2% of the time, Pallas kernels for 1%

profile of v5, /device:TPU:10, one launch (start us, length us, event | category | flops | bytes accessed | tf_op | source)
XLA Modules:
  0.0 719.4 jit_solution(14504142259711687774)
XLA Ops:
  1.9 9.3 %trade.1 = s32[16,8,128]{2,1,0:T(8,128)} custom-call(s32[8,128]{1,0:T(8,128)} %broadcast_in_dim.62.given), custom_call_target="tpu_custom_call" | custom-call | tf_op jit(solution)/shard_map/trade/pallas_call | solution.py:1696
  11.2 0.9 slice_reduce_fusion.1
  12.8 4.1 add_divide_fusion
  18.2 1.4 reshape.119.refs_8_
  20.4 253.5 %gather.1 = (bf16[16,16,128]{2,1,0:T(8,128)(2,1)}, bf16[16,72,3456]{2,1,0:T(8,128)(2,1)}, bf16[16,72,1152]{2,1,0:T(8,128)(2,1)}, bf16[16,72,4608]{2,1,0:T(8,128)...) custom-call(bf16[16,128]{1,0:T(8,128)(2,1)} %pad.32.refs_0_, ...), custom_call_target="tpu_custom_call" | custom-call | bytes 770703360 | tf_op jit(solution)/shard_map/gather/pallas_call | solution.py:452
  273.9 2.2 collective-permute-start.1
  276.1 1.2 reduce_sum.54
  278.6 2.9 broadcast_select_fusion
  282.4 1.3 collective-permute-start
  285.1 1.3 slice.58.out_b
  287.0 1.3 fusion.17
  288.3 2.1 broadcast_select_fusion.2.target_at
  290.4 0.8 broadcast_in_dim.67.live
  291.3 9.5 %head.1 = (f32[512,1152]{1,0:T(8,128)}, bf16[8,2,128,512]{3,2,1,0:T(8,128)(2,1)}, bf16[8,2,128,512]{3,2,1,0:T(8,128)(2,1)}, bf16[8,2,128,512]{3,2,1,0:T(8,128)(2...) custom-call(bf16[512,1152]{1,0:T(8,128)(2,1)} %get-tuple-element.317.hidden_at.refs_5_, ...), custom_call_target="tpu_custom_call" | custom-call | flops 16642998272 | bytes 41943040 | tf_op jit(solution)/shard_map/head/pallas_call | solution.py:1635
  300.8 11.6 %collective-permute-done = bf16[512,1152]{1,0:T(8,128)(2,1)} collective-permute-done((bf16[512,1152]{1,0:T(8,128)(2,1)}, bf16[512,1152]{1,0:T(8,128)(2,1)}, u32[]{:S(2)}, u32[]{:S(2)}) %collective-permute-start) | collective-permute-done | bytes 1179680 | tf_op jit(solution)/shard_map/ppermute | solution.py:1852
  312.4 103.8 %conditional.5 = ((bf16[256,1152]{1,0:T(8,128)(2,1)}, bf16[256,1152]{1,0:T(8,128)(2,1)}, bf16[512,1152]{1,0:T(8,128)(2,1)}, bf16[512,1152]{1,0:T(8,128)(2,1)}, b...) conditional(s32[]{:T(128)} %convert_element_type.47, ...), branch_computations={%region_3.4_spmd, %region_4.5_spmd} | conditional | flops 34728837120 | bytes 170131584 | solution.py:1866
  312.4 18.9 %attend.3 = (bf16[8,2,72,512]{3,2,1,0:T(8,128)(2,1)}, bf16[512,3456]{1,0:T(8,128)(2,1)}, bf16[2,16,256,256]{3,2,1,0:T(8,128)(2,1)}, bf16[8,2,72,512]{3,2,1,0:T(8...) custom-call(bf16[512,1152]{1,0:T(8,128)(2,1)} %get-tuple-element.104.hidden, ...), custom_call_target="tpu_custom_call" | custom-call | flops 6039797760 | bytes 41943040 | tf_op jit(solution)/shard_map/cond/branch_0_fun/attend/pallas_call | solution.py:1154
  331.3 25.0 %mlp.3 = (bf16[8,2,72,512]{3,2,1,0:T(8,128)(2,1)}, bf16[8,2,288,512]{3,2,1,0:T(8,128)(2,1)}, bf16[512,4608]{1,0:T(8,128)(2,1)}, bf16[512,1152]{1,0:T(8,128)(2,1)}, bf16[512,1152]{1,0:T(8,128)(2,1)}) custom-call(f32[512,1152]{1,0:T(8,128)} %get-tuple-element.112.after, f32[2,8,1152]{2,1,0:T(8,128)S(1)} %get-tuple-element.105.pieces, ...), custom_call_target="tpu_custom_call" | custom-call | flops 10871635968 | bytes 41943040 | tf_op jit(solution)/shard_map/cond/branch_0_fun/mlp/pallas_call | solution.py:1244
  356.3 30.4 %mlp_back.3 = (bf16[512,1152]{1,0:T(8,128)(2,1)}, bf16[512,4608]{1,0:T(8,128)(2,1)}, f32[512,1152]{1,0:T(8,128)}, bf16[512,1152]{1,0:T(8,128)(2,1)}, f32[2,8,115...) custom-call(bf16[512,1152]{1,0:T(8,128)(2,1)} %get-tuple-element.111.grad.extra, ...), custom_call_target="tpu_custom_call" | custom-call | flops 10871635968 | bytes 41943040 | tf_op jit(solution)/shard_map/cond/branch_0_fun/mlp_back/pallas_call | solution.py:1344
  386.7 26.7 %attend_back.3 = (bf16[512,3456]{1,0:T(8,128)(2,1)}, bf16[512,1152]{1,0:T(8,128)(2,1)}, f32[2,8,1152]{2,1,0:T(8,128)}, f32[8,3456]{1,0:T(8,128)}) custom-call(bf16[512,1152]{1,0:T(8,128)(2,1)} %get-tuple-element.104.hidden, f32[2,8,1152]{2,1,0:T(8,128)S(1)} %get-tuple-element.105.pieces, bf16[512,3456]{1,0:T(8,128)(2,1)} %get-tuple-element.109.packed, ...), custom_call_target="tpu_custom_call" | custom-call | flops 6945767424 | bytes 41943040 | tf_op jit(solution)/shard_map/cond/branch_0_fun/attend_back/pallas_call | solution.py:1436
  413.4 2.3 fusion.16
  416.2 2.1 collective-permute-start.2
  418.3 2.1 collective-permute-start.3
  420.9 10.7 %collective-permute-done.2 = bf16[256,1152]{1,0:T(8,128)(2,1)} collective-permute-done((bf16[256,1152]{1,0:T(8,128)(2,1)}, bf16[256,1152]{1,0:T(8,128)(2,1)}, u32[]{:S(2)}, u32[]{:S(2)}) %collective-permute-start.2) | collective-permute-done | bytes 589856 | tf_op jit(solution)/shard_map/ppermute | solution.py:1875
  431.7 10.7 %collective-permute-done.3 = bf16[256,1152]{1,0:T(8,128)(2,1)} collective-permute-done((bf16[256,1152]{1,0:T(8,128)(2,1)}, bf16[256,1152]{1,0:T(8,128)(2,1)}, u32[]{:S(2)}, u32[]{:S(2)}) %collective-permute-start.3) | collective-permute-done | bytes 589856 | tf_op jit(solution)/shard_map/ppermute | solution.py:1875
  442.7 252.7 %reduce.7 = (bf16[288,1152]{1,0:T(8,128)(2,1)}, bf16[72,4608]{1,0:T(8,128)(2,1)}, bf16[72,1152]{1,0:T(8,128)(2,1)}, bf16[72,3456]{1,0:T(8,128)(2,1)}, bf16[64,76...) custom-call(bf16[8,2,288,512]{3,2,1,0:T(8,128)(2,1)} %get-tuple-elem, ...), custom_call_target="tpu_custom_call" | custom-call | flops 16307453952 | bytes 509607936 | tf_op jit(solution)/shard_map/reduce/pallas_call | solution.py:1011
  695.4 3.0 convolution_bitcast_fusion
  701.7 4.4 fusion.5
  706.2 1.1 bitcast_convert_fusion
  707.5 1.2 bitcast_convert_fusion.1
  709.3 2.6 fusion.1
  711.9 1.0 bitcast_convert_fusion.2
  (111 shorter events, 16.7 us)
Async XLA Ops:
  12.8 5.0 copy-start.9
  18.1 1.5 copy-start.23
  18.1 1.5 copy-start.24
  18.1 1.6 copy-start.31
  18.1 1.6 copy-start.27
  18.2 1.6 copy-start.28
  18.2 1.6 copy-start.25
  18.2 1.6 copy-start.26
  20.4 256.9 %copy-start.32 = (s32[16]{0:T(128)S(1)}, s32[16]{0:T(128)}, u32[]{:S(2)}) copy-start(s32[16]{0:T(128)} %param.34) | copy-start | bytes 196
  20.4 258.2 %copy-start = (bf16[512,1152]{1,0:T(8,128)(2,1)S(1)}, bf16[512,1152]{1,0:T(8,128)(2,1)}, u32[]{:S(2)}) copy-start(bf16[512,1152]{1,0:T(8,128)(2,1)} %refs_9_.1) | copy-start | bytes 3538948
  20.4 258.2 %copy-start.1 = (bf16[512,1152]{1,0:T(8,128)(2,1)S(1)}, bf16[512,1152]{1,0:T(8,128)(2,1)}, u32[]{:S(2)}) copy-start(bf16[512,1152]{1,0:T(8,128)(2,1)} %refs_10_.1) | copy-start | bytes 3538948
  273.9 14.4 %collective-permute-start.1 = (bf16[512,768]{1,0:T(8,128)(2,1)}, bf16[512,768]{1,0:T(8,128)(2,1)}, u32[]{:S(2)}, u32[]{:S(2)}) collective-permute-start(bf16[512,768]{1,0:T(8,128)(2,1)} %param.32), channel_id=1, source_target_pairs={{1,16},{3,18},{5,20},{7,22},{9,24},{11,26},{13,28},{15,30}} | collective-permute-start | bytes 2359304 | tf_op jit(solution)/shard_map/ppermute | solution.py:1836
  282.2 1.5 copy-start.33
  282.4 30.0 %collective-permute-start = (bf16[512,1152]{1,0:T(8,128)(2,1)}, bf16[512,1152]{1,0:T(8,128)(2,1)}, u32[]{:S(2)}, u32[]{:S(2)}) collective-permute-start(bf16[512,1152]{1,0:T(8,128)(2,1)} %get-tuple-element.317.hidden_at.refs_5_), channel_id=1, source_target_pairs={{0,1},{16,17},{2,3},{18,19},{4,5},{20,21},{6,7},{22,23},{8,9},{24,... | collective-permute-start | bytes 3538952 | tf_op jit(solution)/shard_map/ppermute | solution.py:1852
  291.3 21.1 %copy-start.3 = (f32[2,8,1152]{2,1,0:T(8,128)S(1)}, f32[2,8,1152]{2,1,0:T(8,128)}, u32[]{:S(2)}) copy-start(f32[2,8,1152]{2,1,0:T(8,128)} %pad_maximum_fusion) | copy-start | bytes 221188
  291.3 21.1 %copy-start.29 = (f32[1,10368]{1,0:T(1,128)S(1)}, f32[1,10368]{1,0:T(1,128)}, u32[]{:S(2)}) copy-start(f32[1,10368]{1,0:T(1,128)} %get-tuple-element.309) | copy-start | bytes 124420
  416.2 15.4 %collective-permute-start.2 = (bf16[256,1152]{1,0:T(8,128)(2,1)}, bf16[256,1152]{1,0:T(8,128)(2,1)}, u32[]{:S(2)}, u32[]{:S(2)}) collective-permute-start(bf16[256,1152]{1,0:T(8,128)(2,1)} %get-tuple-element.331), channel_id=1, source_target_pairs={{1,0},{17,16},{3,2},{19,18},{5,4},{21,20},{7,6},{23,22},{9,8},{25,... | collective-permute-start | bytes 1769480 | tf_op jit(solution)/shard_map/ppermute | solution.py:1875
  418.3 24.1 %collective-permute-start.3 = (bf16[256,1152]{1,0:T(8,128)(2,1)}, bf16[256,1152]{1,0:T(8,128)(2,1)}, u32[]{:S(2)}, u32[]{:S(2)}) collective-permute-start(bf16[256,1152]{1,0:T(8,128)(2,1)} %get-tuple-element.355), channel_id=1, source_target_pairs={{1,0},{17,16},{3,2},{19,18},{5,4},{21,20},{7,6},{23,22},{9,8},{25,... | collective-permute-start | bytes 1769480 | tf_op jit(solution)/shard_map/ppermute | solution.py:1875
  695.4 3.0 copy-start.2
  695.4 3.1 copy-start.22
  695.4 4.8 copy-start.21
  695.4 5.9 copy-start.15
  698.4 3.3 copy-start.13
  701.7 4.4 copy-start.11
  706.1 1.3 copy-start.10
  706.2 2.5 copy-start.8
  707.3 1.6 copy-start.7
  707.3 2.0 copy-start.14
  709.3 2.6 copy-start.16
  711.9 1.9 copy-start.18
  711.9 2.6 copy-start.19
  711.9 3.4 copy-start.20
  (2 other events, 1.7 us)

commit v6 on v5

--- a/solution.py
+++ b/solution.py
@@ -1481,7 +1481,7 @@
     return (
         final,
         (packed, probs, attn_out, after, slope, mlp_out),
-        (act_left, rows_left, mixed_left, input_left),
+        (act_left, rows_left, input_left, mixed_left),
     )
 
 
@@ -1494,7 +1494,7 @@
     grad_packed, grad_hidden, low_sums, pack_sums = attend_back(
         hidden, pieces, packed, probs, grad_attn, grad_after, pack_w, out_w, image
     )
-    rights = (grad_mlp, grad_pre, grad_attn, grad_packed)
+    rights = (grad_mlp, grad_pre, grad_packed, grad_attn)
     return grad_hidden, rights, (low_sums, high_sums, pack_sums, pre_sums, out_sums)
 
 
@@ -1831,8 +1831,6 @@
     crossed = core != role
     targets_out, rows_in = lax.optimization_barrier((targets, rows_in))
     hidden_first = jnp.where(crossed, rows_in, tokens_in)
-    outer = jnp.where(crossed, rows_in, cotangent)
-    outer = lax.optimization_barrier(outer)
     own_targets = jnp.where(crossed, lax.ppermute(targets_out, axes, pairs_swap), targets)
 
     def unused(function, *operands_in):
@@ -1851,6 +1849,8 @@
     )
     hidden_second = lax.ppermute(first_out, axes, pairs_up)
 
+    rows_late, _ = lax.optimization_barrier((rows_in, first_out))
+    outer = lax.optimization_barrier(jnp.where(crossed, rows_late, cotangent))
     head_result = head_pass(first_out, own_targets, token_live, head_weights, members)
     hidden_second, head_result = lax.optimization_barrier((hidden_second, head_result))
     grad_hidden, head_lefts, head_rights, head_rows = head_result
@@ -1872,11 +1872,16 @@
         outer,
         block_weights,
     )
-    returning = [lax.ppermute(rows, axes, pairs_back) for rows in second[0]]
+    grad_rows = second[0]
+    returning = [lax.ppermute(grad_rows[0], axes, pairs_back)]
     head_lefts, head_rights, kept = lax.optimization_barrier((head_lefts, head_rights, second[1]))
     second = (second[0], kept) + second[2:]
     head_parts = head_reduce(head_lefts, head_rights + (first_out,), 2)
-    returning[0], head_parts = lax.optimization_barrier((returning[0], head_parts))
+    returning[0], head_parts, grad_rows = lax.optimization_barrier(
+        (returning[0], head_parts, grad_rows)
+    )
+    for i in range(1, images):
+        returning.append(lax.ppermute(grad_rows[i], axes, pairs_back))
     first = []
     for i in range(images):
 
@@ -1923,7 +1928,7 @@
         widths[:4],
         3,
     )
-    down_grad, up_grad, attn_grad, qkv_grad = block_grads
+    down_grad, up_grad, qkv_grad, attn_grad = block_grads
     stream = jnp.where(is_first, jnp.concatenate(fronts[2]), jnp.concatenate(backs[2]))
     stream_own = jnp.where(crossed, stream_in, stream)
     mod_w_grad = product_left_t(silu_depth, narrow(mod_wide))

time: 725 us -> 723 us (level)
  no operation moved by 1% of the time
where the time goes in v6:
time: 723 us; the launch traced here: 718 us
  Pallas kernels  625 us (86%)
  waiting for transfers between devices  28.1 us (4%)
  other arithmetic  20.6 us (3%)
  local copies, waits for them, and re-layouts  15.5 us (2%)
  matrix products  11.8 us (2%)
  starting transfers between devices  10.8 us (1%)
    pallas_call x1, Pallas kernels, gather(): pl.pallas_call(functools.partial(gather_kernel, length, count, heads, wid...  253 us
    pallas_call x1, Pallas kernels, reduce(): pl.pallas_call(functools.partial(reduce_kernel, length, form, count, head...  252 us
    pallas_call x1, Pallas kernels, mlp_back(): pl.pallas_call(functools.partial(mlp_back_kernel, given_grad), grid=(widt...  30.3 us
    pallas_call x1, Pallas kernels, attend_back(): pl.pallas_call(functools.partial(attend_back_kernel, HEADS), grid=(images...  26.7 us
    pallas_call x1, Pallas kernels, mlp(): pl.pallas_call(mlp_kernel, grid=(width // tile,), name='mlp', in_specs=[f...  25.1 us
    pallas_call x1, Pallas kernels, attend(): pl.pallas_call(functools.partial(attend_kernel, HEADS), grid=(images,), n...  18.9 us
  transfers between devices with their start and end apart: 4, of which 3 were waited for; matrix products, arithmetic and copies ran while one was open for 2% of the time, Pallas kernels for 1%

profile of v6, /device:TPU:10, one launch (start us, length us, event | category | flops | bytes accessed | tf_op | source)
XLA Modules:
  0.0 717.5 jit_solution(5748194457699907952)
XLA Ops:
  1.9 9.3 %trade.1 = s32[16,8,128]{2,1,0:T(8,128)} custom-call(s32[8,128]{1,0:T(8,128)} %broadcast_in_dim.62.given), custom_call_target="tpu_custom_call" | custom-call | tf_op jit(solution)/shard_map/trade/pallas_call | solution.py:1696
  11.2 0.9 slice_reduce_fusion.1
  12.8 4.1 add_divide_fusion
  18.2 1.4 reshape.119.refs_8_
  20.4 253.4 %gather.1 = (bf16[16,16,128]{2,1,0:T(8,128)(2,1)}, bf16[16,72,3456]{2,1,0:T(8,128)(2,1)}, bf16[16,72,1152]{2,1,0:T(8,128)(2,1)}, bf16[16,72,4608]{2,1,0:T(8,128)...) custom-call(bf16[16,128]{1,0:T(8,128)(2,1)} %pad.32.refs_0_, ...), custom_call_target="tpu_custom_call" | custom-call | bytes 770703360 | tf_op jit(solution)/shard_map/gather/pallas_call | solution.py:452
  273.9 2.2 collective-permute-start.1
  277.3 1.2 reduce_sum.54
  279.3 2.4 broadcast_select_fusion.1
  281.9 1.3 collective-permute-start
  283.2 2.4 broadcast_select_fusion
  287.6 2.1 broadcast_select_fusion.2.target_at
  289.7 0.8 broadcast_in_dim.67.live
  290.5 9.5 %head.1 = (f32[512,1152]{1,0:T(8,128)}, bf16[8,2,128,512]{3,2,1,0:T(8,128)(2,1)}, bf16[8,2,128,512]{3,2,1,0:T(8,128)(2,1)}, bf16[8,2,128,512]{3,2,1,0:T(8,128)(2...) custom-call(bf16[512,1152]{1,0:T(8,128)(2,1)} %get-tuple-element.319.hidden_at.refs_5_, ...), custom_call_target="tpu_custom_call" | custom-call | flops 16642998272 | bytes 41943040 | tf_op jit(solution)/shard_map/head/pallas_call | solution.py:1635
  300.0 10.6 %collective-permute-done = bf16[512,1152]{1,0:T(8,128)(2,1)} collective-permute-done((bf16[512,1152]{1,0:T(8,128)(2,1)}, bf16[512,1152]{1,0:T(8,128)(2,1)}, u32[]{:S(2)}, u32[]{:S(2)}) %collective-permute-start) | collective-permute-done | bytes 1179680 | tf_op jit(solution)/shard_map/ppermute | solution.py:1850
  310.6 103.7 %conditional.5 = ((bf16[256,1152]{1,0:T(8,128)(2,1)}, bf16[256,1152]{1,0:T(8,128)(2,1)}, bf16[512,1152]{1,0:T(8,128)(2,1)}, bf16[512,1152]{1,0:T(8,128)(2,1)}, b...) conditional(s32[]{:T(128)} %convert_element_type.47, ...), branch_computations={%region_3.4_spmd, %region_4.5_spmd} | conditional | flops 34728837120 | bytes 170131584 | solution.py:1866
  310.6 18.9 %attend.3 = (bf16[8,2,72,512]{3,2,1,0:T(8,128)(2,1)}, bf16[512,3456]{1,0:T(8,128)(2,1)}, bf16[2,16,256,256]{3,2,1,0:T(8,128)(2,1)}, bf16[8,2,72,512]{3,2,1,0:T(8...) custom-call(bf16[512,1152]{1,0:T(8,128)(2,1)} %get-tuple-element.104.hidden, ...), custom_call_target="tpu_custom_call" | custom-call | flops 6039797760 | bytes 41943040 | tf_op jit(solution)/shard_map/cond/branch_0_fun/attend/pallas_call | solution.py:1154
  329.5 25.1 %mlp.3 = (bf16[8,2,72,512]{3,2,1,0:T(8,128)(2,1)}, bf16[8,2,288,512]{3,2,1,0:T(8,128)(2,1)}, bf16[512,4608]{1,0:T(8,128)(2,1)}, bf16[512,1152]{1,0:T(8,128)(2,1)}, bf16[512,1152]{1,0:T(8,128)(2,1)}) custom-call(f32[512,1152]{1,0:T(8,128)} %get-tuple-element.112.after, f32[2,8,1152]{2,1,0:T(8,128)S(1)} %get-tuple-element.105.pieces, ...), custom_call_target="tpu_custom_call" | custom-call | flops 10871635968 | bytes 41943040 | tf_op jit(solution)/shard_map/cond/branch_0_fun/mlp/pallas_call | solution.py:1244
  354.5 30.3 %mlp_back.3 = (bf16[512,1152]{1,0:T(8,128)(2,1)}, bf16[512,4608]{1,0:T(8,128)(2,1)}, f32[512,1152]{1,0:T(8,128)}, bf16[512,1152]{1,0:T(8,128)(2,1)}, f32[2,8,115...) custom-call(bf16[512,1152]{1,0:T(8,128)(2,1)} %get-tuple-element.111.grad.extra, ...), custom_call_target="tpu_custom_call" | custom-call | flops 10871635968 | bytes 41943040 | tf_op jit(solution)/shard_map/cond/branch_0_fun/mlp_back/pallas_call | solution.py:1344
  384.8 26.7 %attend_back.3 = (bf16[512,3456]{1,0:T(8,128)(2,1)}, bf16[512,1152]{1,0:T(8,128)(2,1)}, f32[2,8,1152]{2,1,0:T(8,128)}, f32[8,3456]{1,0:T(8,128)}) custom-call(bf16[512,1152]{1,0:T(8,128)(2,1)} %get-tuple-element.104.hidden, f32[2,8,1152]{2,1,0:T(8,128)S(1)} %get-tuple-element.105.pieces, bf16[512,3456]{1,0:T(8,128)(2,1)} %get-tuple-element.109.packed, ...), custom_call_target="tpu_custom_call" | custom-call | flops 6945767424 | bytes 41943040 | tf_op jit(solution)/shard_map/cond/branch_0_fun/attend_back/pallas_call | solution.py:1436
  411.5 2.3 fusion.16
  414.3 2.1 collective-permute-start.2
  416.9 9.7 %collective-permute-done.2 = bf16[256,1152]{1,0:T(8,128)(2,1)} collective-permute-done((bf16[256,1152]{1,0:T(8,128)(2,1)}, bf16[256,1152]{1,0:T(8,128)(2,1)}, u32[]{:S(2)}, u32[]{:S(2)}) %collective-permute-start.2) | collective-permute-done | bytes 589856 | tf_op jit(solution)/shard_map/ppermute | solution.py:1876
  426.6 5.2 collective-permute-start.3
  433.3 7.8 %collective-permute-done.3 = bf16[256,1152]{1,0:T(8,128)(2,1)} collective-permute-done((bf16[256,1152]{1,0:T(8,128)(2,1)}, bf16[256,1152]{1,0:T(8,128)(2,1)}, u32[]{:S(2)}, u32[]{:S(2)}) %collective-permute-start.3) | collective-permute-done | bytes 589856 | tf_op jit(solution)/shard_map/ppermute | solution.py:1884
  441.7 251.8 %reduce.7 = (bf16[288,1152]{1,0:T(8,128)(2,1)}, bf16[72,4608]{1,0:T(8,128)(2,1)}, bf16[72,3456]{1,0:T(8,128)(2,1)}, bf16[72,1152]{1,0:T(8,128)(2,1)}, bf16[64,76...) custom-call(bf16[8,2,288,512]{3,2,1,0:T(8,128)(2,1)} %get-tuple-elem, ...), custom_call_target="tpu_custom_call" | custom-call | flops 16307453952 | bytes 509607936 | tf_op jit(solution)/shard_map/reduce/pallas_call | solution.py:1011
  693.5 3.0 convolution_bitcast_fusion
  699.8 4.4 fusion.5
  704.3 1.1 bitcast_convert_fusion
  705.6 1.2 bitcast_convert_fusion.1
  707.5 2.6 fusion.1
  710.1 1.0 bitcast_convert_fusion.2
  711.1 0.8 convert_element_type.52
  (110 shorter events, 17.4 us)
Async XLA Ops:
  12.8 5.0 copy-start.8
  18.1 1.5 copy-start.23
  18.1 1.5 copy-start.24
  18.1 1.6 copy-start.31
  18.1 1.6 copy-start.27
  18.2 1.6 copy-start.28
  18.2 1.6 copy-start.25
  18.2 1.6 copy-start.26
  20.4 255.6 %copy-start.32 = (s32[16]{0:T(128)S(1)}, s32[16]{0:T(128)}, u32[]{:S(2)}) copy-start(s32[16]{0:T(128)} %param.34) | copy-start | bytes 196
  20.4 258.8 %copy-start = (bf16[512,1152]{1,0:T(8,128)(2,1)S(1)}, bf16[512,1152]{1,0:T(8,128)(2,1)}, u32[]{:S(2)}) copy-start(bf16[512,1152]{1,0:T(8,128)(2,1)} %refs_9_.1) | copy-start | bytes 3538948
  273.9 13.7 %collective-permute-start.1 = (bf16[512,768]{1,0:T(8,128)(2,1)}, bf16[512,768]{1,0:T(8,128)(2,1)}, u32[]{:S(2)}, u32[]{:S(2)}) collective-permute-start(bf16[512,768]{1,0:T(8,128)(2,1)} %param.32), channel_id=1, source_target_pairs={{1,16},{3,18},{5,20},{7,22},{9,24},{11,26},{13,28},{15,30}} | collective-permute-start | bytes 2359304 | tf_op jit(solution)/shard_map/ppermute | solution.py:1834
  281.9 4.5 copy-start.22
  281.9 28.7 %collective-permute-start = (bf16[512,1152]{1,0:T(8,128)(2,1)}, bf16[512,1152]{1,0:T(8,128)(2,1)}, u32[]{:S(2)}, u32[]{:S(2)}) collective-permute-start(bf16[512,1152]{1,0:T(8,128)(2,1)} %get-tuple-element.319.hidden_at.refs_5_), channel_id=1, source_target_pairs={{0,1},{16,17},{2,3},{18,19},{4,5},{20,21},{6,7},{22,23},{8,9},{24,... | collective-permute-start | bytes 3538952 | tf_op jit(solution)/shard_map/ppermute | solution.py:1850
  290.5 20.1 %copy-start.2 = (f32[2,8,1152]{2,1,0:T(8,128)S(1)}, f32[2,8,1152]{2,1,0:T(8,128)}, u32[]{:S(2)}) copy-start(f32[2,8,1152]{2,1,0:T(8,128)} %pad_maximum_fusion) | copy-start | bytes 221188
  290.5 20.1 %copy-start.29 = (f32[1,10368]{1,0:T(1,128)S(1)}, f32[1,10368]{1,0:T(1,128)}, u32[]{:S(2)}) copy-start(f32[1,10368]{1,0:T(1,128)} %get-tuple-element.311) | copy-start | bytes 124420
  414.3 12.3 %collective-permute-start.2 = (bf16[256,1152]{1,0:T(8,128)(2,1)}, bf16[256,1152]{1,0:T(8,128)(2,1)}, u32[]{:S(2)}, u32[]{:S(2)}) collective-permute-start(bf16[256,1152]{1,0:T(8,128)(2,1)} %get-tuple-element.334), channel_id=1, source_target_pairs={{1,0},{17,16},{3,2},{19,18},{5,4},{21,20},{7,6},{23,22},{9,8},{25,... | collective-permute-start | bytes 1769480 | tf_op jit(solution)/shard_map/ppermute | solution.py:1876
  426.6 14.5 %collective-permute-start.3 = (bf16[256,1152]{1,0:T(8,128)(2,1)}, bf16[256,1152]{1,0:T(8,128)(2,1)}, u32[]{:S(2)}, u32[]{:S(2)}) collective-permute-start(bf16[256,1152]{1,0:T(8,128)(2,1)} %get-tuple-element.359), channel_id=1, source_target_pairs={{1,0},{17,16},{3,2},{19,18},{5,4},{21,20},{7,6},{23,22},{9,8},{25,... | collective-permute-start | bytes 1769480 | tf_op jit(solution)/shard_map/ppermute | solution.py:1884
  693.5 3.0 copy-start.1
  693.5 3.1 copy-start.21
  693.5 4.8 copy-start.20
  693.5 5.9 copy-start.14
  696.5 3.3 copy-start.12
  699.8 4.4 copy-start.10
  704.3 1.3 copy-start.9
  704.3 2.5 copy-start.7
  705.4 1.6 copy-start.6
  705.4 2.0 copy-start.13
  707.5 2.6 copy-start.15
  710.0 1.0 copy-start.16
  710.1 1.9 copy-start.17
  710.1 2.6 copy-start.18
  710.1 3.4 copy-start.19
  (1 other events, 0.7 us)

commit v7 on v6

--- a/solution.py
+++ b/solution.py
@@ -595,12 +595,15 @@
 
     def run(self, finish, early=None, midway=None, late=None):
         length = self.length
-        for layer in self.layers:
+        ahead = 2
+        for layer in self.layers[:ahead]:
             self.fetch(layer, lambda copy: copy.start())
         if early:
             early()
         for layer in self.layers:
             self.fetch(layer, lambda copy: copy.wait())
+            for later in self.layers[layer + ahead : layer + ahead + 1]:
+                self.fetch(later, lambda copy: copy.start())
             self.chunk(layer, 0, 0, False)
             self.onward(layer, 0, 0).start()
 

time: 723 us -> 723 us (level)
  no operation moved by 1% of the time
where the time goes in v7:
time: 723 us; the launch traced here: 717 us
  Pallas kernels  625 us (86%)
  waiting for transfers between devices  28.1 us (4%)
  other arithmetic  20.6 us (3%)
  local copies, waits for them, and re-layouts  15.5 us (2%)
  matrix products  11.8 us (2%)
  starting transfers between devices  10.8 us (1%)
    pallas_call x1, Pallas kernels, gather(): pl.pallas_call(functools.partial(gather_kernel, length, count, heads, wid...  253 us
    pallas_call x1, Pallas kernels, reduce(): pl.pallas_call(functools.partial(reduce_kernel, length, form, count, head...  252 us
    pallas_call x1, Pallas kernels, mlp_back(): pl.pallas_call(functools.partial(mlp_back_kernel, given_grad), grid=(widt...  30.3 us
    pallas_call x1, Pallas kernels, attend_back(): pl.pallas_call(functools.partial(attend_back_kernel, HEADS), grid=(images...  26.7 us
    pallas_call x1, Pallas kernels, mlp(): pl.pallas_call(mlp_kernel, grid=(width // tile,), name='mlp', in_specs=[f...  25.1 us
    pallas_call x1, Pallas kernels, attend(): pl.pallas_call(functools.partial(attend_kernel, HEADS), grid=(images,), n...  18.9 us
  transfers between devices with their start and end apart: 4, of which 3 were waited for; matrix products, arithmetic and copies ran while one was open for 2% of the time, Pallas kernels for 1%

profile of v7, /device:TPU:10, one launch (start us, length us, event | category | flops | bytes accessed | tf_op | source)
XLA Modules:
  0.0 717.5 jit_solution(6022812761488205035)
XLA Ops:
  1.9 9.3 %trade.1 = s32[16,8,128]{2,1,0:T(8,128)} custom-call(s32[8,128]{1,0:T(8,128)} %broadcast_in_dim.62.given), custom_call_target="tpu_custom_call" | custom-call | tf_op jit(solution)/shard_map/trade/pallas_call | solution.py:1699
  11.2 0.9 slice_reduce_fusion.1
  12.8 4.1 add_divide_fusion
  18.2 1.4 reshape.119.refs_8_
  20.4 253.4 %gather.1 = (bf16[16,16,128]{2,1,0:T(8,128)(2,1)}, bf16[16,72,3456]{2,1,0:T(8,128)(2,1)}, bf16[16,72,1152]{2,1,0:T(8,128)(2,1)}, bf16[16,72,4608]{2,1,0:T(8,128)...) custom-call(bf16[16,128]{1,0:T(8,128)(2,1)} %pad.32.refs_0_, ...), custom_call_target="tpu_custom_call" | custom-call | bytes 770703360 | tf_op jit(solution)/shard_map/gather/pallas_call | solution.py:452
  273.9 2.2 collective-permute-start.1
  277.3 1.2 reduce_sum.54
  279.3 2.4 broadcast_select_fusion.1
  281.9 1.3 collective-permute-start
  283.2 2.4 broadcast_select_fusion
  287.6 2.1 broadcast_select_fusion.2.target_at
  289.7 0.8 broadcast_in_dim.67.live
  290.5 9.5 %head.1 = (f32[512,1152]{1,0:T(8,128)}, bf16[8,2,128,512]{3,2,1,0:T(8,128)(2,1)}, bf16[8,2,128,512]{3,2,1,0:T(8,128)(2,1)}, bf16[8,2,128,512]{3,2,1,0:T(8,128)(2...) custom-call(bf16[512,1152]{1,0:T(8,128)(2,1)} %get-tuple-element.319.hidden_at.refs_5_, ...), custom_call_target="tpu_custom_call" | custom-call | flops 16642998272 | bytes 41943040 | tf_op jit(solution)/shard_map/head/pallas_call | solution.py:1638
  300.0 10.6 %collective-permute-done = bf16[512,1152]{1,0:T(8,128)(2,1)} collective-permute-done((bf16[512,1152]{1,0:T(8,128)(2,1)}, bf16[512,1152]{1,0:T(8,128)(2,1)}, u32[]{:S(2)}, u32[]{:S(2)}) %collective-permute-start) | collective-permute-done | bytes 1179680 | tf_op jit(solution)/shard_map/ppermute | solution.py:1853
  310.6 103.7 %conditional.5 = ((bf16[256,1152]{1,0:T(8,128)(2,1)}, bf16[256,1152]{1,0:T(8,128)(2,1)}, bf16[512,1152]{1,0:T(8,128)(2,1)}, bf16[512,1152]{1,0:T(8,128)(2,1)}, b...) conditional(s32[]{:T(128)} %convert_element_type.47, ...), branch_computations={%region_3.4_spmd, %region_4.5_spmd} | conditional | flops 34728837120 | bytes 170131584 | solution.py:1869
  310.6 18.9 %attend.3 = (bf16[8,2,72,512]{3,2,1,0:T(8,128)(2,1)}, bf16[512,3456]{1,0:T(8,128)(2,1)}, bf16[2,16,256,256]{3,2,1,0:T(8,128)(2,1)}, bf16[8,2,72,512]{3,2,1,0:T(8...) custom-call(bf16[512,1152]{1,0:T(8,128)(2,1)} %get-tuple-element.104.hidden, ...), custom_call_target="tpu_custom_call" | custom-call | flops 6039797760 | bytes 41943040 | tf_op jit(solution)/shard_map/cond/branch_0_fun/attend/pallas_call | solution.py:1157
  329.5 25.1 %mlp.3 = (bf16[8,2,72,512]{3,2,1,0:T(8,128)(2,1)}, bf16[8,2,288,512]{3,2,1,0:T(8,128)(2,1)}, bf16[512,4608]{1,0:T(8,128)(2,1)}, bf16[512,1152]{1,0:T(8,128)(2,1)}, bf16[512,1152]{1,0:T(8,128)(2,1)}) custom-call(f32[512,1152]{1,0:T(8,128)} %get-tuple-element.112.after, f32[2,8,1152]{2,1,0:T(8,128)S(1)} %get-tuple-element.105.pieces, ...), custom_call_target="tpu_custom_call" | custom-call | flops 10871635968 | bytes 41943040 | tf_op jit(solution)/shard_map/cond/branch_0_fun/mlp/pallas_call | solution.py:1247
  354.5 30.3 %mlp_back.3 = (bf16[512,1152]{1,0:T(8,128)(2,1)}, bf16[512,4608]{1,0:T(8,128)(2,1)}, f32[512,1152]{1,0:T(8,128)}, bf16[512,1152]{1,0:T(8,128)(2,1)}, f32[2,8,115...) custom-call(bf16[512,1152]{1,0:T(8,128)(2,1)} %get-tuple-element.111.grad.extra, ...), custom_call_target="tpu_custom_call" | custom-call | flops 10871635968 | bytes 41943040 | tf_op jit(solution)/shard_map/cond/branch_0_fun/mlp_back/pallas_call | solution.py:1347
  384.8 26.7 %attend_back.3 = (bf16[512,3456]{1,0:T(8,128)(2,1)}, bf16[512,1152]{1,0:T(8,128)(2,1)}, f32[2,8,1152]{2,1,0:T(8,128)}, f32[8,3456]{1,0:T(8,128)}) custom-call(bf16[512,1152]{1,0:T(8,128)(2,1)} %get-tuple-element.104.hidden, f32[2,8,1152]{2,1,0:T(8,128)S(1)} %get-tuple-element.105.pieces, bf16[512,3456]{1,0:T(8,128)(2,1)} %get-tuple-element.109.packed, ...), custom_call_target="tpu_custom_call" | custom-call | flops 6945767424 | bytes 41943040 | tf_op jit(solution)/shard_map/cond/branch_0_fun/attend_back/pallas_call | solution.py:1439
  411.5 2.3 fusion.16
  414.3 2.1 collective-permute-start.2
  416.9 9.7 %collective-permute-done.2 = bf16[256,1152]{1,0:T(8,128)(2,1)} collective-permute-done((bf16[256,1152]{1,0:T(8,128)(2,1)}, bf16[256,1152]{1,0:T(8,128)(2,1)}, u32[]{:S(2)}, u32[]{:S(2)}) %collective-permute-start.2) | collective-permute-done | bytes 589856 | tf_op jit(solution)/shard_map/ppermute | solution.py:1879
  426.6 5.2 collective-permute-start.3
  433.3 7.8 %collective-permute-done.3 = bf16[256,1152]{1,0:T(8,128)(2,1)} collective-permute-done((bf16[256,1152]{1,0:T(8,128)(2,1)}, bf16[256,1152]{1,0:T(8,128)(2,1)}, u32[]{:S(2)}, u32[]{:S(2)}) %collective-permute-start.3) | collective-permute-done | bytes 589856 | tf_op jit(solution)/shard_map/ppermute | solution.py:1887
  441.6 251.8 %reduce.7 = (bf16[288,1152]{1,0:T(8,128)(2,1)}, bf16[72,4608]{1,0:T(8,128)(2,1)}, bf16[72,3456]{1,0:T(8,128)(2,1)}, bf16[72,1152]{1,0:T(8,128)(2,1)}, bf16[64,76...) custom-call(bf16[8,2,288,512]{3,2,1,0:T(8,128)(2,1)} %get-tuple-elem, ...), custom_call_target="tpu_custom_call" | custom-call | flops 16307453952 | bytes 509607936 | tf_op jit(solution)/shard_map/reduce/pallas_call | solution.py:1014
  693.4 3.0 convolution_bitcast_fusion
  699.8 4.4 fusion.5
  704.2 1.1 bitcast_convert_fusion
  705.5 1.2 bitcast_convert_fusion.1
  707.4 2.6 fusion.1
  710.0 1.0 bitcast_convert_fusion.2
  711.0 0.8 convert_element_type.52
  (110 shorter events, 17.4 us)
Async XLA Ops:
  12.8 5.0 copy-start.8
  18.1 1.5 copy-start.23
  18.1 1.5 copy-start.24
  18.1 1.6 copy-start.31
  18.1 1.6 copy-start.27
  18.2 1.6 copy-start.28
  18.2 1.6 copy-start.25
  18.2 1.6 copy-start.26
  20.4 255.6 %copy-start.32 = (s32[16]{0:T(128)S(1)}, s32[16]{0:T(128)}, u32[]{:S(2)}) copy-start(s32[16]{0:T(128)} %param.34) | copy-start | bytes 196
  20.4 258.8 %copy-start = (bf16[512,1152]{1,0:T(8,128)(2,1)S(1)}, bf16[512,1152]{1,0:T(8,128)(2,1)}, u32[]{:S(2)}) copy-start(bf16[512,1152]{1,0:T(8,128)(2,1)} %refs_9_.1) | copy-start | bytes 3538948
  273.9 13.7 %collective-permute-start.1 = (bf16[512,768]{1,0:T(8,128)(2,1)}, bf16[512,768]{1,0:T(8,128)(2,1)}, u32[]{:S(2)}, u32[]{:S(2)}) collective-permute-start(bf16[512,768]{1,0:T(8,128)(2,1)} %param.32), channel_id=1, source_target_pairs={{1,16},{3,18},{5,20},{7,22},{9,24},{11,26},{13,28},{15,30}} | collective-permute-start | bytes 2359304 | tf_op jit(solution)/shard_map/ppermute | solution.py:1837
  281.9 4.5 copy-start.22
  281.9 28.7 %collective-permute-start = (bf16[512,1152]{1,0:T(8,128)(2,1)}, bf16[512,1152]{1,0:T(8,128)(2,1)}, u32[]{:S(2)}, u32[]{:S(2)}) collective-permute-start(bf16[512,1152]{1,0:T(8,128)(2,1)} %get-tuple-element.319.hidden_at.refs_5_), channel_id=1, source_target_pairs={{0,1},{16,17},{2,3},{18,19},{4,5},{20,21},{6,7},{22,23},{8,9},{24,... | collective-permute-start | bytes 3538952 | tf_op jit(solution)/shard_map/ppermute | solution.py:1853
  290.5 20.1 %copy-start.2 = (f32[2,8,1152]{2,1,0:T(8,128)S(1)}, f32[2,8,1152]{2,1,0:T(8,128)}, u32[]{:S(2)}) copy-start(f32[2,8,1152]{2,1,0:T(8,128)} %pad_maximum_fusion) | copy-start | bytes 221188
  290.5 20.1 %copy-start.29 = (f32[1,10368]{1,0:T(1,128)S(1)}, f32[1,10368]{1,0:T(1,128)}, u32[]{:S(2)}) copy-start(f32[1,10368]{1,0:T(1,128)} %get-tuple-element.311) | copy-start | bytes 124420
  414.3 12.3 %collective-permute-start.2 = (bf16[256,1152]{1,0:T(8,128)(2,1)}, bf16[256,1152]{1,0:T(8,128)(2,1)}, u32[]{:S(2)}, u32[]{:S(2)}) collective-permute-start(bf16[256,1152]{1,0:T(8,128)(2,1)} %get-tuple-element.334), channel_id=1, source_target_pairs={{1,0},{17,16},{3,2},{19,18},{5,4},{21,20},{7,6},{23,22},{9,8},{25,... | collective-permute-start | bytes 1769480 | tf_op jit(solution)/shard_map/ppermute | solution.py:1879
  426.6 14.5 %collective-permute-start.3 = (bf16[256,1152]{1,0:T(8,128)(2,1)}, bf16[256,1152]{1,0:T(8,128)(2,1)}, u32[]{:S(2)}, u32[]{:S(2)}) collective-permute-start(bf16[256,1152]{1,0:T(8,128)(2,1)} %get-tuple-element.359), channel_id=1, source_target_pairs={{1,0},{17,16},{3,2},{19,18},{5,4},{21,20},{7,6},{23,22},{9,8},{25,... | collective-permute-start | bytes 1769480 | tf_op jit(solution)/shard_map/ppermute | solution.py:1887
  693.4 3.0 copy-start.1
  693.4 3.1 copy-start.21
  693.4 4.8 copy-start.20
  693.4 5.9 copy-start.14
  696.4 3.3 copy-start.12
  699.7 4.4 copy-start.10
  704.2 1.3 copy-start.9
  704.2 2.5 copy-start.7
  705.3 1.6 copy-start.6
  705.3 2.0 copy-start.13
  707.4 2.6 copy-start.15
  710.0 1.0 copy-start.16
  710.0 1.9 copy-start.17
  710.0 2.6 copy-start.18
  710.0 3.4 copy-start.19
  (1 other events, 0.7 us)
